TPU v7x, 32 devices: a whole 2x2x4 slice. The times are simulated.
32 devices in a mesh: replica: 2 (over y), width: 2 (over core), hidden: 8 (over z, x).
Axes of the slice: x: 2, y: 2, z: 4, core: 2. Of those that a mesh axis runs over, the one named last changes fastest.
Arguments:
- acts: bfloat16 [160, 8192], P(('replica', 'hidden'), 'width'), parts along dimension 0, may hold values from -6 to 6
- gate_codes: bfloat16 [8192, 26624], P('width', 'hidden'), may hold values from -4 to 4
- gate_scales: float32 [256, 26624], P('width', 'hidden'), may hold values from 0.0055242716 to 0.022097087
- up_codes: bfloat16 [8192, 26624], P('width', 'hidden'), may hold values from -4 to 4
- up_scales: float32 [256, 26624], P('width', 'hidden'), may hold values from 0.0055242716 to 0.022097087
- down_codes: bfloat16 [26624, 8192], P('hidden', 'width'), may hold values from -4 to 4
- down_scales: float32 [832, 8192], P('hidden', 'width'), may hold values from 0.006128629 to 0.024514517
Outputs:
- mixed: bfloat16 [160, 8192], P(('replica', 'hidden'), 'width'), parts along dimension 0
There are 2 independent parts, one for each index of `replica`. A program takes and returns all parts, laid end to end along the dimension named above; an argument that names none is the same for every part. Nothing has to cross between parts.
All inputs are finite; a program needn't handle non-finite values.
Results may differ from a plain program's by a relative error of at most 0.0072.
Values may be sent and summed in bfloat16 or wider, within the bound.
No kernel may reach another device: no remote copies, remote signals or barrier semaphores. Data moves between devices by JAX's collectives and lax.ppermute only.
A program may use at most 320 MiB of HBM per device.

v0:
```python
import jax
import jax.numpy as jnp
from jax import lax
from jax.sharding import PartitionSpec as P


def dequant(codes, scales):
    groups = scales.shape[0]
    shaped = codes.reshape(groups, codes.shape[0] // groups, codes.shape[1]).astype(jnp.float32)
    return (shaped * scales[:, None, :]).reshape(codes.shape).astype(jnp.bfloat16)


def swiglu(sums, units):
    return (jax.nn.silu(sums[:, :units]) * sums[:, units:]).astype(jnp.bfloat16)


def local(acts, gate_codes, gate_scales, up_codes, up_scales, down_codes, down_scales):
    units = gate_codes.shape[1]
    both_weights = jnp.concatenate(
        [dequant(gate_codes, gate_scales), dequant(up_codes, up_scales)], axis=1
    )
    down_weight = dequant(down_codes, down_scales)
    partial_value = jnp.dot(
        lax.all_gather(acts, "hidden", axis=0, tiled=True),
        both_weights,
        preferred_element_type=jnp.float32,
    )
    shared = lax.psum_scatter(partial_value, "width", scatter_dimension=0, tiled=True)
    hidden_all = lax.all_gather(swiglu(shared, units), "width", axis=0, tiled=True)
    terms = jnp.dot(hidden_all, down_weight, preferred_element_type=jnp.float32)
    mixed = lax.psum_scatter(terms, "hidden", scatter_dimension=0, tiled=True)
    return mixed.astype(jnp.bfloat16)


def solution(mesh):
    placed = (
        P(("replica", "hidden"), "width"),
        P("width", "hidden"),
        P("width", "hidden"),
        P("width", "hidden"),
        P("width", "hidden"),
        P("hidden", "width"),
        P("hidden", "width"),
    )
    return jax.shard_map(
        local,
        mesh=mesh,
        in_specs=placed,
        out_specs=P(("replica", "hidden"), "width"),
        check_vma=False,
    )
```

profile of v0, /device:TPU:0, one launch (start us, length us, event | category | flops | bytes accessed | tf_op | source)
XLA Modules:
  0.0 219.5 jit_solution(2864208064432612500)
XLA Ops:
  6.5 0.0 reduce-scatter.2.cloned.1.call-start
  6.5 34.9 %all-gather = bf16[8,10,4096]{2,1,0:T(8,128)(2,1)S(1)} all-gather(bf16[1,10,4096]{2,1,0:T(8,128)(2,1)} %bitcast.19), channel_id=1, replica_groups=mesh['replica'=2,'width'=2,'hidden'=8] {'hidden'}, dimensions={0}, use_global_device_ids=true | all-gather | bytes 737280 | tf_op jit(solution)/shard_map/all_gather | solution.py:24
  41.4 0.2 reshape.13
  41.6 37.6 %fusion.5 = (bf16[4096,3328]{1,0:T(8,128)(2,1)}, bf16[4096,3328]{1,0:T(8,128)(2,1)}) fusion(bf16[4096,3328]{1,0:T(8,128)(2,1)} %param.10, f32[128,3328]{1,0:T(8,128)} %param.11, f32[128,3328]{1,0:T(8,128)} %param.9, bf16[4096,3328]{1,0:T(8,128)(2,1)} %param.8), kind=kLoop, calls=%fused_computation.7 | loop fusion | flops 81788928 | bytes 112459776 | tf_op jit(solution)/shard_map/convert_element_type | solution.py:10
  79.3 0.0 copy-start
  79.3 20.7 %fusion.7 = f32[80,6656]{1,0:T(8,128)} fusion(bf16[80,4096]{1,0:T(8,128)(2,1)S(1)} %reshape.13, bf16[4096,3328]{1,0:T(8,128)(2,1)} %get-tuple-element.5, bf16[4096,3328]{1,0:T(8,128)(2,1)} %get-tuple-element.6), kind=kOutput, calls=%fused_computation.10 | convolution fusion | flops 4471128064 | bytes 57311232 | tf_op jit(solution)/shard_map/dot_general | solution.py:23
  100.0 0.0 reduce-scatter.2.cloned.1.call-update
  100.0 0.0 copy-done
  100.0 0.0 copy-start.1
  100.0 19.7 %fusion.4 = bf16[3328,4096]{1,0:T(8,128)(2,1)} fusion(bf16[3328,4096]{1,0:T(8,128)(2,1)} %param.12, f32[104,4096]{1,0:T(8,128)S(1)} %copy-done), kind=kLoop, calls=%fused_computation.5 | loop fusion | flops 40894464 | bytes 56229888 | tf_op jit(solution)/shard_map/convert_element_type | solution.py:10
  119.7 0.0 copy-done.1
  119.7 0.6 dynamic-slice
  121.0 0.0 reduce-scatter.2.cloned.1.call-done
  121.0 1.4 fusion.10
  122.4 2.2 all_gather.7
  124.5 11.3 %fusion.12 = f32[80,4096]{1,0:T(8,128)S(1)} fusion(bf16[80,3328]{1,0:T(8,128)(2,1)S(1)} %all_gather.7, bf16[3328,4096]{1,0:T(8,128)(2,1)} %fusion.4), kind=kOutput, calls=%fused_computation.15 | convolution fusion | flops 2181038080 | bytes 29106176 | tf_op jit(solution)/shard_map/dot_general | solution.py:30
  135.9 76.0 %all-reduce.2 = bf16[80,4096]{1,0:T(8,128)(2,1)S(1)} all-reduce(f32[80,4096]{1,0:T(8,128)S(1)} %fusion.12), channel_id=3, replica_groups=mesh['replica'=2,'width'=2,'hidden'=8] {'hidden'}, use_global_device_ids=true, to_apply=%region_1.2.clone | all-reduce | flops 327680 | bytes 1966080
  211.9 0.7 dynamic-slice_convert_fusion
Async XLA Ops:
  6.5 114.5 %reduce-scatter.2.cloned.1.call-start = ((), (), s32[]{:S(2)}) async-start(), calls=%async_computation.1 | async-start | bytes 3194880 | tf_op jit(solution)/shard_map/reduce_scatter | solution.py:28
  79.3 20.7 %copy-start = (f32[104,4096]{1,0:T(8,128)S(1)}, f32[104,4096]{1,0:T(8,128)}, u32[]{:S(2)}) copy-start(f32[104,4096]{1,0:T(8,128)} %param.13) | copy-start | bytes 5111812
  100.0 19.7 %copy-start.1 = (u32[32]{0:T(128)S(1)}, u32[32]{0:T(128)}, u32[]{:S(2)}) copy-start(u32[32]{0:T(128)} %constant.6) | copy-start | bytes 388
Sparse Core Ops, SparseCore 0:
  100.1 10.4 reduce-scatter.1
where the time goes:
time: 220 us; the launch traced here: 219 us
  blocking collectives  113 us (51%)
  other arithmetic  58.7 us (27%)
  matrix products  32 us (15%)
  between operations  14.1 us (6%)
    unnamed x1, blocking collectives  76 us
    convert_element_type x2, other arithmetic, dequant(): (shaped * scales[:, None, :]).reshape(codes.shape).astype(jnp.bfloat16)  57.3 us
    all_gather x1, blocking collectives, local(): lax.all_gather(acts, 'hidden', axis=0, tiled=True)  34.9 us
    dot_general x1, matrix products, local(): jnp.dot(lax.all_gather(acts, 'hidden', axis=0, tiled=True), both_weights,...  20.7 us
    dot_general x1, matrix products, local(): terms = jnp.dot(hidden_all, down_weight, preferred_element_type=jnp.float32)  11.3 us
  transfers between devices with their start and end apart: 1, of which 0 were waited for; matrix products, arithmetic and copies ran while one was open for 9% of the time, Pallas kernels for 0%

commit v1 on v0

v1 whole, which is shorter than its diff:
```python
import functools

import jax
import jax.numpy as jnp
from jax import lax
from jax.experimental import pallas as pl
from jax.experimental.pallas import tpu as pltpu
from jax.sharding import PartitionSpec as P

BF16, F32 = jnp.bfloat16, jnp.float32
MIB = 1 << 20
TILE = 8


def divisor(extent, limit, step):
    for size in range(limit - limit % step, 0, -step):
        if extent % size == 0:
            return size
    return extent


def whole(count):
    return [pl.BlockSpec(memory_space=pltpu.VMEM)] * count


def call(body, out_shape, operands, name, limit, scratch=(), flops=0):
    single = not isinstance(out_shape, (list, tuple))
    shapes = [out_shape] if single else out_shape
    moved = sum(x.size * x.dtype.itemsize for x in operands)
    return pl.pallas_call(
        body,
        in_specs=whole(len(operands)),
        out_specs=whole(1)[0] if single else whole(len(shapes)),
        out_shape=out_shape,
        scratch_shapes=list(scratch),
        compiler_params=pltpu.CompilerParams(vmem_limit_bytes=limit),
        cost_estimate=pl.CostEstimate(flops=flops, bytes_accessed=moved, transcendentals=0),
        name=name,
    )(*operands)


def pack_body(a_ref, o_ref):
    m, width = a_ref.shape
    rest = m - TILE
    piece = rest * width // TILE
    a = a_ref[...].astype(F32)
    o_ref[:, :width] = a[:TILE].astype(BF16)
    left = [a[TILE:, k * piece : (k + 1) * piece] for k in range(TILE // rest)]
    o_ref[:, width:] = jnp.concatenate(left, axis=0).astype(BF16)


def unpack_rows(block, rest, store):
    width = block.shape[1] * TILE // (TILE + rest)
    piece = rest * width // TILE
    store(0, 0, block[:, :width])
    for k in range(TILE // rest):
        store(TILE, k * piece, block[k * rest : (k + 1) * rest, width:])


def pack_all(total, first, rest, blocks):
    width = total.shape[1]
    piece = rest * width // TILE
    base = blocks * TILE + first * rest
    left = [total[base : base + rest, k * piece : (k + 1) * piece] for k in range(TILE // rest)]
    return total[first * TILE : (first + 1) * TILE, :], jnp.concatenate(left, axis=0)


def dequant(codes, scales):
    depth, width = codes.shape
    groups = scales.shape[0]
    shaped = codes.astype(F32).reshape(groups, depth // groups, width)
    return (shaped * scales[:, None, :]).astype(BF16).reshape(depth, width)


def project(a_ref, codes_ref, scales_ref, store):
    depth, width = codes_ref.shape
    block = depth // scales_ref.shape[0]
    columns = divisor(width, 1664, 128)
    rows = divisor(depth, 512, 8 * block)

    def step(j):
        cols = pl.ds(j * columns if isinstance(j, int) else pl.multiple_of(j * columns, columns), columns)
        total = jnp.zeros((a_ref.shape[0], columns), F32)
        for k in range(0, depth, rows):
            w = dequant(codes_ref[k : k + rows, cols], scales_ref[k // block : (k + rows) // block, cols])
            total += jnp.dot(a_ref[:, k : k + rows], w, preferred_element_type=F32)
        store(cols, total)

    if width == columns:
        step(0)
    else:
        pl.loop(0, width // columns)(step)


def gate_body(count, rest, *refs):
    blocks, (codes, scales), (acts, own, sent), wide = refs[:count], refs[count : count + 2], refs[count + 2 : count + 5], refs[count + 5]
    total = sum(b.shape[0] for b in blocks) // TILE
    at = 0
    for ref in blocks:
        for i in range(ref.shape[0] // TILE):
            def store(row, column, values):
                first = at * TILE if row == 0 else total * TILE + at * rest
                wide[first : first + values.shape[0], column : column + values.shape[1]] = values
            unpack_rows(ref[i * TILE : (i + 1) * TILE, :].astype(F32), rest, store)
            at += 1
    acts[...] = wide[...].astype(BF16)
    up_body(acts, codes, scales, own, sent)


def up_body(acts, codes, scales, own, sent):
    def store(cols, total):
        own[:, cols] = total
        sent[:, cols] = total.astype(BF16)

    project(acts, codes, scales, store)


def down_body(rest, blocks, kept, *refs):
    gate, gate_other, up, up_other, codes, scales = refs[:6]
    outs, (hidden, terms) = refs[6:-2], refs[-2:]
    width = divisor(hidden.shape[1], 512, 128)
    for c in range(0, hidden.shape[1], width):
        cols = slice(c, c + width)
        g = gate[:, cols] + gate_other[:, cols].astype(F32)
        u = up[:, cols] + up_other[:, cols].astype(F32)
        hidden[:, cols] = (jax.nn.silu(g) * u).astype(BF16)

    def store(cols, total):
        terms[:, cols] = total

    project(hidden, codes, scales, store)
    width = terms.shape[1]
    for i in range(blocks):
        main, left = pack_all(terms, i, rest, blocks)
        out, at = (outs[0], i) if i < kept else (outs[1], i - kept)
        out[at * TILE : (at + 1) * TILE, :width] = main.astype(out.dtype)
        out[at * TILE : (at + 1) * TILE, width:] = left.astype(out.dtype)


def add_body(mine, other, first, *later):
    first[...] = mine[:TILE, :] + other[:TILE, :].astype(F32)
    for i, ref in enumerate(later):
        rows = slice((i + 1) * TILE, (i + 2) * TILE)
        ref[...] = (mine[rows, :] + other[rows, :].astype(F32)).astype(BF16)


def last_body(*refs):
    out = refs[-1]
    total = refs[0][...]
    for ref in refs[1:-1]:
        total += ref[...].astype(F32)

    def store(row, column, values):
        out[row : row + values.shape[0], column : column + values.shape[1]] = values.astype(out.dtype)

    unpack_rows(total, out.shape[0] - TILE, store)


def local(peers, acts, gate_codes, gate_scales, up_codes, up_scales, down_codes, down_scales):
    m, width = acts.shape
    units = gate_codes.shape[1]
    rest = m - TILE
    dense = width + rest * width // TILE
    rows = peers * m
    sds = jax.ShapeDtypeStruct
    pair = peers == 8
    far = peers // 2

    def flip(x):
        return lax.ppermute(x, "hidden", [(h, h ^ 1) for h in range(peers)])

    def along(x, s):
        return lax.ppermute(x, "hidden", [(h, (h + 2 * s) % peers) for h in range(peers)])

    def swap(x):
        return lax.ppermute(x, "width", [(0, 1), (1, 0)])

    def in_vmem(x):
        return pltpu.with_memory_space_constraint(x, pltpu.VMEM)

    packed = call(pack_body, sds((TILE, dense), BF16), [acts], "pack", 4 * MIB)
    if pair:
        line = [packed] + [along(packed, s) for s in range(1, far)]
        blocks = line + [flip(x) for x in line]
    else:
        blocks = [lax.all_gather(packed, "hidden", axis=0, tiled=True)]
    work = 2 * rows * width * units
    spare = 4 * rows * (width + 3 * units) + 12 * MIB
    acts_all, gate, gate_sent = call(
        functools.partial(gate_body, len(blocks), rest),
        [sds((rows, width), BF16), sds((rows, units), F32), sds((rows, units), BF16)],
        blocks + [in_vmem(gate_codes), gate_scales],
        "gate",
        min(spare, 40 * MIB),
        scratch=[pltpu.VMEM((rows, width), F32)],
        flops=work,
    )
    gate_other = swap(gate_sent)
    up, up_sent = call(
        up_body,
        [sds((rows, units), F32), sds((rows, units), BF16)],
        [acts_all, in_vmem(up_codes), up_scales],
        "up",
        min(spare, 40 * MIB),
        flops=work,
    )
    up_other = swap(up_sent)
    kept = far if pair else peers
    outs = [sds((kept * TILE, dense), F32)] + ([sds((far * TILE, dense), BF16)] if pair else [])
    parts = call(
        functools.partial(down_body, rest, peers, kept),
        outs,
        [gate, gate_other, up, up_other, in_vmem(down_codes), down_scales],
        "down",
        min(4 * rows * (3 * width + 3 * units) + 8 * MIB, 48 * MIB),
        scratch=[pltpu.VMEM((rows, units), BF16), pltpu.VMEM((rows, width), F32)],
        flops=work,
    )
    if pair:
        mine, sent = parts
        other = flip(sent)
        sums = call(
            add_body,
            [sds((TILE, dense), F32)] + [sds((TILE, dense), BF16)] * (far - 1),
            [mine, other],
            "add",
            8 * MIB,
        )
        terms = [sums[0]] + [along(x, far - s) for s, x in zip(range(1, far), sums[1:])]
    else:
        terms = [lax.psum_scatter(parts[0], "hidden", scatter_dimension=0, tiled=True)]
    return call(last_body, sds((m, width), BF16), terms, "last", 8 * MIB)


def solution(mesh):
    placed = (
        P(("replica", "hidden"), "width"),
        P("width", "hidden"),
        P("width", "hidden"),
        P("width", "hidden"),
        P("width", "hidden"),
        P("hidden", "width"),
        P("hidden", "width"),
    )
    return jax.shard_map(
        functools.partial(local, mesh.shape["hidden"]),
        mesh=mesh,
        in_specs=placed,
        out_specs=P(("replica", "hidden"), "width"),
        check_vma=False,
    )
```

time: 220 us -> 91.3 us (0.41)
  blocking collectives: 113 us -> 0 us
  other arithmetic: 58.7 us -> 0 us
  matrix products: 32 us -> 0 us
  local copies, waits for them, and re-layouts: 1.53 us -> 28.6 us
  waiting for transfers between devices: 0.04 us -> 25 us
  Pallas kernels: 0 us -> 21.7 us
  starting transfers between devices: 0.01 us -> 15.6 us
  between operations: 14.1 us -> 0.06 us
    unnamed x1 -> x0, blocking collectives: 76 us -> none
    convert_element_type x3 -> x0, other arithmetic: 58.7 us -> none  [the longest x2 57.3 us: dequant(): (shaped * scales[:, None, :]).reshape(codes.shape).astype(jnp.bfloat16)]
    all_gather x2 -> x0, blocking collectives: 37.1 us -> none  [the longest x1 34.9 us: local(): lax.all_gather(acts, 'hidden', axis=0, tiled=True)]
    dot_general x2 -> x0, matrix products: 32 us -> none  [the longest x1 20.7 us: local(): jnp.dot(lax.all_gather(acts, 'hidden', axis=0, tiled=True), both_weights,...]
    unnamed x6 -> x14, local copies, waits for them, and re-layouts: 0.83 us -> 28.6 us
    ppermute x0 -> x13, waiting for transfers between devices: none -> 25 us  [the longest x5 12.9 us: flip(): return lax.ppermute(x, 'hidden', [(h, h ^ 1) for h in range(peers)])]
    pallas_call x0 -> x6, Pallas kernels: none -> 21.7 us  [call(): pl.pallas_call(body, in_specs=whole(len(operands)), out_specs=whole(1)[0]...]
    ppermute x0 -> x13, starting transfers between devices: none -> 15.6 us  [the longest x6 8.73 us: along(): lax.ppermute(x, 'hidden', [(h, (h + 2 * s) % peers) for h in range(peers)])]
  transfers between devices with their start and end apart: 1 -> 13, of which waited for: 0 -> 8; matrix products, arithmetic and copies ran while one was open for 9% -> 0% of each run, Pallas kernels for 0% -> 7%
where the time goes in v1:
time: 91.3 us; the launch traced here: 91 us
  local copies, waits for them, and re-layouts  28.6 us (31%)
  waiting for transfers between devices  25 us (27%)
  Pallas kernels  21.7 us (24%)
  starting transfers between devices  15.6 us (17%)
    unnamed x14, local copies, waits for them, and re-layouts  28.6 us
    pallas_call x6, Pallas kernels, call(): pl.pallas_call(body, in_specs=whole(len(operands)), out_specs=whole(1)[0]...  21.7 us
    ppermute x5, waiting for transfers between devices, flip(): return lax.ppermute(x, 'hidden', [(h, h ^ 1) for h in range(peers)])  12.9 us
    ppermute x6, waiting for transfers between devices, along(): lax.ppermute(x, 'hidden', [(h, (h + 2 * s) % peers) for h in range(peers)])  10.6 us
    ppermute x6, starting transfers between devices, along(): lax.ppermute(x, 'hidden', [(h, (h + 2 * s) % peers) for h in range(peers)])  8.73 us
    ppermute x5, starting transfers between devices, flip(): return lax.ppermute(x, 'hidden', [(h, h ^ 1) for h in range(peers)])  6.25 us
  transfers between devices with their start and end apart: 13, of which 8 were waited for; matrix products, arithmetic and copies ran while one was open for 0% of the time, Pallas kernels for 7%

profile of v1, /device:TPU:0, one launch (start us, length us, event | category | flops | bytes accessed | tf_op | source)
XLA Modules:
  0.0 91.0 jit_solution(16702918536223603651)
XLA Ops:
  0.0 0.9 copy-done.6
  0.9 5.1 %collective-permute-start.2 = (bf16[8,5120]{1,0:T(8,128)(2,1)S(1)}, bf16[8,5120]{1,0:T(8,128)(2,1)S(1)}, u32[]{:S(2)}, u32[]{:S(2)}) collective-permute-start(bf16[8,5120]{1,0:T(8,128)(2,1)S(1)} %pack.1.refs_0_), channel_id=1, source_target_pairs={{0,6},{1,7},{2,0},{3,1},{4,2},{5,3},{6,4},{7,5},{8,14},{9,15},{10,... | collective-permute-start | bytes 245768 | tf_op jit(solution)/shard_map/ppermute | solution.py:173
  6.0 1.0 %collective-permute-start = (bf16[8,5120]{1,0:T(8,128)(2,1)S(1)}, bf16[8,5120]{1,0:T(8,128)(2,1)S(1)}, u32[]{:S(2)}, u32[]{:S(2)}) collective-permute-start(bf16[8,5120]{1,0:T(8,128)(2,1)S(1)} %pack.1.refs_0_), channel_id=1, source_target_pairs={{0,2},{1,3},{2,4},{3,5},{4,6},{5,7},{6,0},{7,1},{8,10},{9,11},{10,... | collective-permute-start | bytes 245768 | tf_op jit(solution)/shard_map/ppermute | solution.py:173
  7.0 1.5 %collective-permute-start.3 = (bf16[8,5120]{1,0:T(8,128)(2,1)S(1)}, bf16[8,5120]{1,0:T(8,128)(2,1)S(1)}, u32[]{:S(2)}, u32[]{:S(2)}) collective-permute-start(bf16[8,5120]{1,0:T(8,128)(2,1)S(1)} %pack.1.refs_0_), channel_id=1, source_target_pairs={{0,1},{1,0},{2,3},{3,2},{4,5},{5,4},{6,7},{7,6},{8,9},{9,8},{10,11... | collective-permute-start | bytes 245768 | tf_op jit(solution)/shard_map/ppermute | solution.py:170
  8.9 1.5 %collective-permute-start.6 = (bf16[8,5120]{1,0:T(8,128)(2,1)S(1)}, bf16[8,5120]{1,0:T(8,128)(2,1)S(1)}, u32[]{:S(2)}, u32[]{:S(2)}) collective-permute-start(bf16[8,5120]{1,0:T(8,128)(2,1)S(1)} %collective-permute-done.2.refs_3_), channel_id=1, source_target_pairs={{0,1},{1,0},{2,3},{3,2},{4,5},{5,4},{6,7},{7,6},{8,9},{9,8},{10,11... | collective-permute-start | bytes 245768 | tf_op jit(solution)/shard_map/ppermute | solution.py:170
  10.4 3.2 %collective-permute-done.1.refs_2_ = bf16[8,5120]{1,0:T(8,128)(2,1)S(1)} collective-permute-done((bf16[8,5120]{1,0:T(8,128)(2,1)S(1)}, bf16[8,5120]{1,0:T(8,128)(2,1)S(1)}, u32[]{:S(2)}, u32[]{:S(2)}) %collective-permute-start.1) | collective-permute-done | bytes 81952 | tf_op jit(solution)/shard_map/ppermute | solution.py:173
  13.5 1.5 %collective-permute-start.5 = (bf16[8,5120]{1,0:T(8,128)(2,1)S(1)}, bf16[8,5120]{1,0:T(8,128)(2,1)S(1)}, u32[]{:S(2)}, u32[]{:S(2)}) collective-permute-start(bf16[8,5120]{1,0:T(8,128)(2,1)S(1)} %collective-permute-done.1.refs_2_), channel_id=1, source_target_pairs={{0,1},{1,0},{2,3},{3,2},{4,5},{5,4},{6,7},{7,6},{8,9},{9,8},{10,11... | collective-permute-start | bytes 245768 | tf_op jit(solution)/shard_map/ppermute | solution.py:170
  15.6 3.2 %collective-permute-done.5.refs_6_ = bf16[8,5120]{1,0:T(8,128)(2,1)S(1)} collective-permute-done((bf16[8,5120]{1,0:T(8,128)(2,1)S(1)}, bf16[8,5120]{1,0:T(8,128)(2,1)S(1)}, u32[]{:S(2)}, u32[]{:S(2)}) %collective-permute-start.5) | collective-permute-done | bytes 81952 | tf_op jit(solution)/shard_map/ppermute | solution.py:170
  18.8 0.9 collective-permute-done.4.refs_5_
  19.7 8.8 %copy-done = bf16[4096,3328]{1,0:T(8,128)(2,1)S(1)} copy-done((bf16[4096,3328]{1,0:T(8,128)(2,1)S(1)}, bf16[4096,3328]{1,0:T(8,128)(2,1)}, u32[]{:S(2)}) %copy-start) | copy-done | bytes 27263000
  28.5 1.5 %copy-done.3 = f32[128,3328]{1,0:T(8,128)S(1)} copy-done((f32[128,3328]{1,0:T(8,128)S(1)}, f32[128,3328]{1,0:T(8,128)}, u32[]{:S(2)}) %copy-start.3) | copy-done | bytes 1703960
  29.9 6.9 %gate.1 = (bf16[80,4096]{1,0:T(8,128)(2,1)S(1)}, f32[80,3328]{1,0:T(8,128)S(1)}, bf16[80,3328]{1,0:T(8,128)(2,1)S(1)}) custom-call(bf16[8,5120]{1,0:T(8,128)(2,1)S(1)} %pack.1.refs_0_, bf16[8,5120]{1,0:T(8,128)(2,1)S(1)} %collective-permute-done.refs_1_, bf16[8,5120]{1,0:T(8,128)(2,1)S(1)} %collective-permute-done.1.refs_2_, ...), custom_call_target="tpu_custom_call" | custom-call | flops 2181038080 | bytes 29622272 | tf_op jit(solution)/shard_map/gate/pallas_call | solution.py:30
  36.9 8.7 %copy-done.1 = bf16[4096,3328]{1,0:T(8,128)(2,1)S(1)} copy-done((bf16[4096,3328]{1,0:T(8,128)(2,1)S(1)}, bf16[4096,3328]{1,0:T(8,128)(2,1)}, u32[]{:S(2)}) %copy-start.1) | copy-done | bytes 27263000
  45.7 6.8 %up.1 = (f32[80,3328]{1,0:T(8,128)S(1)}, bf16[80,3328]{1,0:T(8,128)(2,1)S(1)}) custom-call(bf16[80,4096]{1,0:T(8,128)(2,1)S(1)} %get-tuple-element.18.acts, bf16[4096,3328]{1,0:T(8,128)(2,1)S(1)} %copy-done.1, f32[128,3328]{1,0:T(8,128)S(1)} %copy-done.4), custom_call_target="tpu_custom_call" | custom-call | flops 2181038080 | bytes 29622272 | tf_op jit(solution)/shard_map/up/pallas_call | solution.py:30
  53.0 1.5 %collective-permute-done.8.refs_3_ = bf16[80,3328]{1,0:T(8,128)(2,1)S(1)} collective-permute-done((bf16[80,3328]{1,0:T(8,128)(2,1)S(1)}, bf16[80,3328]{1,0:T(8,128)(2,1)S(1)}, u32[]{:S(2)}, u32[]{:S(2)}) %collective-permute-start.8) | collective-permute-done | bytes 532512 | tf_op jit(solution)/shard_map/ppermute | solution.py:176
  54.6 8.8 %copy-done.2 = bf16[3328,4096]{1,0:T(8,128)(2,1)S(1)} copy-done((bf16[3328,4096]{1,0:T(8,128)(2,1)S(1)}, bf16[3328,4096]{1,0:T(8,128)(2,1)}, u32[]{:S(2)}) %copy-start.2) | copy-done | bytes 27263000
  63.3 7.2 %down.1 = (f32[32,5120]{1,0:T(8,128)S(1)}, bf16[32,5120]{1,0:T(8,128)(2,1)S(1)}) custom-call(f32[80,3328]{1,0:T(8,128)S(1)} %get-tuple-element.16.refs_0_, bf16[80,3328]{1,0:T(8,128)(2,1)S(1)} %collective-permute-done.7.refs_1_, f32[80,3328]{1,0:T(8,128)S(1)} %get-tuple-element.19.refs_2_, bf16[80,3328]{1,0:T(8,128)(2,1)S(1)} %collective-permute-done.8.refs_3_, ...), custom_call_target="tpu_custom_call" | custom-call | flops 2181038080 | bytes 32161792 | tf_op jit(solution)/shard_map/down/pallas_call | solution.py:30
  70.5 1.2 %collective-permute-start.9 = (bf16[32,5120]{1,0:T(8,128)(2,1)S(1)}, bf16[32,5120]{1,0:T(8,128)(2,1)S(1)}, u32[]{:S(2)}, u32[]{:S(2)}) collective-permute-start(bf16[32,5120]{1,0:T(8,128)(2,1)S(1)} %get-tuple-element.22), channel_id=1, source_target_pairs={{0,1},{1,0},{2,3},{3,2},{4,5},{5,4},{6,7},{7,6},{8,9},{9,8},{10,11... | collective-permute-start | bytes 983048 | tf_op jit(solution)/shard_map/ppermute | solution.py:170
  71.8 8.8 %collective-permute-done.9.other = bf16[32,5120]{1,0:T(8,128)(2,1)S(1)} collective-permute-done((bf16[32,5120]{1,0:T(8,128)(2,1)S(1)}, bf16[32,5120]{1,0:T(8,128)(2,1)S(1)}, u32[]{:S(2)}, u32[]{:S(2)}) %collective-permute-start.9) | collective-permute-done | bytes 327712 | tf_op jit(solution)/shard_map/ppermute | solution.py:170
  80.6 2.0 %collective-permute-start.10 = (bf16[8,5120]{1,0:T(8,128)(2,1)S(1)}, bf16[8,5120]{1,0:T(8,128)(2,1)S(1)}, u32[]{:S(2)}, u32[]{:S(2)}) collective-permute-start(bf16[8,5120]{1,0:T(8,128)(2,1)S(1)} %get-tuple-element.24), channel_id=1, source_target_pairs={{0,6},{1,7},{2,0},{3,1},{4,2},{5,3},{6,4},{7,5},{8,14},{9,15},{10,... | collective-permute-start | bytes 245768 | tf_op jit(solution)/shard_map/ppermute | solution.py:173
  82.6 0.6 collective-permute-start.12
  83.3 2.3 %collective-permute-done.10.refs_1_ = bf16[8,5120]{1,0:T(8,128)(2,1)S(1)} collective-permute-done((bf16[8,5120]{1,0:T(8,128)(2,1)S(1)}, bf16[8,5120]{1,0:T(8,128)(2,1)S(1)}, u32[]{:S(2)}, u32[]{:S(2)}) %collective-permute-start.10) | collective-permute-done | bytes 81952 | tf_op jit(solution)/shard_map/ppermute | solution.py:173
  85.6 4.8 %collective-permute-done.11.refs_2_ = bf16[8,5120]{1,0:T(8,128)(2,1)S(1)} collective-permute-done((bf16[8,5120]{1,0:T(8,128)(2,1)S(1)}, bf16[8,5120]{1,0:T(8,128)(2,1)S(1)}, u32[]{:S(2)}, u32[]{:S(2)}) %collective-permute-start.11) | collective-permute-done | bytes 81952 | tf_op jit(solution)/shard_map/ppermute | solution.py:173
  90.3 0.7 last.1
  (22 shorter events, 1.6 us)
Async XLA Ops:
  0.0 0.9 copy-start.6
  0.9 8.0 %collective-permute-start.2 = (bf16[8,5120]{1,0:T(8,128)(2,1)S(1)}, bf16[8,5120]{1,0:T(8,128)(2,1)S(1)}, u32[]{:S(2)}, u32[]{:S(2)}) collective-permute-start(bf16[8,5120]{1,0:T(8,128)(2,1)S(1)} %pack.1.refs_0_), channel_id=1, source_target_pairs={{0,6},{1,7},{2,0},{3,1},{4,2},{5,3},{6,4},{7,5},{8,14},{9,15},{10,... | collective-permute-start | bytes 245768 | tf_op jit(solution)/shard_map/ppermute | solution.py:173
  6.0 7.5 %collective-permute-start.1 = (bf16[8,5120]{1,0:T(8,128)(2,1)S(1)}, bf16[8,5120]{1,0:T(8,128)(2,1)S(1)}, u32[]{:S(2)}, u32[]{:S(2)}) collective-permute-start(bf16[8,5120]{1,0:T(8,128)(2,1)S(1)} %pack.1.refs_0_), channel_id=1, source_target_pairs={{0,4},{1,5},{2,6},{3,7},{4,0},{5,1},{6,2},{7,3},{8,12},{9,13},{10,... | collective-permute-start | bytes 245768 | tf_op jit(solution)/shard_map/ppermute | solution.py:173
  6.0 9.0 %collective-permute-start = (bf16[8,5120]{1,0:T(8,128)(2,1)S(1)}, bf16[8,5120]{1,0:T(8,128)(2,1)S(1)}, u32[]{:S(2)}, u32[]{:S(2)}) collective-permute-start(bf16[8,5120]{1,0:T(8,128)(2,1)S(1)} %pack.1.refs_0_), channel_id=1, source_target_pairs={{0,2},{1,3},{2,4},{3,5},{4,6},{5,7},{6,0},{7,1},{8,10},{9,11},{10,... | collective-permute-start | bytes 245768 | tf_op jit(solution)/shard_map/ppermute | solution.py:173
  7.0 8.5 %collective-permute-start.3 = (bf16[8,5120]{1,0:T(8,128)(2,1)S(1)}, bf16[8,5120]{1,0:T(8,128)(2,1)S(1)}, u32[]{:S(2)}, u32[]{:S(2)}) collective-permute-start(bf16[8,5120]{1,0:T(8,128)(2,1)S(1)} %pack.1.refs_0_), channel_id=1, source_target_pairs={{0,1},{1,0},{2,3},{3,2},{4,5},{5,4},{6,7},{7,6},{8,9},{9,8},{10,11... | collective-permute-start | bytes 245768 | tf_op jit(solution)/shard_map/ppermute | solution.py:170
  8.9 6.7 %collective-permute-start.6 = (bf16[8,5120]{1,0:T(8,128)(2,1)S(1)}, bf16[8,5120]{1,0:T(8,128)(2,1)S(1)}, u32[]{:S(2)}, u32[]{:S(2)}) collective-permute-start(bf16[8,5120]{1,0:T(8,128)(2,1)S(1)} %collective-permute-done.2.refs_3_), channel_id=1, source_target_pairs={{0,1},{1,0},{2,3},{3,2},{4,5},{5,4},{6,7},{7,6},{8,9},{9,8},{10,11... | collective-permute-start | bytes 245768 | tf_op jit(solution)/shard_map/ppermute | solution.py:170
  13.5 5.3 %collective-permute-start.5 = (bf16[8,5120]{1,0:T(8,128)(2,1)S(1)}, bf16[8,5120]{1,0:T(8,128)(2,1)S(1)}, u32[]{:S(2)}, u32[]{:S(2)}) collective-permute-start(bf16[8,5120]{1,0:T(8,128)(2,1)S(1)} %collective-permute-done.1.refs_2_), channel_id=1, source_target_pairs={{0,1},{1,0},{2,3},{3,2},{4,5},{5,4},{6,7},{7,6},{8,9},{9,8},{10,11... | collective-permute-start | bytes 245768 | tf_op jit(solution)/shard_map/ppermute | solution.py:170
  15.0 4.7 %collective-permute-start.4 = (bf16[8,5120]{1,0:T(8,128)(2,1)S(1)}, bf16[8,5120]{1,0:T(8,128)(2,1)S(1)}, u32[]{:S(2)}, u32[]{:S(2)}) collective-permute-start(bf16[8,5120]{1,0:T(8,128)(2,1)S(1)} %collective-permute-done.refs_1_), channel_id=1, source_target_pairs={{0,1},{1,0},{2,3},{3,2},{4,5},{5,4},{6,7},{7,6},{8,9},{9,8},{10,11... | collective-permute-start | bytes 245768 | tf_op jit(solution)/shard_map/ppermute | solution.py:170
  19.7 8.8 %copy-start = (bf16[4096,3328]{1,0:T(8,128)(2,1)S(1)}, bf16[4096,3328]{1,0:T(8,128)(2,1)}, u32[]{:S(2)}) copy-start(bf16[4096,3328]{1,0:T(8,128)(2,1)} %refs_8_.1) | copy-start | bytes 81788928
  28.4 1.5 %copy-start.3 = (f32[128,3328]{1,0:T(8,128)S(1)}, f32[128,3328]{1,0:T(8,128)}, u32[]{:S(2)}) copy-start(f32[128,3328]{1,0:T(8,128)} %refs_9_.1) | copy-start | bytes 5111812
  29.9 7.0 %copy-start.4 = (f32[128,3328]{1,0:T(8,128)S(1)}, f32[128,3328]{1,0:T(8,128)}, u32[]{:S(2)}) copy-start(f32[128,3328]{1,0:T(8,128)} %scales.1) | copy-start | bytes 5111812
  36.8 16.2 %collective-permute-start.7 = (bf16[80,3328]{1,0:T(8,128)(2,1)S(1)}, bf16[80,3328]{1,0:T(8,128)(2,1)S(1)}, u32[]{:S(2)}, u32[]{:S(2)}) collective-permute-start(bf16[80,3328]{1,0:T(8,128)(2,1)S(1)} %get-tuple-element.17), channel_id=1, source_target_pairs={{0,8},{8,0},{1,9},{9,1},{2,10},{10,2},{3,11},{11,3},{4,12},{12,4},... | collective-permute-start | bytes 1597448 | tf_op jit(solution)/shard_map/ppermute | solution.py:176
  36.9 8.8 %copy-start.1 = (bf16[4096,3328]{1,0:T(8,128)(2,1)S(1)}, bf16[4096,3328]{1,0:T(8,128)(2,1)}, u32[]{:S(2)}) copy-start(bf16[4096,3328]{1,0:T(8,128)(2,1)} %codes.1) | copy-start | bytes 81788928
  45.7 8.9 %copy-start.5 = (f32[104,4096]{1,0:T(8,128)S(1)}, f32[104,4096]{1,0:T(8,128)}, u32[]{:S(2)}) copy-start(f32[104,4096]{1,0:T(8,128)} %refs_5_.1) | copy-start | bytes 5111812
  52.5 2.1 %collective-permute-start.8 = (bf16[80,3328]{1,0:T(8,128)(2,1)S(1)}, bf16[80,3328]{1,0:T(8,128)(2,1)S(1)}, u32[]{:S(2)}, u32[]{:S(2)}) collective-permute-start(bf16[80,3328]{1,0:T(8,128)(2,1)S(1)} %get-tuple-element.20), channel_id=1, source_target_pairs={{0,8},{8,0},{1,9},{9,1},{2,10},{10,2},{3,11},{11,3},{4,12},{12,4},... | collective-permute-start | bytes 1597448 | tf_op jit(solution)/shard_map/ppermute | solution.py:176
  54.6 8.8 %copy-start.2 = (bf16[3328,4096]{1,0:T(8,128)(2,1)S(1)}, bf16[3328,4096]{1,0:T(8,128)(2,1)}, u32[]{:S(2)}) copy-start(bf16[3328,4096]{1,0:T(8,128)(2,1)} %refs_4_.1) | copy-start | bytes 81788928
  70.5 10.0 %collective-permute-start.9 = (bf16[32,5120]{1,0:T(8,128)(2,1)S(1)}, bf16[32,5120]{1,0:T(8,128)(2,1)S(1)}, u32[]{:S(2)}, u32[]{:S(2)}) collective-permute-start(bf16[32,5120]{1,0:T(8,128)(2,1)S(1)} %get-tuple-element.22), channel_id=1, source_target_pairs={{0,1},{1,0},{2,3},{3,2},{4,5},{5,4},{6,7},{7,6},{8,9},{9,8},{10,11... | collective-permute-start | bytes 983048 | tf_op jit(solution)/shard_map/ppermute | solution.py:170
  80.6 4.9 %collective-permute-start.10 = (bf16[8,5120]{1,0:T(8,128)(2,1)S(1)}, bf16[8,5120]{1,0:T(8,128)(2,1)S(1)}, u32[]{:S(2)}, u32[]{:S(2)}) collective-permute-start(bf16[8,5120]{1,0:T(8,128)(2,1)S(1)} %get-tuple-element.24), channel_id=1, source_target_pairs={{0,6},{1,7},{2,0},{3,1},{4,2},{5,3},{6,4},{7,5},{8,14},{9,15},{10,... | collective-permute-start | bytes 245768 | tf_op jit(solution)/shard_map/ppermute | solution.py:173
  82.6 7.7 %collective-permute-start.11 = (bf16[8,5120]{1,0:T(8,128)(2,1)S(1)}, bf16[8,5120]{1,0:T(8,128)(2,1)S(1)}, u32[]{:S(2)}, u32[]{:S(2)}) collective-permute-start(bf16[8,5120]{1,0:T(8,128)(2,1)S(1)} %get-tuple-element.25), channel_id=1, source_target_pairs={{0,4},{1,5},{2,6},{3,7},{4,0},{5,1},{6,2},{7,3},{8,12},{9,13},{10,... | collective-permute-start | bytes 245768 | tf_op jit(solution)/shard_map/ppermute | solution.py:173
  82.6 7.7 %collective-permute-start.12 = (bf16[8,5120]{1,0:T(8,128)(2,1)S(1)}, bf16[8,5120]{1,0:T(8,128)(2,1)S(1)}, u32[]{:S(2)}, u32[]{:S(2)}) collective-permute-start(bf16[8,5120]{1,0:T(8,128)(2,1)S(1)} %get-tuple-element.26), channel_id=1, source_target_pairs={{0,2},{1,3},{2,4},{3,5},{4,6},{5,7},{6,0},{7,1},{8,10},{9,11},{10,... | collective-permute-start | bytes 245768 | tf_op jit(solution)/shard_map/ppermute | solution.py:173

commit v2 on v1

--- a/solution.py
+++ b/solution.py
@@ -1,4 +1,5 @@
 import functools
+import math
 
 import jax
 import jax.numpy as jnp
@@ -9,6 +10,7 @@
 
 BF16, F32 = jnp.bfloat16, jnp.float32
 MIB = 1 << 20
+PACK_WEIGHT, GATE_WEIGHT, UP_WEIGHT = 60_000_000_000, 10_000_000_000, 10_000_000_000
 TILE = 8
 
 
@@ -23,13 +25,15 @@
     return [pl.BlockSpec(memory_space=pltpu.VMEM)] * count
 
 
-def call(body, out_shape, operands, name, limit, scratch=(), flops=0):
+def call(body, out_shape, operands, name, scratch=(), flops=0, apart=(), spare=2 * MIB):
     single = not isinstance(out_shape, (list, tuple))
     shapes = [out_shape] if single else out_shape
+    held = [x for x in scratch if getattr(x, "dtype", None) in (BF16, F32)]
+    limit = spare + sum(math.prod(x.shape) * jnp.dtype(x.dtype).itemsize for x in held)
     moved = sum(x.size * x.dtype.itemsize for x in operands)
     return pl.pallas_call(
         body,
-        in_specs=whole(len(operands)),
+        in_specs=[pl.BlockSpec(memory_space=pl.ANY if i in apart else pltpu.VMEM) for i in range(len(operands))],
         out_specs=whole(1)[0] if single else whole(len(shapes)),
         out_shape=out_shape,
         scratch_shapes=list(scratch),
@@ -72,28 +76,40 @@
     return (shaped * scales[:, None, :]).astype(BF16).reshape(depth, width)
 
 
-def project(a_ref, codes_ref, scales_ref, store):
-    depth, width = codes_ref.shape
+def pieces(width, count):
+    if width % 128 or width < 128 * 2 * count:
+        return [(0, width)]
+    tiles = width // 128
+    ends = [0, tiles // 2, (3 * tiles + 2) // 4, tiles] if count == 3 else [tiles * k // count for k in range(count + 1)]
+    return [(128 * a, 128 * (b - a)) for a, b in zip(ends, ends[1:])]
+
+
+def project(a_ref, codes_ref, at, scales_ref, start, size):
+    depth = codes_ref.shape[0]
     block = depth // scales_ref.shape[0]
-    columns = divisor(width, 1664, 128)
     rows = divisor(depth, 512, 8 * block)
-
-    def step(j):
-        cols = pl.ds(j * columns if isinstance(j, int) else pl.multiple_of(j * columns, columns), columns)
-        total = jnp.zeros((a_ref.shape[0], columns), F32)
-        for k in range(0, depth, rows):
-            w = dequant(codes_ref[k : k + rows, cols], scales_ref[k // block : (k + rows) // block, cols])
-            total += jnp.dot(a_ref[:, k : k + rows], w, preferred_element_type=F32)
-        store(cols, total)
-
-    if width == columns:
-        step(0)
-    else:
-        pl.loop(0, width // columns)(step)
+    total = jnp.zeros((a_ref.shape[0], size), F32)
+    for k in range(0, depth, rows):
+        w = dequant(codes_ref[k : k + rows, at : at + size], scales_ref[k // block : (k + rows) // block, start : start + size])
+        total += jnp.dot(a_ref[:, k : k + rows], w, preferred_element_type=F32)
+    return total
+
+
+def fetch(source, start, size, target, at, done):
+    copy = pltpu.make_async_copy(source.at[:, start : start + size], target.at[:, at : at + size], done)
+    copy.start()
+    return copy
+
+
+def fetch_rest(source, cuts, target, done):
+    ahead = cuts[0][1]
+    return [fetch(source, start, size, target, start - ahead, done.at[i]) for i, (start, size) in enumerate(cuts[1:])]
 
 
 def gate_body(count, rest, *refs):
-    blocks, (codes, scales), (acts, own, sent), wide = refs[:count], refs[count : count + 2], refs[count + 2 : count + 5], refs[count + 5]
+    blocks = refs[:count]
+    codes, scales, later, acts, own, sent, head, wide, done = refs[count:]
+    copy = fetch(later, 0, head.shape[1], head, 0, done)
     total = sum(b.shape[0] for b in blocks) // TILE
     at = 0
     for ref in blocks:
@@ -104,31 +120,41 @@
             unpack_rows(ref[i * TILE : (i + 1) * TILE, :].astype(F32), rest, store)
             at += 1
     acts[...] = wide[...].astype(BF16)
-    up_body(acts, codes, scales, own, sent)
-
-
-def up_body(acts, codes, scales, own, sent):
-    def store(cols, total):
-        own[:, cols] = total
-        sent[:, cols] = total.astype(BF16)
-
-    project(acts, codes, scales, store)
-
-
-def down_body(rest, blocks, kept, *refs):
-    gate, gate_other, up, up_other, codes, scales = refs[:6]
-    outs, (hidden, terms) = refs[6:-2], refs[-2:]
+    for start, size in pieces(codes.shape[1], 2):
+        total = project(acts, codes, start, scales, start, size)
+        own[:, start : start + size] = total
+        sent[:, start : start + size] = total.astype(BF16)
+    copy.wait()
+
+
+def up_body(cuts, acts, first, codes, scales, later, own, sent, head, *refs):
+    ahead = first.shape[1]
+    rest = fetch_rest(codes, cuts, *refs[1:]) if len(cuts) > 1 else []
+    copy = fetch(later, 0, head.shape[1], head, 0, refs[0])
+    for i, (start, size) in enumerate(cuts):
+        if i:
+            rest[i - 1].wait()
+        total = project(acts, refs[1] if i else first, start - ahead if i else 0, scales, start, size)
+        own[:, start : start + size] = total
+        sent[:, start : start + size] = total.astype(BF16)
+    copy.wait()
+
+
+def down_body(cuts, rest, blocks, kept, two, gate, gate_other, up, up_other, head, codes, scales, *refs):
+    outs, (hidden, terms) = refs[: 1 + two], refs[1 + two : 3 + two]
+    held = refs[3 + two :]
+    ahead = head.shape[1]
+    copies = fetch_rest(codes, cuts, *held) if held else []
     width = divisor(hidden.shape[1], 512, 128)
     for c in range(0, hidden.shape[1], width):
         cols = slice(c, c + width)
         g = gate[:, cols] + gate_other[:, cols].astype(F32)
         u = up[:, cols] + up_other[:, cols].astype(F32)
         hidden[:, cols] = (jax.nn.silu(g) * u).astype(BF16)
-
-    def store(cols, total):
-        terms[:, cols] = total
-
-    project(hidden, codes, scales, store)
+    for i, (start, size) in enumerate(cuts):
+        if i:
+            copies[i - 1].wait()
+        terms[:, start : start + size] = project(hidden, held[0] if i else head, start - ahead if i else 0, scales, start, size)
     width = terms.shape[1]
     for i in range(blocks):
         main, left = pack_all(terms, i, rest, blocks)
@@ -154,6 +180,12 @@
         out[row : row + values.shape[0], column : column + values.shape[1]] = values.astype(out.dtype)
 
     unpack_rows(total, out.shape[0] - TILE, store)
+
+
+def rest_space(depth, cuts):
+    if len(cuts) == 1:
+        return []
+    return [pltpu.VMEM((depth, sum(size for _, size in cuts[1:])), BF16), pltpu.SemaphoreType.DMA((len(cuts) - 1,))]
 
 
 def local(peers, acts, gate_codes, gate_scales, up_codes, up_scales, down_codes, down_scales):
@@ -178,43 +210,47 @@
     def in_vmem(x):
         return pltpu.with_memory_space_constraint(x, pltpu.VMEM)
 
-    packed = call(pack_body, sds((TILE, dense), BF16), [acts], "pack", 4 * MIB)
+    packed = call(pack_body, sds((TILE, dense), BF16), [acts], "pack", flops=PACK_WEIGHT)
     if pair:
         line = [packed] + [along(packed, s) for s in range(1, far)]
         blocks = line + [flip(x) for x in line]
     else:
         blocks = [lax.all_gather(packed, "hidden", axis=0, tiled=True)]
-    work = 2 * rows * width * units
-    spare = 4 * rows * (width + 3 * units) + 12 * MIB
-    acts_all, gate, gate_sent = call(
+    spare = 2 * MIB + 4096 * rows
+    up_cuts, down_cuts = pieces(units, 3), pieces(width, 4)
+    acts_all, gate, gate_sent, up_head = call(
         functools.partial(gate_body, len(blocks), rest),
-        [sds((rows, width), BF16), sds((rows, units), F32), sds((rows, units), BF16)],
-        blocks + [in_vmem(gate_codes), gate_scales],
+        [sds((rows, width), BF16), sds((rows, units), F32), sds((rows, units), BF16), pltpu.VMEM((width, up_cuts[0][1]), BF16)],
+        blocks + [in_vmem(gate_codes), gate_scales, up_codes],
         "gate",
-        min(spare, 40 * MIB),
-        scratch=[pltpu.VMEM((rows, width), F32)],
-        flops=work,
+        scratch=[pltpu.VMEM((rows, width), F32), pltpu.SemaphoreType.DMA],
+        flops=GATE_WEIGHT,
+        spare=spare,
+        apart=(len(blocks) + 2,),
     )
     gate_other = swap(gate_sent)
-    up, up_sent = call(
-        up_body,
-        [sds((rows, units), F32), sds((rows, units), BF16)],
-        [acts_all, in_vmem(up_codes), up_scales],
+    up, up_sent, down_head = call(
+        functools.partial(up_body, up_cuts),
+        [sds((rows, units), F32), sds((rows, units), BF16), pltpu.VMEM((units, down_cuts[0][1]), BF16)],
+        [acts_all, in_vmem(up_head), up_codes, up_scales, down_codes],
         "up",
-        min(spare, 40 * MIB),
-        flops=work,
+        scratch=[pltpu.SemaphoreType.DMA] + rest_space(width, up_cuts),
+        flops=UP_WEIGHT,
+        spare=spare,
+        apart=(2, 4),
     )
     up_other = swap(up_sent)
     kept = far if pair else peers
     outs = [sds((kept * TILE, dense), F32)] + ([sds((far * TILE, dense), BF16)] if pair else [])
     parts = call(
-        functools.partial(down_body, rest, peers, kept),
+        functools.partial(down_body, down_cuts, rest, peers, kept, int(pair)),
         outs,
-        [gate, gate_other, up, up_other, in_vmem(down_codes), down_scales],
+        [gate, gate_other, up, up_other, in_vmem(down_head), down_codes, down_scales],
         "down",
-        min(4 * rows * (3 * width + 3 * units) + 8 * MIB, 48 * MIB),
-        scratch=[pltpu.VMEM((rows, units), BF16), pltpu.VMEM((rows, width), F32)],
-        flops=work,
+        scratch=[pltpu.VMEM((rows, units), BF16), pltpu.VMEM((rows, width), F32)] + rest_space(units, down_cuts),
+        flops=2 * rows * width * units,
+        spare=spare,
+        apart=(5,),
     )
     if pair:
         mine, sent = parts
@@ -224,12 +260,11 @@
             [sds((TILE, dense), F32)] + [sds((TILE, dense), BF16)] * (far - 1),
             [mine, other],
             "add",
-            8 * MIB,
         )
         terms = [sums[0]] + [along(x, far - s) for s, x in zip(range(1, far), sums[1:])]
     else:
         terms = [lax.psum_scatter(parts[0], "hidden", scatter_dimension=0, tiled=True)]
-    return call(last_body, sds((m, width), BF16), terms, "last", 8 * MIB)
+    return call(last_body, sds((m, width), BF16), terms, "last")
 
 
 def solution(mesh):

time: 91.3 us -> 69.1 us (0.76)
  local copies, waits for them, and re-layouts: 28.6 us -> 1.05 us
  Pallas kernels: 21.7 us -> 27.2 us
    unnamed x14 -> x10, local copies, waits for them, and re-layouts: 28.6 us -> 1.05 us
    pallas_call x6, Pallas kernels: 21.7 us -> 27.2 us  [call(): pl.pallas_call(body, in_specs=[pl.BlockSpec(memory_space=pl.ANY if i in a...]
  transfers between devices with their start and end apart: 13 -> 13, of which waited for: 8 -> 8; matrix products, arithmetic and copies ran while one was open for 0% -> 0% of each run, Pallas kernels for 7% -> 14%
where the time goes in v2:
time: 69.1 us; the launch traced here: 69 us
  Pallas kernels  27.2 us (39%)
  waiting for transfers between devices  25.1 us (36%)
  starting transfers between devices  15.6 us (23%)
  local copies, waits for them, and re-layouts  1.05 us (2%)
    pallas_call x6, Pallas kernels, call(): pl.pallas_call(body, in_specs=[pl.BlockSpec(memory_space=pl.ANY if i in a...  27.2 us
    ppermute x5, waiting for transfers between devices, flip(): return lax.ppermute(x, 'hidden', [(h, h ^ 1) for h in range(peers)])  12.9 us
    ppermute x6, waiting for transfers between devices, along(): lax.ppermute(x, 'hidden', [(h, (h + 2 * s) % peers) for h in range(peers)])  10.6 us
    ppermute x6, starting transfers between devices, along(): lax.ppermute(x, 'hidden', [(h, (h + 2 * s) % peers) for h in range(peers)])  8.72 us
    ppermute x5, starting transfers between devices, flip(): return lax.ppermute(x, 'hidden', [(h, h ^ 1) for h in range(peers)])  6.24 us
    ppermute x2, waiting for transfers between devices, swap(): return lax.ppermute(x, 'width', [(0, 1), (1, 0)])  1.55 us
  transfers between devices with their start and end apart: 13, of which 8 were waited for; matrix products, arithmetic and copies ran while one was open for 0% of the time, Pallas kernels for 14%

profile of v2, /device:TPU:0, one launch (start us, length us, event | category | flops | bytes accessed | tf_op | source)
XLA Modules:
  0.0 69.0 jit_solution(17152256989103594979)
XLA Ops:
  0.0 1.0 %copy-done.4 = bf16[10,4096]{1,0:T(8,128)(2,1)S(1)} copy-done((bf16[10,4096]{1,0:T(8,128)(2,1)S(1)}, bf16[10,4096]{1,0:T(8,128)(2,1)}, u32[]{:S(2)}) %copy-start.4) | copy-done | bytes 81944
  1.1 5.1 %collective-permute-start.2 = (bf16[8,5120]{1,0:T(8,128)(2,1)S(1)}, bf16[8,5120]{1,0:T(8,128)(2,1)S(1)}, u32[]{:S(2)}, u32[]{:S(2)}) collective-permute-start(bf16[8,5120]{1,0:T(8,128)(2,1)S(1)} %pack.1.refs_0_), channel_id=1, source_target_pairs={{0,6},{1,7},{2,0},{3,1},{4,2},{5,3},{6,4},{7,5},{8,14},{9,15},{10,... | collective-permute-start | bytes 245768 | tf_op jit(solution)/shard_map/ppermute | solution.py:205
  6.2 1.0 %collective-permute-start = (bf16[8,5120]{1,0:T(8,128)(2,1)S(1)}, bf16[8,5120]{1,0:T(8,128)(2,1)S(1)}, u32[]{:S(2)}, u32[]{:S(2)}) collective-permute-start(bf16[8,5120]{1,0:T(8,128)(2,1)S(1)} %pack.1.refs_0_), channel_id=1, source_target_pairs={{0,2},{1,3},{2,4},{3,5},{4,6},{5,7},{6,0},{7,1},{8,10},{9,11},{10,... | collective-permute-start | bytes 245768 | tf_op jit(solution)/shard_map/ppermute | solution.py:205
  7.2 1.5 %collective-permute-start.3 = (bf16[8,5120]{1,0:T(8,128)(2,1)S(1)}, bf16[8,5120]{1,0:T(8,128)(2,1)S(1)}, u32[]{:S(2)}, u32[]{:S(2)}) collective-permute-start(bf16[8,5120]{1,0:T(8,128)(2,1)S(1)} %pack.1.refs_0_), channel_id=1, source_target_pairs={{0,1},{1,0},{2,3},{3,2},{4,5},{5,4},{6,7},{7,6},{8,9},{9,8},{10,11... | collective-permute-start | bytes 245768 | tf_op jit(solution)/shard_map/ppermute | solution.py:202
  8.7 0.3 collective-permute-done.2.refs_3_
  9.0 1.5 %collective-permute-start.6 = (bf16[8,5120]{1,0:T(8,128)(2,1)S(1)}, bf16[8,5120]{1,0:T(8,128)(2,1)S(1)}, u32[]{:S(2)}, u32[]{:S(2)}) collective-permute-start(bf16[8,5120]{1,0:T(8,128)(2,1)S(1)} %collective-permute-done.2.refs_3_), channel_id=1, source_target_pairs={{0,1},{1,0},{2,3},{3,2},{4,5},{5,4},{6,7},{7,6},{8,9},{9,8},{10,11... | collective-permute-start | bytes 245768 | tf_op jit(solution)/shard_map/ppermute | solution.py:202
  10.5 3.2 %collective-permute-done.1.refs_2_ = bf16[8,5120]{1,0:T(8,128)(2,1)S(1)} collective-permute-done((bf16[8,5120]{1,0:T(8,128)(2,1)S(1)}, bf16[8,5120]{1,0:T(8,128)(2,1)S(1)}, u32[]{:S(2)}, u32[]{:S(2)}) %collective-permute-start.1) | collective-permute-done | bytes 81952 | tf_op jit(solution)/shard_map/ppermute | solution.py:205
  13.7 1.5 %collective-permute-start.5 = (bf16[8,5120]{1,0:T(8,128)(2,1)S(1)}, bf16[8,5120]{1,0:T(8,128)(2,1)S(1)}, u32[]{:S(2)}, u32[]{:S(2)}) collective-permute-start(bf16[8,5120]{1,0:T(8,128)(2,1)S(1)} %collective-permute-done.1.refs_2_), channel_id=1, source_target_pairs={{0,1},{1,0},{2,3},{3,2},{4,5},{5,4},{6,7},{7,6},{8,9},{9,8},{10,11... | collective-permute-start | bytes 245768 | tf_op jit(solution)/shard_map/ppermute | solution.py:202
  15.2 0.5 collective-permute-start.4
  15.7 3.2 %collective-permute-done.5.refs_6_ = bf16[8,5120]{1,0:T(8,128)(2,1)S(1)} collective-permute-done((bf16[8,5120]{1,0:T(8,128)(2,1)S(1)}, bf16[8,5120]{1,0:T(8,128)(2,1)S(1)}, u32[]{:S(2)}, u32[]{:S(2)}) %collective-permute-start.5) | collective-permute-done | bytes 81952 | tf_op jit(solution)/shard_map/ppermute | solution.py:202
  19.0 0.9 %collective-permute-done.4.refs_5_ = bf16[8,5120]{1,0:T(8,128)(2,1)S(1)} collective-permute-done((bf16[8,5120]{1,0:T(8,128)(2,1)S(1)}, bf16[8,5120]{1,0:T(8,128)(2,1)S(1)}, u32[]{:S(2)}, u32[]{:S(2)}) %collective-permute-start.4) | collective-permute-done | bytes 81952 | tf_op jit(solution)/shard_map/ppermute | solution.py:202
  19.8 6.7 %gate.1 = (bf16[80,4096]{1,0:T(8,128)(2,1)S(1)}, f32[80,3328]{1,0:T(8,128)S(1)}, bf16[80,3328]{1,0:T(8,128)(2,1)S(1)}, bf16[4096,1664]{1,0:T(8,128)(2,1)S(1)}) custom-call(bf16[8,5120]{1,0:T(8,128)(2,1)S(1)} %pack.1.refs_0_, bf16[8,5120]{1,0:T(8,128)(2,1)S(1)} %collective-permute-done.refs_1_, bf16[8,5120]{1,0:T(8,128)(2,1)S(1)} %collective-permute-done.1.refs_2_, ...), custom_call_target="tpu_custom_call" | custom-call | flops 10000000000 | bytes 56885248 | tf_op jit(solution)/shard_map/gate/pallas_call | solution.py:34
  26.6 9.3 %up.1 = (f32[80,3328]{1,0:T(8,128)S(1)}, bf16[80,3328]{1,0:T(8,128)(2,1)S(1)}, bf16[3328,1024]{1,0:T(8,128)(2,1)S(1)}) custom-call(bf16[80,4096]{1,0:T(8,128)(2,1)S(1)} %get-tuple-element.20.acts, bf16[4096,1664]{1,0:T(8,128)(2,1)S(1)} %get-tuple-element.21.first, bf16[4096,3328]{1,0:T(8,128)(2,1)} %codes.2, f32[128,3328]{1,0:T(8,128)S(1)} %copy-done.2, ...), custom_call_target="tpu_custom_call" | custom-call | flops 10000000000 | bytes 70516736 | tf_op jit(solution)/shard_map/up/pallas_call | solution.py:34
  36.0 0.5 collective-permute-start.8
  36.5 1.5 %collective-permute-done.8.up_other = bf16[80,3328]{1,0:T(8,128)(2,1)S(1)} collective-permute-done((bf16[80,3328]{1,0:T(8,128)(2,1)S(1)}, bf16[80,3328]{1,0:T(8,128)(2,1)S(1)}, u32[]{:S(2)}, u32[]{:S(2)}) %collective-permute-start.8) | collective-permute-done | bytes 532512 | tf_op jit(solution)/shard_map/ppermute | solution.py:208
  38.1 10.4 %down.1 = (f32[32,5120]{1,0:T(8,128)S(1)}, bf16[32,5120]{1,0:T(8,128)(2,1)S(1)}) custom-call(f32[80,3328]{1,0:T(8,128)S(1)} %get-tuple-element.18.gate, bf16[80,3328]{1,0:T(8,128)(2,1)S(1)} %collective-permute-done.7.gate_other, f32[80,3328]{1,0:T(8,128)S(1)} %get-tuple-element.22.up, bf16[80,3328]{1,0:T(8,128)(2,1)S(1)} %collective-permute-done.8.up_other, ...), custom_call_target="tpu_custom_call" | custom-call | flops 2181038080 | bytes 38977536 | tf_op jit(solution)/shard_map/down/pallas_call | solution.py:34
  48.5 1.2 %collective-permute-start.9 = (bf16[32,5120]{1,0:T(8,128)(2,1)S(1)}, bf16[32,5120]{1,0:T(8,128)(2,1)S(1)}, u32[]{:S(2)}, u32[]{:S(2)}) collective-permute-start(bf16[32,5120]{1,0:T(8,128)(2,1)S(1)} %get-tuple-element.26), channel_id=1, source_target_pairs={{0,1},{1,0},{2,3},{3,2},{4,5},{5,4},{6,7},{7,6},{8,9},{9,8},{10,11... | collective-permute-start | bytes 983048 | tf_op jit(solution)/shard_map/ppermute | solution.py:202
  49.7 8.8 %collective-permute-done.9.other = bf16[32,5120]{1,0:T(8,128)(2,1)S(1)} collective-permute-done((bf16[32,5120]{1,0:T(8,128)(2,1)S(1)}, bf16[32,5120]{1,0:T(8,128)(2,1)S(1)}, u32[]{:S(2)}, u32[]{:S(2)}) %collective-permute-start.9) | collective-permute-done | bytes 327712 | tf_op jit(solution)/shard_map/ppermute | solution.py:202
  58.5 0.1 add.1
  58.6 2.0 %collective-permute-start.10 = (bf16[8,5120]{1,0:T(8,128)(2,1)S(1)}, bf16[8,5120]{1,0:T(8,128)(2,1)S(1)}, u32[]{:S(2)}, u32[]{:S(2)}) collective-permute-start(bf16[8,5120]{1,0:T(8,128)(2,1)S(1)} %get-tuple-element.28), channel_id=1, source_target_pairs={{0,6},{1,7},{2,0},{3,1},{4,2},{5,3},{6,4},{7,5},{8,14},{9,15},{10,... | collective-permute-start | bytes 245768 | tf_op jit(solution)/shard_map/ppermute | solution.py:205
  60.6 0.6 collective-permute-start.12
  61.2 2.3 %collective-permute-done.10.refs_1_ = bf16[8,5120]{1,0:T(8,128)(2,1)S(1)} collective-permute-done((bf16[8,5120]{1,0:T(8,128)(2,1)S(1)}, bf16[8,5120]{1,0:T(8,128)(2,1)S(1)}, u32[]{:S(2)}, u32[]{:S(2)}) %collective-permute-start.10) | collective-permute-done | bytes 81952 | tf_op jit(solution)/shard_map/ppermute | solution.py:205
  63.5 4.8 %collective-permute-done.11.refs_2_ = bf16[8,5120]{1,0:T(8,128)(2,1)S(1)} collective-permute-done((bf16[8,5120]{1,0:T(8,128)(2,1)S(1)}, bf16[8,5120]{1,0:T(8,128)(2,1)S(1)}, u32[]{:S(2)}, u32[]{:S(2)}) %collective-permute-start.11) | collective-permute-done | bytes 81952 | tf_op jit(solution)/shard_map/ppermute | solution.py:205
  68.3 0.7 %last.1 = bf16[10,4096]{1,0:T(8,128)(2,1)} custom-call(f32[8,5120]{1,0:T(8,128)S(1)} %get-tuple-element.27.refs_0_, bf16[8,5120]{1,0:T(8,128)(2,1)S(1)} %collective-permute-done.10.refs_1_, bf16[8,5120]{1,0:T(8,128)(2,1)S(1)} %collective-permute-done.11.refs_2_, bf16[8,5120]{1,0:T(8,128)(2,1)S(1)} %collective-permute-done.12.refs_3_), custom_call_target="tpu_custom_call" | custom-call | bytes 409600 | tf_op jit(solution)/shard_map/last/pallas_call | solution.py:34
  (18 shorter events, 0.1 us)
Async XLA Ops:
  0.0 19.8 %copy-start.1 = (f32[128,3328]{1,0:T(8,128)S(1)}, f32[128,3328]{1,0:T(8,128)}, u32[]{:S(2)}) copy-start(f32[128,3328]{1,0:T(8,128)} %refs_9_.1) | copy-start | bytes 5111812
  0.0 1.0 %copy-start.4 = (bf16[10,4096]{1,0:T(8,128)(2,1)S(1)}, bf16[10,4096]{1,0:T(8,128)(2,1)}, u32[]{:S(2)}) copy-start(bf16[10,4096]{1,0:T(8,128)(2,1)} %a_ref.1) | copy-start | bytes 245764
  1.0 18.8 %copy-start = (bf16[4096,3328]{1,0:T(8,128)(2,1)S(1)}, bf16[4096,3328]{1,0:T(8,128)(2,1)}, u32[]{:S(2)}) copy-start(bf16[4096,3328]{1,0:T(8,128)(2,1)} %refs_8_.1) | copy-start | bytes 81788928
  1.1 25.6 %copy-start.2 = (f32[128,3328]{1,0:T(8,128)S(1)}, f32[128,3328]{1,0:T(8,128)}, u32[]{:S(2)}) copy-start(f32[128,3328]{1,0:T(8,128)} %scales.2) | copy-start | bytes 5111812
  1.1 8.0 %collective-permute-start.2 = (bf16[8,5120]{1,0:T(8,128)(2,1)S(1)}, bf16[8,5120]{1,0:T(8,128)(2,1)S(1)}, u32[]{:S(2)}, u32[]{:S(2)}) collective-permute-start(bf16[8,5120]{1,0:T(8,128)(2,1)S(1)} %pack.1.refs_0_), channel_id=1, source_target_pairs={{0,6},{1,7},{2,0},{3,1},{4,2},{5,3},{6,4},{7,5},{8,14},{9,15},{10,... | collective-permute-start | bytes 245768 | tf_op jit(solution)/shard_map/ppermute | solution.py:205
  6.2 7.5 %collective-permute-start.1 = (bf16[8,5120]{1,0:T(8,128)(2,1)S(1)}, bf16[8,5120]{1,0:T(8,128)(2,1)S(1)}, u32[]{:S(2)}, u32[]{:S(2)}) collective-permute-start(bf16[8,5120]{1,0:T(8,128)(2,1)S(1)} %pack.1.refs_0_), channel_id=1, source_target_pairs={{0,4},{1,5},{2,6},{3,7},{4,0},{5,1},{6,2},{7,3},{8,12},{9,13},{10,... | collective-permute-start | bytes 245768 | tf_op jit(solution)/shard_map/ppermute | solution.py:205
  6.2 9.0 %collective-permute-start = (bf16[8,5120]{1,0:T(8,128)(2,1)S(1)}, bf16[8,5120]{1,0:T(8,128)(2,1)S(1)}, u32[]{:S(2)}, u32[]{:S(2)}) collective-permute-start(bf16[8,5120]{1,0:T(8,128)(2,1)S(1)} %pack.1.refs_0_), channel_id=1, source_target_pairs={{0,2},{1,3},{2,4},{3,5},{4,6},{5,7},{6,0},{7,1},{8,10},{9,11},{10,... | collective-permute-start | bytes 245768 | tf_op jit(solution)/shard_map/ppermute | solution.py:205
  7.2 8.5 %collective-permute-start.3 = (bf16[8,5120]{1,0:T(8,128)(2,1)S(1)}, bf16[8,5120]{1,0:T(8,128)(2,1)S(1)}, u32[]{:S(2)}, u32[]{:S(2)}) collective-permute-start(bf16[8,5120]{1,0:T(8,128)(2,1)S(1)} %pack.1.refs_0_), channel_id=1, source_target_pairs={{0,1},{1,0},{2,3},{3,2},{4,5},{5,4},{6,7},{7,6},{8,9},{9,8},{10,11... | collective-permute-start | bytes 245768 | tf_op jit(solution)/shard_map/ppermute | solution.py:202
  9.0 6.7 %collective-permute-start.6 = (bf16[8,5120]{1,0:T(8,128)(2,1)S(1)}, bf16[8,5120]{1,0:T(8,128)(2,1)S(1)}, u32[]{:S(2)}, u32[]{:S(2)}) collective-permute-start(bf16[8,5120]{1,0:T(8,128)(2,1)S(1)} %collective-permute-done.2.refs_3_), channel_id=1, source_target_pairs={{0,1},{1,0},{2,3},{3,2},{4,5},{5,4},{6,7},{7,6},{8,9},{9,8},{10,11... | collective-permute-start | bytes 245768 | tf_op jit(solution)/shard_map/ppermute | solution.py:202
  13.7 5.3 %collective-permute-start.5 = (bf16[8,5120]{1,0:T(8,128)(2,1)S(1)}, bf16[8,5120]{1,0:T(8,128)(2,1)S(1)}, u32[]{:S(2)}, u32[]{:S(2)}) collective-permute-start(bf16[8,5120]{1,0:T(8,128)(2,1)S(1)} %collective-permute-done.1.refs_2_), channel_id=1, source_target_pairs={{0,1},{1,0},{2,3},{3,2},{4,5},{5,4},{6,7},{7,6},{8,9},{9,8},{10,11... | collective-permute-start | bytes 245768 | tf_op jit(solution)/shard_map/ppermute | solution.py:202
  15.2 4.7 %collective-permute-start.4 = (bf16[8,5120]{1,0:T(8,128)(2,1)S(1)}, bf16[8,5120]{1,0:T(8,128)(2,1)S(1)}, u32[]{:S(2)}, u32[]{:S(2)}) collective-permute-start(bf16[8,5120]{1,0:T(8,128)(2,1)S(1)} %collective-permute-done.refs_1_), channel_id=1, source_target_pairs={{0,1},{1,0},{2,3},{3,2},{4,5},{5,4},{6,7},{7,6},{8,9},{9,8},{10,11... | collective-permute-start | bytes 245768 | tf_op jit(solution)/shard_map/ppermute | solution.py:202
  26.5 10.0 %collective-permute-start.7 = (bf16[80,3328]{1,0:T(8,128)(2,1)S(1)}, bf16[80,3328]{1,0:T(8,128)(2,1)S(1)}, u32[]{:S(2)}, u32[]{:S(2)}) collective-permute-start(bf16[80,3328]{1,0:T(8,128)(2,1)S(1)} %get-tuple-element.19), channel_id=1, source_target_pairs={{0,8},{8,0},{1,9},{9,1},{2,10},{10,2},{3,11},{11,3},{4,12},{12,4},... | collective-permute-start | bytes 1597448 | tf_op jit(solution)/shard_map/ppermute | solution.py:208
  26.6 11.4 %copy-start.3 = (f32[104,4096]{1,0:T(8,128)S(1)}, f32[104,4096]{1,0:T(8,128)}, u32[]{:S(2)}) copy-start(f32[104,4096]{1,0:T(8,128)} %scales.3) | copy-start | bytes 5111812
  36.0 2.1 %collective-permute-start.8 = (bf16[80,3328]{1,0:T(8,128)(2,1)S(1)}, bf16[80,3328]{1,0:T(8,128)(2,1)S(1)}, u32[]{:S(2)}, u32[]{:S(2)}) collective-permute-start(bf16[80,3328]{1,0:T(8,128)(2,1)S(1)} %get-tuple-element.23), channel_id=1, source_target_pairs={{0,8},{8,0},{1,9},{9,1},{2,10},{10,2},{3,11},{11,3},{4,12},{12,4},... | collective-permute-start | bytes 1597448 | tf_op jit(solution)/shard_map/ppermute | solution.py:208
  48.5 10.1 %collective-permute-start.9 = (bf16[32,5120]{1,0:T(8,128)(2,1)S(1)}, bf16[32,5120]{1,0:T(8,128)(2,1)S(1)}, u32[]{:S(2)}, u32[]{:S(2)}) collective-permute-start(bf16[32,5120]{1,0:T(8,128)(2,1)S(1)} %get-tuple-element.26), channel_id=1, source_target_pairs={{0,1},{1,0},{2,3},{3,2},{4,5},{5,4},{6,7},{7,6},{8,9},{9,8},{10,11... | collective-permute-start | bytes 983048 | tf_op jit(solution)/shard_map/ppermute | solution.py:202
  58.6 4.9 %collective-permute-start.10 = (bf16[8,5120]{1,0:T(8,128)(2,1)S(1)}, bf16[8,5120]{1,0:T(8,128)(2,1)S(1)}, u32[]{:S(2)}, u32[]{:S(2)}) collective-permute-start(bf16[8,5120]{1,0:T(8,128)(2,1)S(1)} %get-tuple-element.28), channel_id=1, source_target_pairs={{0,6},{1,7},{2,0},{3,1},{4,2},{5,3},{6,4},{7,5},{8,14},{9,15},{10,... | collective-permute-start | bytes 245768 | tf_op jit(solution)/shard_map/ppermute | solution.py:205
  60.6 7.7 %collective-permute-start.11 = (bf16[8,5120]{1,0:T(8,128)(2,1)S(1)}, bf16[8,5120]{1,0:T(8,128)(2,1)S(1)}, u32[]{:S(2)}, u32[]{:S(2)}) collective-permute-start(bf16[8,5120]{1,0:T(8,128)(2,1)S(1)} %get-tuple-element.29), channel_id=1, source_target_pairs={{0,4},{1,5},{2,6},{3,7},{4,0},{5,1},{6,2},{7,3},{8,12},{9,13},{10,... | collective-permute-start | bytes 245768 | tf_op jit(solution)/shard_map/ppermute | solution.py:205
  60.6 7.7 %collective-permute-start.12 = (bf16[8,5120]{1,0:T(8,128)(2,1)S(1)}, bf16[8,5120]{1,0:T(8,128)(2,1)S(1)}, u32[]{:S(2)}, u32[]{:S(2)}) collective-permute-start(bf16[8,5120]{1,0:T(8,128)(2,1)S(1)} %get-tuple-element.30), channel_id=1, source_target_pairs={{0,2},{1,3},{2,4},{3,5},{4,6},{5,7},{6,0},{7,1},{8,10},{9,11},{10,... | collective-permute-start | bytes 245768 | tf_op jit(solution)/shard_map/ppermute | solution.py:205

commit v3 on v2

v3 whole, which is shorter than its diff:
```python
import functools
import math

import jax
import jax.numpy as jnp
from jax import lax
from jax.experimental import pallas as pl
from jax.experimental.pallas import tpu as pltpu
from jax.sharding import PartitionSpec as P

BF16, F32 = jnp.bfloat16, jnp.float32
MIB = 1 << 20
PACK_WEIGHT, GATE_WEIGHT, UP_WEIGHT = 60_000_000_000, 10_000_000_000, 10_000_000_000
TILE = 8


def divisor(extent, limit, step):
    for size in range(limit - limit % step, 0, -step):
        if extent % size == 0:
            return size
    return extent


def whole(count):
    return [pl.BlockSpec(memory_space=pltpu.VMEM)] * count


def call(body, out_shape, operands, name, scratch=(), flops=0, apart=(), spare=2 * MIB):
    single = not isinstance(out_shape, list)
    shapes = [out_shape] if single else out_shape
    operands = [pltpu.with_memory_space_constraint(x, pltpu.HBM) if i in apart else x for i, x in enumerate(operands)]
    held = [x for x in scratch if getattr(x, "dtype", None) in (BF16, F32)]
    limit = spare + sum(math.prod(x.shape) * jnp.dtype(x.dtype).itemsize for x in held)
    moved = sum(x.size * x.dtype.itemsize for x in operands)
    return pl.pallas_call(
        body,
        in_specs=[pl.BlockSpec(memory_space=pltpu.HBM if i in apart else pltpu.VMEM) for i in range(len(operands))],
        out_specs=whole(1)[0] if single else whole(len(shapes)),
        out_shape=out_shape,
        scratch_shapes=list(scratch),
        compiler_params=pltpu.CompilerParams(vmem_limit_bytes=limit),
        cost_estimate=pl.CostEstimate(flops=flops, bytes_accessed=moved, transcendentals=0),
        name=name,
    )(*operands)


def pack_body(a_ref, o_ref):
    m, width = a_ref.shape
    rest = m - TILE
    piece = rest * width // TILE
    a = a_ref[...].astype(F32)
    o_ref[:, :width] = a[:TILE].astype(BF16)
    left = [a[TILE:, k * piece : (k + 1) * piece] for k in range(TILE // rest)]
    o_ref[:, width:] = jnp.concatenate(left, axis=0).astype(BF16)


def unpack_rows(block, rest, store):
    width = block.shape[1] * TILE // (TILE + rest)
    piece = rest * width // TILE
    store(0, 0, block[:, :width])
    for k in range(TILE // rest):
        store(TILE, k * piece, block[k * rest : (k + 1) * rest, width:])


def pack_all(total, first, rest, blocks):
    width = total.shape[1]
    piece = rest * width // TILE
    base = blocks * TILE + first * rest
    left = [total[base : base + rest, k * piece : (k + 1) * piece] for k in range(TILE // rest)]
    return total[first * TILE : (first + 1) * TILE, :], jnp.concatenate(left, axis=0)


def dequant(codes, scales):
    depth, width = codes.shape
    groups = scales.shape[0]
    shaped = codes.astype(F32).reshape(groups, depth // groups, width)
    return (shaped * scales[:, None, :]).astype(BF16).reshape(depth, width)


def pieces(width, shares):
    tiles, total = width // 128, sum(shares)
    if width % 128 or tiles < total:
        return [(0, width)]
    ends = [tiles * sum(shares[:k]) // total for k in range(len(shares) + 1)]
    return [(128 * a, 128 * (b - a)) for a, b in zip(ends, ends[1:])]


def project(a_ref, codes_ref, at, scales_ref, start, size):
    depth = codes_ref.shape[0]
    block = depth // scales_ref.shape[0]
    rows = divisor(depth, 512, 8 * block)
    total = jnp.zeros((a_ref.shape[0], size), F32)
    for k in range(0, depth, rows):
        w = dequant(codes_ref[k : k + rows, at : at + size], scales_ref[k // block : (k + rows) // block, start : start + size])
        total += jnp.dot(a_ref[:, k : k + rows], w, preferred_element_type=F32)
    return total


class Copies:
    def __init__(self, *wanted):
        self.waiting, self.started = list(wanted), {}
        self.start()

    def start(self):
        if self.waiting:
            source, start, size, target, at, done = self.waiting.pop(0)
            copy = pltpu.make_async_copy(source.at[:, start : start + size], target.at[:, at : at + size], done)
            copy.start()
            self.started[len(self.started)] = copy

    def wait(self, number):
        while number not in self.started:
            self.start()
        self.started[number].wait()


def gate_body(count, rest, *refs):
    blocks = refs[:count]
    codes, scales, later, acts, own, sent, head, wide, done = refs[count:]
    copy = Copies((later, 0, head.shape[1], head, 0, done))
    total = sum(b.shape[0] for b in blocks) // TILE
    at = 0
    for ref in blocks:
        for i in range(ref.shape[0] // TILE):
            def store(row, column, values):
                first = at * TILE if row == 0 else total * TILE + at * rest
                wide[first : first + values.shape[0], column : column + values.shape[1]] = values
            unpack_rows(ref[i * TILE : (i + 1) * TILE, :].astype(F32), rest, store)
            at += 1
    acts[...] = wide[...].astype(BF16)
    for start, size in pieces(codes.shape[1], (1, 1)):
        total = project(acts, codes, start, scales, start, size)
        own[:, start : start + size] = total
        sent[:, start : start + size] = total.astype(BF16)
    copy.wait(0)


def up_body(cuts, acts, first, codes, scales, later, own, sent, head, done, *tail):
    ahead = first.shape[1]
    ours = [(start, size) for start, size in cuts if start >= ahead]
    wanted = [(codes, start, size, tail[0], start - ahead, done.at[i]) for i, (start, size) in enumerate(ours)]
    copies = Copies(*wanted, (later, 0, head.shape[1], head, 0, done.at[len(ours)]))
    for start, size in cuts:
        if start < ahead:
            total = project(acts, first, start, scales, start, size)
        else:
            copies.wait(ours.index((start, size)))
            total = project(acts, tail[0], start - ahead, scales, start, size)
        copies.start()
        own[:, start : start + size] = total
        sent[:, start : start + size] = total.astype(BF16)
    copies.wait(len(ours))


def emit(terms, blocks, rest, outs):
    width = terms.shape[1]
    kept = outs[0].shape[0] // TILE
    for i in range(blocks):
        main, left = pack_all(terms, i, rest, blocks)
        out, at = (outs[0], i) if i < kept else (outs[1], i - kept)
        out[at * TILE : (at + 1) * TILE, :width] = main.astype(out.dtype)
        out[at * TILE : (at + 1) * TILE, width:] = left.astype(out.dtype)


def first_body(rest, blocks, gate, gate_other, up, up_other, codes, later, scales, *refs):
    *outs, hidden, head, terms, tail, done = refs
    size = codes.shape[1]
    copies = Copies((later, size, size, tail, 0, done.at[0]), (later, 2 * size, size, head, 0, done.at[1]))
    width = divisor(hidden.shape[1], 512, 128)
    for c in range(0, hidden.shape[1], width):
        cols = slice(c, c + width)
        g = gate[:, cols] + gate_other[:, cols].astype(F32)
        u = up[:, cols] + up_other[:, cols].astype(F32)
        hidden[:, cols] = (jax.nn.silu(g) * u).astype(BF16)
    terms[:, :size] = project(hidden, codes, 0, scales, 0, size)
    copies.wait(0)
    copies.start()
    terms[:, size:] = project(hidden, tail, 0, scales, size, size)
    emit(terms, blocks, rest, outs)
    copies.wait(1)


def second_body(rest, blocks, hidden, codes, later, scales, *refs):
    *outs, terms, tail, done = refs
    size = codes.shape[1]
    copies = Copies((later, 3 * size, size, tail, 0, done))
    terms[:, :size] = project(hidden, codes, 0, scales, 2 * size, size)
    copies.wait(0)
    terms[:, size:] = project(hidden, tail, 0, scales, 3 * size, size)
    emit(terms, blocks, rest, outs)


def add_body(count, *refs):
    halves, outs = refs[: 2 * count], refs[2 * count :]
    width = halves[0].shape[1]
    for i, ref in enumerate(outs):
        rows = slice(i * TILE, (i + 1) * TILE)
        for k in range(count):
            total = halves[2 * k][rows, :] + halves[2 * k + 1][rows, :].astype(F32)
            ref[:, k * width : (k + 1) * width] = total.astype(ref.dtype)


def last_body(halves, *refs):
    out = refs[-1]
    total = refs[0][...]
    for ref in refs[1:-1]:
        total += ref[...].astype(F32)
    dense, width = total.shape[1] // halves, out.shape[1] // halves
    for k in range(halves):
        def store(row, column, values):
            column += k * width
            out[row : row + values.shape[0], column : column + values.shape[1]] = values.astype(out.dtype)

        unpack_rows(total[:, k * dense : (k + 1) * dense], out.shape[0] - TILE, store)


def local(peers, acts, gate_codes, gate_scales, up_codes, up_scales, down_codes, down_scales):
    m, width = acts.shape
    units = gate_codes.shape[1]
    rest = m - TILE
    dense = width + rest * width // TILE
    rows = peers * m
    sds = jax.ShapeDtypeStruct
    pair = peers == 8
    far = peers // 2

    def flip(x):
        return lax.ppermute(x, "hidden", [(h, h ^ 1) for h in range(peers)])

    def along(x, s):
        return lax.ppermute(x, "hidden", [(h, (h + 2 * s) % peers) for h in range(peers)])

    def swap(x):
        return lax.ppermute(x, "width", [(0, 1), (1, 0)])

    def in_vmem(x):
        return pltpu.with_memory_space_constraint(x, pltpu.VMEM)

    packed = call(pack_body, sds((TILE, dense), BF16), [acts], "pack", flops=PACK_WEIGHT)
    if pair:
        line = [packed] + [along(packed, s) for s in range(1, far)]
        blocks = line + [flip(x) for x in line]
    else:
        blocks = [lax.all_gather(packed, "hidden", axis=0, tiled=True)]
    spare = 2 * MIB + 4096 * rows
    half, packed_half = width // 2, dense // 2
    quarter = half // 2
    cuts = pieces(units, (1, 1, 1, 1))
    ahead = sum(size for _, size in cuts[:2])
    acts_all, gate, gate_sent, up_head = call(
        functools.partial(gate_body, len(blocks), rest),
        [sds((rows, width), BF16), sds((rows, units), F32), sds((rows, units), BF16), pltpu.VMEM((width, ahead), BF16)],
        blocks + [in_vmem(gate_codes), gate_scales, up_codes],
        "gate",
        scratch=[pltpu.VMEM((rows, width), F32), pltpu.SemaphoreType.DMA],
        flops=GATE_WEIGHT,
        spare=spare,
        apart=(len(blocks) + 2,),
    )
    gate_other = swap(gate_sent)
    tail = [pltpu.VMEM((width, units - ahead), BF16)] if ahead < units else []
    up, up_sent, down_head = call(
        functools.partial(up_body, cuts),
        [sds((rows, units), F32), sds((rows, units), BF16), pltpu.VMEM((units, quarter), BF16)],
        [acts_all, in_vmem(up_head), up_codes, up_scales, down_codes],
        "up",
        scratch=[pltpu.SemaphoreType.DMA((max(len(cuts) - 1, 1),))] + tail,
        flops=UP_WEIGHT,
        spare=spare + 4 * MIB,
        apart=(2, 4),
    )
    up_other = swap(up_sent)
    kept = far if pair else peers
    outs = [sds((kept * TILE, packed_half), F32)] + ([sds((far * TILE, packed_half), BF16)] if pair else [])
    work = rows * width * units
    *first, hidden, down_rest = call(
        functools.partial(first_body, rest, peers),
        outs + [sds((rows, units), BF16), pltpu.VMEM((units, quarter), BF16)],
        [gate, gate_other, up, up_other, in_vmem(down_head), down_codes, down_scales],
        "first",
        scratch=[pltpu.VMEM((rows, half), F32), pltpu.VMEM((units, quarter), BF16), pltpu.SemaphoreType.DMA((2,))],
        flops=work,
        spare=spare,
        apart=(5,),
    )
    if pair:
        first_other = flip(first[1])
    second = call(
        functools.partial(second_body, rest, peers),
        outs,
        [hidden, in_vmem(down_rest), down_codes, down_scales],
        "second",
        scratch=[pltpu.VMEM((rows, half), F32), pltpu.VMEM((units, quarter), BF16), pltpu.SemaphoreType.DMA],
        flops=work,
        spare=spare,
        apart=(2,),
    )
    if pair:
        sums = call(
            functools.partial(add_body, 2),
            [sds((TILE, dense), F32)] + [sds((TILE, dense), BF16)] * (far - 1),
            [first[0], first_other, second[0], flip(second[1])],
            "add",
        )
        terms = [sums[0]] + [along(x, far - s) for s, x in zip(range(1, far), sums[1:])]
    else:
        both = jnp.concatenate([first[0], second[0]], axis=1)
        terms = [lax.psum_scatter(both, "hidden", scatter_dimension=0, tiled=True)]
    return call(functools.partial(last_body, 2), sds((m, width), BF16), terms, "last")


def solution(mesh):
    placed = (
        P(("replica", "hidden"), "width"),
        P("width", "hidden"),
        P("width", "hidden"),
        P("width", "hidden"),
        P("width", "hidden"),
        P("hidden", "width"),
        P("hidden", "width"),
    )
    return jax.shard_map(
        functools.partial(local, mesh.shape["hidden"]),
        mesh=mesh,
        in_specs=placed,
        out_specs=P(("replica", "hidden"), "width"),
        check_vma=False,
    )
```

time: 69.1 us -> 67.8 us (0.981)
  waiting for transfers between devices: 25.1 us -> 21 us
  Pallas kernels: 27.2 us -> 28.7 us
  starting transfers between devices: 15.6 us -> 16.7 us
    ppermute x5 -> x6, waiting for transfers between devices: 12.9 us -> 9.43 us  [flip(): return lax.ppermute(x, 'hidden', [(h, h ^ 1) for h in range(peers)])]
    pallas_call x6 -> x7, Pallas kernels: 27.2 us -> 28.7 us  [call(): pl.pallas_call(body, in_specs=[pl.BlockSpec(memory_space=pltpu.HBM if i i...]
    ppermute x5 -> x6, starting transfers between devices: 6.24 us -> 7.18 us  [flip(): return lax.ppermute(x, 'hidden', [(h, h ^ 1) for h in range(peers)])]
  transfers between devices with their start and end apart: 13 -> 14, of which waited for: 8 -> 8; matrix products, arithmetic and copies ran while one was open for 0% -> 0% of each run, Pallas kernels for 14% -> 20%
where the time goes in v3:
time: 67.8 us; the launch traced here: 67.6 us
  Pallas kernels  28.7 us (42%)
  waiting for transfers between devices  21 us (31%)
  starting transfers between devices  16.7 us (25%)
  local copies, waits for them, and re-layouts  1.05 us (2%)
    pallas_call x7, Pallas kernels, call(): pl.pallas_call(body, in_specs=[pl.BlockSpec(memory_space=pltpu.HBM if i i...  28.7 us
    ppermute x6, waiting for transfers between devices, along(): lax.ppermute(x, 'hidden', [(h, (h + 2 * s) % peers) for h in range(peers)])  10 us
    ppermute x6, waiting for transfers between devices, flip(): return lax.ppermute(x, 'hidden', [(h, h ^ 1) for h in range(peers)])  9.43 us
    ppermute x6, starting transfers between devices, along(): lax.ppermute(x, 'hidden', [(h, (h + 2 * s) % peers) for h in range(peers)])  8.93 us
    ppermute x6, starting transfers between devices, flip(): return lax.ppermute(x, 'hidden', [(h, h ^ 1) for h in range(peers)])  7.18 us
    ppermute x2, waiting for transfers between devices, swap(): return lax.ppermute(x, 'width', [(0, 1), (1, 0)])  1.55 us
  transfers between devices with their start and end apart: 14, of which 8 were waited for; matrix products, arithmetic and copies ran while one was open for 0% of the time, Pallas kernels for 20%

profile of v3, /device:TPU:0, one launch (start us, length us, event | category | flops | bytes accessed | tf_op | source)
XLA Modules:
  0.0 67.6 jit_solution(7794546428339328734)
XLA Ops:
  0.0 1.0 %copy-done.4 = bf16[10,4096]{1,0:T(8,128)(2,1)S(1)} copy-done((bf16[10,4096]{1,0:T(8,128)(2,1)S(1)}, bf16[10,4096]{1,0:T(8,128)(2,1)}, u32[]{:S(2)}) %copy-start.4) | copy-done | bytes 81944
  1.1 5.1 %collective-permute-start.2 = (bf16[8,5120]{1,0:T(8,128)(2,1)S(1)}, bf16[8,5120]{1,0:T(8,128)(2,1)S(1)}, u32[]{:S(2)}, u32[]{:S(2)}) collective-permute-start(bf16[8,5120]{1,0:T(8,128)(2,1)S(1)} %pack.1.refs_0_), channel_id=1, source_target_pairs={{0,6},{1,7},{2,0},{3,1},{4,2},{5,3},{6,4},{7,5},{8,14},{9,15},{10,... | collective-permute-start | bytes 245768 | tf_op jit(solution)/shard_map/ppermute | solution.py:231
  6.2 1.0 %collective-permute-start = (bf16[8,5120]{1,0:T(8,128)(2,1)S(1)}, bf16[8,5120]{1,0:T(8,128)(2,1)S(1)}, u32[]{:S(2)}, u32[]{:S(2)}) collective-permute-start(bf16[8,5120]{1,0:T(8,128)(2,1)S(1)} %pack.1.refs_0_), channel_id=1, source_target_pairs={{0,2},{1,3},{2,4},{3,5},{4,6},{5,7},{6,0},{7,1},{8,10},{9,11},{10,... | collective-permute-start | bytes 245768 | tf_op jit(solution)/shard_map/ppermute | solution.py:231
  7.2 1.5 %collective-permute-start.3 = (bf16[8,5120]{1,0:T(8,128)(2,1)S(1)}, bf16[8,5120]{1,0:T(8,128)(2,1)S(1)}, u32[]{:S(2)}, u32[]{:S(2)}) collective-permute-start(bf16[8,5120]{1,0:T(8,128)(2,1)S(1)} %pack.1.refs_0_), channel_id=1, source_target_pairs={{0,1},{1,0},{2,3},{3,2},{4,5},{5,4},{6,7},{7,6},{8,9},{9,8},{10,11... | collective-permute-start | bytes 245768 | tf_op jit(solution)/shard_map/ppermute | solution.py:228
  9.0 1.5 %collective-permute-start.6 = (bf16[8,5120]{1,0:T(8,128)(2,1)S(1)}, bf16[8,5120]{1,0:T(8,128)(2,1)S(1)}, u32[]{:S(2)}, u32[]{:S(2)}) collective-permute-start(bf16[8,5120]{1,0:T(8,128)(2,1)S(1)} %collective-permute-done.2.refs_3_), channel_id=1, source_target_pairs={{0,1},{1,0},{2,3},{3,2},{4,5},{5,4},{6,7},{7,6},{8,9},{9,8},{10,11... | collective-permute-start | bytes 245768 | tf_op jit(solution)/shard_map/ppermute | solution.py:228
  10.5 3.2 %collective-permute-done.1.refs_2_ = bf16[8,5120]{1,0:T(8,128)(2,1)S(1)} collective-permute-done((bf16[8,5120]{1,0:T(8,128)(2,1)S(1)}, bf16[8,5120]{1,0:T(8,128)(2,1)S(1)}, u32[]{:S(2)}, u32[]{:S(2)}) %collective-permute-start.1) | collective-permute-done | bytes 81952 | tf_op jit(solution)/shard_map/ppermute | solution.py:231
  13.7 1.5 %collective-permute-start.5 = (bf16[8,5120]{1,0:T(8,128)(2,1)S(1)}, bf16[8,5120]{1,0:T(8,128)(2,1)S(1)}, u32[]{:S(2)}, u32[]{:S(2)}) collective-permute-start(bf16[8,5120]{1,0:T(8,128)(2,1)S(1)} %collective-permute-done.1.refs_2_), channel_id=1, source_target_pairs={{0,1},{1,0},{2,3},{3,2},{4,5},{5,4},{6,7},{7,6},{8,9},{9,8},{10,11... | collective-permute-start | bytes 245768 | tf_op jit(solution)/shard_map/ppermute | solution.py:228
  15.2 0.5 collective-permute-start.4
  15.7 3.2 %collective-permute-done.5.refs_6_ = bf16[8,5120]{1,0:T(8,128)(2,1)S(1)} collective-permute-done((bf16[8,5120]{1,0:T(8,128)(2,1)S(1)}, bf16[8,5120]{1,0:T(8,128)(2,1)S(1)}, u32[]{:S(2)}, u32[]{:S(2)}) %collective-permute-start.5) | collective-permute-done | bytes 81952 | tf_op jit(solution)/shard_map/ppermute | solution.py:228
  19.0 0.9 %collective-permute-done.4.refs_5_ = bf16[8,5120]{1,0:T(8,128)(2,1)S(1)} collective-permute-done((bf16[8,5120]{1,0:T(8,128)(2,1)S(1)}, bf16[8,5120]{1,0:T(8,128)(2,1)S(1)}, u32[]{:S(2)}, u32[]{:S(2)}) %collective-permute-start.4) | collective-permute-done | bytes 81952 | tf_op jit(solution)/shard_map/ppermute | solution.py:228
  19.8 6.6 %gate.1 = (bf16[80,4096]{1,0:T(8,128)(2,1)S(1)}, f32[80,3328]{1,0:T(8,128)S(1)}, bf16[80,3328]{1,0:T(8,128)(2,1)S(1)}, bf16[4096,1664]{1,0:T(8,128)(2,1)S(1)}) custom-call(bf16[8,5120]{1,0:T(8,128)(2,1)S(1)} %pack.1.refs_0_, bf16[8,5120]{1,0:T(8,128)(2,1)S(1)} %collective-permute-done.refs_1_, bf16[8,5120]{1,0:T(8,128)(2,1)S(1)} %collective-permute-done.1.refs_2_, ...), custom_call_target="tpu_custom_call" | custom-call | flops 10000000000 | bytes 56885248 | tf_op jit(solution)/shard_map/gate/pallas_call | solution.py:35
  26.6 7.4 %up.1 = (f32[80,3328]{1,0:T(8,128)S(1)}, bf16[80,3328]{1,0:T(8,128)(2,1)S(1)}, bf16[3328,1024]{1,0:T(8,128)(2,1)S(1)}) custom-call(bf16[80,4096]{1,0:T(8,128)(2,1)S(1)} %get-tuple-element.24.acts, bf16[4096,1664]{1,0:T(8,128)(2,1)S(1)} %get-tuple-element.25.first, bf16[4096,3328]{1,0:T(8,128)(2,1)} %codes.1, f32[128,3328]{1,0:T(8,128)S(1)} %copy-done.3, ...), custom_call_target="tpu_custom_call" | custom-call | flops 10000000000 | bytes 70516736 | tf_op jit(solution)/shard_map/up/pallas_call | solution.py:35
  34.0 0.5 collective-permute-start.8
  34.5 1.5 %collective-permute-done.8.up_other = bf16[80,3328]{1,0:T(8,128)(2,1)S(1)} collective-permute-done((bf16[80,3328]{1,0:T(8,128)(2,1)S(1)}, bf16[80,3328]{1,0:T(8,128)(2,1)S(1)}, u32[]{:S(2)}, u32[]{:S(2)}) %collective-permute-start.8) | collective-permute-done | bytes 532512 | tf_op jit(solution)/shard_map/ppermute | solution.py:234
  36.0 7.7 %first.1 = (f32[32,2560]{1,0:T(8,128)S(1)}, bf16[32,2560]{1,0:T(8,128)(2,1)S(1)}, bf16[80,3328]{1,0:T(8,128)(2,1)S(1)}, bf16[3328,1024]{1,0:T(8,128)(2,1)S(1)}) custom-call(f32[80,3328]{1,0:T(8,128)S(1)} %get-tuple-element.22.gate, bf16[80,3328]{1,0:T(8,128)(2,1)S(1)} %collective-permute-done.7.gate_other, f32[80,3328]{1,0:T(8,128)S(1)} %get-tuple-element.26.up, ...), custom_call_target="tpu_custom_call" | custom-call | flops 1090519040 | bytes 38977536 | tf_op jit(solution)/shard_map/first/pallas_call | solution.py:35
  43.7 1.2 %collective-permute-start.9 = (bf16[32,2560]{1,0:T(8,128)(2,1)S(1)}, bf16[32,2560]{1,0:T(8,128)(2,1)S(1)}, u32[]{:S(2)}, u32[]{:S(2)}) collective-permute-start(bf16[32,2560]{1,0:T(8,128)(2,1)S(1)} %get-tuple-element.30), channel_id=1, source_target_pairs={{0,1},{1,0},{2,3},{3,2},{4,5},{5,4},{6,7},{7,6},{8,9},{9,8},{10,11... | collective-permute-start | bytes 491528 | tf_op jit(solution)/shard_map/ppermute | solution.py:228
  45.0 6.2 %second.1 = (f32[32,2560]{1,0:T(8,128)S(1)}, bf16[32,2560]{1,0:T(8,128)(2,1)S(1)}) custom-call(bf16[80,3328]{1,0:T(8,128)(2,1)S(1)} %get-tuple-element.31.hidden, bf16[3328,1024]{1,0:T(8,128)(2,1)S(1)} %get-tuple-element.32.codes, bf16[3328,4096]{1,0:T(8,128)(2,1)} %later.5, f32[104,4096]{1,0:T(8,128)S(1)} %copy-done.1), custom_call_target="tpu_custom_call" | custom-call | flops 1090519040 | bytes 36315136 | tf_op jit(solution)/shard_map/second/pallas_call | solution.py:35
  51.2 0.9 %collective-permute-start.10 = (bf16[32,2560]{1,0:T(8,128)(2,1)S(1)}, bf16[32,2560]{1,0:T(8,128)(2,1)S(1)}, u32[]{:S(2)}, u32[]{:S(2)}) collective-permute-start(bf16[32,2560]{1,0:T(8,128)(2,1)S(1)} %get-tuple-element.34), channel_id=1, source_target_pairs={{0,1},{1,0},{2,3},{3,2},{4,5},{5,4},{6,7},{7,6},{8,9},{9,8},{10,11... | collective-permute-start | bytes 491528 | tf_op jit(solution)/shard_map/ppermute | solution.py:228
  52.1 5.3 %collective-permute-done.10.refs_3_ = bf16[32,2560]{1,0:T(8,128)(2,1)S(1)} collective-permute-done((bf16[32,2560]{1,0:T(8,128)(2,1)S(1)}, bf16[32,2560]{1,0:T(8,128)(2,1)S(1)}, u32[]{:S(2)}, u32[]{:S(2)}) %collective-permute-start.10) | collective-permute-done | bytes 163872 | tf_op jit(solution)/shard_map/ppermute | solution.py:228
  57.5 1.7 %collective-permute-start.11 = (bf16[8,5120]{1,0:T(8,128)(2,1)S(1)}, bf16[8,5120]{1,0:T(8,128)(2,1)S(1)}, u32[]{:S(2)}, u32[]{:S(2)}) collective-permute-start(bf16[8,5120]{1,0:T(8,128)(2,1)S(1)} %get-tuple-element.36), channel_id=1, source_target_pairs={{0,6},{1,7},{2,0},{3,1},{4,2},{5,3},{6,4},{7,5},{8,14},{9,15},{10,... | collective-permute-start | bytes 245768 | tf_op jit(solution)/shard_map/ppermute | solution.py:231
  59.2 1.1 %collective-permute-start.13 = (bf16[8,5120]{1,0:T(8,128)(2,1)S(1)}, bf16[8,5120]{1,0:T(8,128)(2,1)S(1)}, u32[]{:S(2)}, u32[]{:S(2)}) collective-permute-start(bf16[8,5120]{1,0:T(8,128)(2,1)S(1)} %get-tuple-element.38), channel_id=1, source_target_pairs={{0,2},{1,3},{2,4},{3,5},{4,6},{5,7},{6,0},{7,1},{8,10},{9,11},{10,... | collective-permute-start | bytes 245768 | tf_op jit(solution)/shard_map/ppermute | solution.py:231
  60.3 2.0 %collective-permute-done.11.refs_1_ = bf16[8,5120]{1,0:T(8,128)(2,1)S(1)} collective-permute-done((bf16[8,5120]{1,0:T(8,128)(2,1)S(1)}, bf16[8,5120]{1,0:T(8,128)(2,1)S(1)}, u32[]{:S(2)}, u32[]{:S(2)}) %collective-permute-start.11) | collective-permute-done | bytes 81952 | tf_op jit(solution)/shard_map/ppermute | solution.py:231
  62.3 4.5 %collective-permute-done.12.refs_2_ = bf16[8,5120]{1,0:T(8,128)(2,1)S(1)} collective-permute-done((bf16[8,5120]{1,0:T(8,128)(2,1)S(1)}, bf16[8,5120]{1,0:T(8,128)(2,1)S(1)}, u32[]{:S(2)}, u32[]{:S(2)}) %collective-permute-start.12) | collective-permute-done | bytes 81952 | tf_op jit(solution)/shard_map/ppermute | solution.py:231
  66.9 0.7 %last.1 = bf16[10,4096]{1,0:T(8,128)(2,1)} custom-call(f32[8,5120]{1,0:T(8,128)S(1)} %get-tuple-element.35.refs_0_, bf16[8,5120]{1,0:T(8,128)(2,1)S(1)} %collective-permute-done.11.refs_1_, bf16[8,5120]{1,0:T(8,128)(2,1)S(1)} %collective-permute-done.12.refs_2_, bf16[8,5120]{1,0:T(8,128)(2,1)S(1)} %collective-permute-done.13.refs_3_), custom_call_target="tpu_custom_call" | custom-call | bytes 409600 | tf_op jit(solution)/shard_map/last/pallas_call | solution.py:35
  (21 shorter events, 0.6 us)
Async XLA Ops:
  0.0 19.8 %copy-start.2 = (f32[128,3328]{1,0:T(8,128)S(1)}, f32[128,3328]{1,0:T(8,128)}, u32[]{:S(2)}) copy-start(f32[128,3328]{1,0:T(8,128)} %refs_9_.1) | copy-start | bytes 5111812
  0.0 1.0 %copy-start.4 = (bf16[10,4096]{1,0:T(8,128)(2,1)S(1)}, bf16[10,4096]{1,0:T(8,128)(2,1)}, u32[]{:S(2)}) copy-start(bf16[10,4096]{1,0:T(8,128)(2,1)} %a_ref.1) | copy-start | bytes 245764
  1.0 18.8 %copy-start = (bf16[4096,3328]{1,0:T(8,128)(2,1)S(1)}, bf16[4096,3328]{1,0:T(8,128)(2,1)}, u32[]{:S(2)}) copy-start(bf16[4096,3328]{1,0:T(8,128)(2,1)} %refs_8_.1) | copy-start | bytes 81788928
  1.1 25.5 %copy-start.3 = (f32[128,3328]{1,0:T(8,128)S(1)}, f32[128,3328]{1,0:T(8,128)}, u32[]{:S(2)}) copy-start(f32[128,3328]{1,0:T(8,128)} %scales.3) | copy-start | bytes 5111812
  1.1 8.0 %collective-permute-start.2 = (bf16[8,5120]{1,0:T(8,128)(2,1)S(1)}, bf16[8,5120]{1,0:T(8,128)(2,1)S(1)}, u32[]{:S(2)}, u32[]{:S(2)}) collective-permute-start(bf16[8,5120]{1,0:T(8,128)(2,1)S(1)} %pack.1.refs_0_), channel_id=1, source_target_pairs={{0,6},{1,7},{2,0},{3,1},{4,2},{5,3},{6,4},{7,5},{8,14},{9,15},{10,... | collective-permute-start | bytes 245768 | tf_op jit(solution)/shard_map/ppermute | solution.py:231
  6.2 7.5 %collective-permute-start.1 = (bf16[8,5120]{1,0:T(8,128)(2,1)S(1)}, bf16[8,5120]{1,0:T(8,128)(2,1)S(1)}, u32[]{:S(2)}, u32[]{:S(2)}) collective-permute-start(bf16[8,5120]{1,0:T(8,128)(2,1)S(1)} %pack.1.refs_0_), channel_id=1, source_target_pairs={{0,4},{1,5},{2,6},{3,7},{4,0},{5,1},{6,2},{7,3},{8,12},{9,13},{10,... | collective-permute-start | bytes 245768 | tf_op jit(solution)/shard_map/ppermute | solution.py:231
  6.2 9.0 %collective-permute-start = (bf16[8,5120]{1,0:T(8,128)(2,1)S(1)}, bf16[8,5120]{1,0:T(8,128)(2,1)S(1)}, u32[]{:S(2)}, u32[]{:S(2)}) collective-permute-start(bf16[8,5120]{1,0:T(8,128)(2,1)S(1)} %pack.1.refs_0_), channel_id=1, source_target_pairs={{0,2},{1,3},{2,4},{3,5},{4,6},{5,7},{6,0},{7,1},{8,10},{9,11},{10,... | collective-permute-start | bytes 245768 | tf_op jit(solution)/shard_map/ppermute | solution.py:231
  7.2 8.5 %collective-permute-start.3 = (bf16[8,5120]{1,0:T(8,128)(2,1)S(1)}, bf16[8,5120]{1,0:T(8,128)(2,1)S(1)}, u32[]{:S(2)}, u32[]{:S(2)}) collective-permute-start(bf16[8,5120]{1,0:T(8,128)(2,1)S(1)} %pack.1.refs_0_), channel_id=1, source_target_pairs={{0,1},{1,0},{2,3},{3,2},{4,5},{5,4},{6,7},{7,6},{8,9},{9,8},{10,11... | collective-permute-start | bytes 245768 | tf_op jit(solution)/shard_map/ppermute | solution.py:228
  9.0 6.7 %collective-permute-start.6 = (bf16[8,5120]{1,0:T(8,128)(2,1)S(1)}, bf16[8,5120]{1,0:T(8,128)(2,1)S(1)}, u32[]{:S(2)}, u32[]{:S(2)}) collective-permute-start(bf16[8,5120]{1,0:T(8,128)(2,1)S(1)} %collective-permute-done.2.refs_3_), channel_id=1, source_target_pairs={{0,1},{1,0},{2,3},{3,2},{4,5},{5,4},{6,7},{7,6},{8,9},{9,8},{10,11... | collective-permute-start | bytes 245768 | tf_op jit(solution)/shard_map/ppermute | solution.py:228
  13.7 5.3 %collective-permute-start.5 = (bf16[8,5120]{1,0:T(8,128)(2,1)S(1)}, bf16[8,5120]{1,0:T(8,128)(2,1)S(1)}, u32[]{:S(2)}, u32[]{:S(2)}) collective-permute-start(bf16[8,5120]{1,0:T(8,128)(2,1)S(1)} %collective-permute-done.1.refs_2_), channel_id=1, source_target_pairs={{0,1},{1,0},{2,3},{3,2},{4,5},{5,4},{6,7},{7,6},{8,9},{9,8},{10,11... | collective-permute-start | bytes 245768 | tf_op jit(solution)/shard_map/ppermute | solution.py:228
  15.2 4.7 %collective-permute-start.4 = (bf16[8,5120]{1,0:T(8,128)(2,1)S(1)}, bf16[8,5120]{1,0:T(8,128)(2,1)S(1)}, u32[]{:S(2)}, u32[]{:S(2)}) collective-permute-start(bf16[8,5120]{1,0:T(8,128)(2,1)S(1)} %collective-permute-done.refs_1_), channel_id=1, source_target_pairs={{0,1},{1,0},{2,3},{3,2},{4,5},{5,4},{6,7},{7,6},{8,9},{9,8},{10,11... | collective-permute-start | bytes 245768 | tf_op jit(solution)/shard_map/ppermute | solution.py:228
  26.4 8.0 %collective-permute-start.7 = (bf16[80,3328]{1,0:T(8,128)(2,1)S(1)}, bf16[80,3328]{1,0:T(8,128)(2,1)S(1)}, u32[]{:S(2)}, u32[]{:S(2)}) collective-permute-start(bf16[80,3328]{1,0:T(8,128)(2,1)S(1)} %get-tuple-element.23), channel_id=1, source_target_pairs={{0,8},{8,0},{1,9},{9,1},{2,10},{10,2},{3,11},{11,3},{4,12},{12,4},... | collective-permute-start | bytes 1597448 | tf_op jit(solution)/shard_map/ppermute | solution.py:234
  26.5 9.5 %copy-start.1 = (f32[104,4096]{1,0:T(8,128)S(1)}, f32[104,4096]{1,0:T(8,128)}, u32[]{:S(2)}) copy-start(f32[104,4096]{1,0:T(8,128)} %scales.5) | copy-start | bytes 5111812
  34.0 2.1 %collective-permute-start.8 = (bf16[80,3328]{1,0:T(8,128)(2,1)S(1)}, bf16[80,3328]{1,0:T(8,128)(2,1)S(1)}, u32[]{:S(2)}, u32[]{:S(2)}) collective-permute-start(bf16[80,3328]{1,0:T(8,128)(2,1)S(1)} %get-tuple-element.27), channel_id=1, source_target_pairs={{0,8},{8,0},{1,9},{9,1},{2,10},{10,2},{3,11},{11,3},{4,12},{12,4},... | collective-permute-start | bytes 1597448 | tf_op jit(solution)/shard_map/ppermute | solution.py:234
  43.7 8.4 %collective-permute-start.9 = (bf16[32,2560]{1,0:T(8,128)(2,1)S(1)}, bf16[32,2560]{1,0:T(8,128)(2,1)S(1)}, u32[]{:S(2)}, u32[]{:S(2)}) collective-permute-start(bf16[32,2560]{1,0:T(8,128)(2,1)S(1)} %get-tuple-element.30), channel_id=1, source_target_pairs={{0,1},{1,0},{2,3},{3,2},{4,5},{5,4},{6,7},{7,6},{8,9},{9,8},{10,11... | collective-permute-start | bytes 491528 | tf_op jit(solution)/shard_map/ppermute | solution.py:228
  51.2 6.3 %collective-permute-start.10 = (bf16[32,2560]{1,0:T(8,128)(2,1)S(1)}, bf16[32,2560]{1,0:T(8,128)(2,1)S(1)}, u32[]{:S(2)}, u32[]{:S(2)}) collective-permute-start(bf16[32,2560]{1,0:T(8,128)(2,1)S(1)} %get-tuple-element.34), channel_id=1, source_target_pairs={{0,1},{1,0},{2,3},{3,2},{4,5},{5,4},{6,7},{7,6},{8,9},{9,8},{10,11... | collective-permute-start | bytes 491528 | tf_op jit(solution)/shard_map/ppermute | solution.py:228
  57.5 4.8 %collective-permute-start.11 = (bf16[8,5120]{1,0:T(8,128)(2,1)S(1)}, bf16[8,5120]{1,0:T(8,128)(2,1)S(1)}, u32[]{:S(2)}, u32[]{:S(2)}) collective-permute-start(bf16[8,5120]{1,0:T(8,128)(2,1)S(1)} %get-tuple-element.36), channel_id=1, source_target_pairs={{0,6},{1,7},{2,0},{3,1},{4,2},{5,3},{6,4},{7,5},{8,14},{9,15},{10,... | collective-permute-start | bytes 245768 | tf_op jit(solution)/shard_map/ppermute | solution.py:231
  59.2 7.6 %collective-permute-start.12 = (bf16[8,5120]{1,0:T(8,128)(2,1)S(1)}, bf16[8,5120]{1,0:T(8,128)(2,1)S(1)}, u32[]{:S(2)}, u32[]{:S(2)}) collective-permute-start(bf16[8,5120]{1,0:T(8,128)(2,1)S(1)} %get-tuple-element.37), channel_id=1, source_target_pairs={{0,4},{1,5},{2,6},{3,7},{4,0},{5,1},{6,2},{7,3},{8,12},{9,13},{10,... | collective-permute-start | bytes 245768 | tf_op jit(solution)/shard_map/ppermute | solution.py:231
  59.2 7.6 %collective-permute-start.13 = (bf16[8,5120]{1,0:T(8,128)(2,1)S(1)}, bf16[8,5120]{1,0:T(8,128)(2,1)S(1)}, u32[]{:S(2)}, u32[]{:S(2)}) collective-permute-start(bf16[8,5120]{1,0:T(8,128)(2,1)S(1)} %get-tuple-element.38), channel_id=1, source_target_pairs={{0,2},{1,3},{2,4},{3,5},{4,6},{5,7},{6,0},{7,1},{8,10},{9,11},{10,... | collective-permute-start | bytes 245768 | tf_op jit(solution)/shard_map/ppermute | solution.py:231

commit v4 on v3

--- a/solution.py
+++ b/solution.py
@@ -73,8 +73,8 @@
 def dequant(codes, scales):
     depth, width = codes.shape
     groups = scales.shape[0]
-    shaped = codes.astype(F32).reshape(groups, depth // groups, width)
-    return (shaped * scales[:, None, :]).astype(BF16).reshape(depth, width)
+    spread = jnp.broadcast_to(scales[:, None, :], (groups, depth // groups, width)).astype(BF16)
+    return (codes.reshape(groups, depth // groups, width) * spread).reshape(depth, width)
 
 
 def pieces(width, shares):
@@ -165,28 +165,39 @@
 def first_body(rest, blocks, gate, gate_other, up, up_other, codes, later, scales, *refs):
     *outs, hidden, head, terms, tail, done = refs
     size = codes.shape[1]
-    copies = Copies((later, size, size, tail, 0, done.at[0]), (later, 2 * size, size, head, 0, done.at[1]))
+    part = size // 2
+    copies = Copies(
+        (later, size, part, tail, 0, done.at[0]),
+        (later, size + part, part, tail, part, done.at[1]),
+        (later, 2 * size, size, head, 0, done.at[2]),
+    )
     width = divisor(hidden.shape[1], 512, 128)
     for c in range(0, hidden.shape[1], width):
         cols = slice(c, c + width)
         g = gate[:, cols] + gate_other[:, cols].astype(F32)
         u = up[:, cols] + up_other[:, cols].astype(F32)
         hidden[:, cols] = (jax.nn.silu(g) * u).astype(BF16)
+    copies.start()
     terms[:, :size] = project(hidden, codes, 0, scales, 0, size)
-    copies.wait(0)
     copies.start()
-    terms[:, size:] = project(hidden, tail, 0, scales, size, size)
+    for k in range(2):
+        copies.wait(k)
+        terms[:, size + k * part : size + (k + 1) * part] = project(hidden, tail, k * part, scales, size + k * part, part)
     emit(terms, blocks, rest, outs)
-    copies.wait(1)
+    copies.wait(2)
 
 
 def second_body(rest, blocks, hidden, codes, later, scales, *refs):
     *outs, terms, tail, done = refs
     size = codes.shape[1]
-    copies = Copies((later, 3 * size, size, tail, 0, done))
-    terms[:, :size] = project(hidden, codes, 0, scales, 2 * size, size)
-    copies.wait(0)
-    terms[:, size:] = project(hidden, tail, 0, scales, 3 * size, size)
+    part = size // 2
+    copies = Copies(*[(later, 3 * size + k * part, part, tail, k * part, done.at[k]) for k in range(2)])
+    for k in range(2):
+        terms[:, k * part : (k + 1) * part] = project(hidden, codes, k * part, scales, 2 * size + k * part, part)
+        copies.start()
+    for k in range(2):
+        copies.wait(k)
+        terms[:, size + k * part : size + (k + 1) * part] = project(hidden, tail, k * part, scales, 3 * size + k * part, part)
     emit(terms, blocks, rest, outs)
 
 
@@ -278,7 +289,7 @@
         outs + [sds((rows, units), BF16), pltpu.VMEM((units, quarter), BF16)],
         [gate, gate_other, up, up_other, in_vmem(down_head), down_codes, down_scales],
         "first",
-        scratch=[pltpu.VMEM((rows, half), F32), pltpu.VMEM((units, quarter), BF16), pltpu.SemaphoreType.DMA((2,))],
+        scratch=[pltpu.VMEM((rows, half), F32), pltpu.VMEM((units, quarter), BF16), pltpu.SemaphoreType.DMA((3,))],
         flops=work,
         spare=spare,
         apart=(5,),
@@ -290,7 +301,7 @@
         outs,
         [hidden, in_vmem(down_rest), down_codes, down_scales],
         "second",
-        scratch=[pltpu.VMEM((rows, half), F32), pltpu.VMEM((units, quarter), BF16), pltpu.SemaphoreType.DMA],
+        scratch=[pltpu.VMEM((rows, half), F32), pltpu.VMEM((units, quarter), BF16), pltpu.SemaphoreType.DMA((2,))],
         flops=work,
         spare=spare,
         apart=(2,),

time: 67.8 us -> 63 us (0.929)
  Pallas kernels: 28.7 us -> 24 us
    pallas_call x7, Pallas kernels: 28.7 us -> 24 us  [call(): pl.pallas_call(body, in_specs=[pl.BlockSpec(memory_space=pltpu.HBM if i i...]
  transfers between devices with their start and end apart: 14 -> 14, of which waited for: 8 -> 8; matrix products, arithmetic and copies ran while one was open for 0% -> 0% of each run, Pallas kernels for 20% -> 19%
where the time goes in v4:
time: 63 us; the launch traced here: 62.8 us
  Pallas kernels  24 us (38%)
  waiting for transfers between devices  21 us (33%)
  starting transfers between devices  16.7 us (27%)
  local copies, waits for them, and re-layouts  1.05 us (2%)
    pallas_call x7, Pallas kernels, call(): pl.pallas_call(body, in_specs=[pl.BlockSpec(memory_space=pltpu.HBM if i i...  24 us
    ppermute x6, waiting for transfers between devices, along(): lax.ppermute(x, 'hidden', [(h, (h + 2 * s) % peers) for h in range(peers)])  10 us
    ppermute x6, waiting for transfers between devices, flip(): return lax.ppermute(x, 'hidden', [(h, h ^ 1) for h in range(peers)])  9.43 us
    ppermute x6, starting transfers between devices, along(): lax.ppermute(x, 'hidden', [(h, (h + 2 * s) % peers) for h in range(peers)])  8.92 us
    ppermute x6, starting transfers between devices, flip(): return lax.ppermute(x, 'hidden', [(h, h ^ 1) for h in range(peers)])  7.18 us
    ppermute x2, waiting for transfers between devices, swap(): return lax.ppermute(x, 'width', [(0, 1), (1, 0)])  1.55 us
  transfers between devices with their start and end apart: 14, of which 8 were waited for; matrix products, arithmetic and copies ran while one was open for 0% of the time, Pallas kernels for 19%

profile of v4, /device:TPU:0, one launch (start us, length us, event | category | flops | bytes accessed | tf_op | source)
XLA Modules:
  0.0 62.8 jit_solution(7048936408233108983)
XLA Ops:
  0.0 1.0 %copy-done.4 = bf16[10,4096]{1,0:T(8,128)(2,1)S(1)} copy-done((bf16[10,4096]{1,0:T(8,128)(2,1)S(1)}, bf16[10,4096]{1,0:T(8,128)(2,1)}, u32[]{:S(2)}) %copy-start.4) | copy-done | bytes 81944
  1.1 5.1 %collective-permute-start.2 = (bf16[8,5120]{1,0:T(8,128)(2,1)S(1)}, bf16[8,5120]{1,0:T(8,128)(2,1)S(1)}, u32[]{:S(2)}, u32[]{:S(2)}) collective-permute-start(bf16[8,5120]{1,0:T(8,128)(2,1)S(1)} %pack.1.refs_0_), channel_id=1, source_target_pairs={{0,6},{1,7},{2,0},{3,1},{4,2},{5,3},{6,4},{7,5},{8,14},{9,15},{10,... | collective-permute-start | bytes 245768 | tf_op jit(solution)/shard_map/ppermute | solution.py:242
  6.2 1.0 %collective-permute-start = (bf16[8,5120]{1,0:T(8,128)(2,1)S(1)}, bf16[8,5120]{1,0:T(8,128)(2,1)S(1)}, u32[]{:S(2)}, u32[]{:S(2)}) collective-permute-start(bf16[8,5120]{1,0:T(8,128)(2,1)S(1)} %pack.1.refs_0_), channel_id=1, source_target_pairs={{0,2},{1,3},{2,4},{3,5},{4,6},{5,7},{6,0},{7,1},{8,10},{9,11},{10,... | collective-permute-start | bytes 245768 | tf_op jit(solution)/shard_map/ppermute | solution.py:242
  7.2 1.5 %collective-permute-start.3 = (bf16[8,5120]{1,0:T(8,128)(2,1)S(1)}, bf16[8,5120]{1,0:T(8,128)(2,1)S(1)}, u32[]{:S(2)}, u32[]{:S(2)}) collective-permute-start(bf16[8,5120]{1,0:T(8,128)(2,1)S(1)} %pack.1.refs_0_), channel_id=1, source_target_pairs={{0,1},{1,0},{2,3},{3,2},{4,5},{5,4},{6,7},{7,6},{8,9},{9,8},{10,11... | collective-permute-start | bytes 245768 | tf_op jit(solution)/shard_map/ppermute | solution.py:239
  9.0 1.5 %collective-permute-start.6 = (bf16[8,5120]{1,0:T(8,128)(2,1)S(1)}, bf16[8,5120]{1,0:T(8,128)(2,1)S(1)}, u32[]{:S(2)}, u32[]{:S(2)}) collective-permute-start(bf16[8,5120]{1,0:T(8,128)(2,1)S(1)} %collective-permute-done.2.refs_3_), channel_id=1, source_target_pairs={{0,1},{1,0},{2,3},{3,2},{4,5},{5,4},{6,7},{7,6},{8,9},{9,8},{10,11... | collective-permute-start | bytes 245768 | tf_op jit(solution)/shard_map/ppermute | solution.py:239
  10.5 3.2 %collective-permute-done.1.refs_2_ = bf16[8,5120]{1,0:T(8,128)(2,1)S(1)} collective-permute-done((bf16[8,5120]{1,0:T(8,128)(2,1)S(1)}, bf16[8,5120]{1,0:T(8,128)(2,1)S(1)}, u32[]{:S(2)}, u32[]{:S(2)}) %collective-permute-start.1) | collective-permute-done | bytes 81952 | tf_op jit(solution)/shard_map/ppermute | solution.py:242
  13.7 1.5 %collective-permute-start.5 = (bf16[8,5120]{1,0:T(8,128)(2,1)S(1)}, bf16[8,5120]{1,0:T(8,128)(2,1)S(1)}, u32[]{:S(2)}, u32[]{:S(2)}) collective-permute-start(bf16[8,5120]{1,0:T(8,128)(2,1)S(1)} %collective-permute-done.1.refs_2_), channel_id=1, source_target_pairs={{0,1},{1,0},{2,3},{3,2},{4,5},{5,4},{6,7},{7,6},{8,9},{9,8},{10,11... | collective-permute-start | bytes 245768 | tf_op jit(solution)/shard_map/ppermute | solution.py:239
  15.2 0.5 collective-permute-start.4
  15.7 3.2 %collective-permute-done.5.refs_6_ = bf16[8,5120]{1,0:T(8,128)(2,1)S(1)} collective-permute-done((bf16[8,5120]{1,0:T(8,128)(2,1)S(1)}, bf16[8,5120]{1,0:T(8,128)(2,1)S(1)}, u32[]{:S(2)}, u32[]{:S(2)}) %collective-permute-start.5) | collective-permute-done | bytes 81952 | tf_op jit(solution)/shard_map/ppermute | solution.py:239
  19.0 0.9 %collective-permute-done.4.refs_5_ = bf16[8,5120]{1,0:T(8,128)(2,1)S(1)} collective-permute-done((bf16[8,5120]{1,0:T(8,128)(2,1)S(1)}, bf16[8,5120]{1,0:T(8,128)(2,1)S(1)}, u32[]{:S(2)}, u32[]{:S(2)}) %collective-permute-start.4) | collective-permute-done | bytes 81952 | tf_op jit(solution)/shard_map/ppermute | solution.py:239
  19.8 5.0 %gate.1 = (bf16[80,4096]{1,0:T(8,128)(2,1)S(1)}, f32[80,3328]{1,0:T(8,128)S(1)}, bf16[80,3328]{1,0:T(8,128)(2,1)S(1)}, bf16[4096,1664]{1,0:T(8,128)(2,1)S(1)}) custom-call(bf16[8,5120]{1,0:T(8,128)(2,1)S(1)} %pack.1.refs_0_, bf16[8,5120]{1,0:T(8,128)(2,1)S(1)} %collective-permute-done.refs_1_, bf16[8,5120]{1,0:T(8,128)(2,1)S(1)} %collective-permute-done.1.refs_2_, ...), custom_call_target="tpu_custom_call" | custom-call | flops 10000000000 | bytes 56885248 | tf_op jit(solution)/shard_map/gate/pallas_call | solution.py:35
  25.0 7.0 %up.1 = (f32[80,3328]{1,0:T(8,128)S(1)}, bf16[80,3328]{1,0:T(8,128)(2,1)S(1)}, bf16[3328,1024]{1,0:T(8,128)(2,1)S(1)}) custom-call(bf16[80,4096]{1,0:T(8,128)(2,1)S(1)} %get-tuple-element.24.acts, bf16[4096,1664]{1,0:T(8,128)(2,1)S(1)} %get-tuple-element.25.first, bf16[4096,3328]{1,0:T(8,128)(2,1)} %codes.1, f32[128,3328]{1,0:T(8,128)S(1)} %copy-done.3, ...), custom_call_target="tpu_custom_call" | custom-call | flops 10000000000 | bytes 70516736 | tf_op jit(solution)/shard_map/up/pallas_call | solution.py:35
  32.0 0.5 collective-permute-start.8
  32.6 1.5 %collective-permute-done.8.up_other = bf16[80,3328]{1,0:T(8,128)(2,1)S(1)} collective-permute-done((bf16[80,3328]{1,0:T(8,128)(2,1)S(1)}, bf16[80,3328]{1,0:T(8,128)(2,1)S(1)}, u32[]{:S(2)}, u32[]{:S(2)}) %collective-permute-start.8) | collective-permute-done | bytes 532512 | tf_op jit(solution)/shard_map/ppermute | solution.py:245
  34.1 6.1 %first.1 = (f32[32,2560]{1,0:T(8,128)S(1)}, bf16[32,2560]{1,0:T(8,128)(2,1)S(1)}, bf16[80,3328]{1,0:T(8,128)(2,1)S(1)}, bf16[3328,1024]{1,0:T(8,128)(2,1)S(1)}) custom-call(f32[80,3328]{1,0:T(8,128)S(1)} %get-tuple-element.22.gate, bf16[80,3328]{1,0:T(8,128)(2,1)S(1)} %collective-permute-done.7.gate_other, f32[80,3328]{1,0:T(8,128)S(1)} %get-tuple-element.26.up, ...), custom_call_target="tpu_custom_call" | custom-call | flops 1090519040 | bytes 38977536 | tf_op jit(solution)/shard_map/first/pallas_call | solution.py:35
  40.3 1.2 %collective-permute-start.9 = (bf16[32,2560]{1,0:T(8,128)(2,1)S(1)}, bf16[32,2560]{1,0:T(8,128)(2,1)S(1)}, u32[]{:S(2)}, u32[]{:S(2)}) collective-permute-start(bf16[32,2560]{1,0:T(8,128)(2,1)S(1)} %get-tuple-element.30), channel_id=1, source_target_pairs={{0,1},{1,0},{2,3},{3,2},{4,5},{5,4},{6,7},{7,6},{8,9},{9,8},{10,11... | collective-permute-start | bytes 491528 | tf_op jit(solution)/shard_map/ppermute | solution.py:239
  41.5 5.0 %second.1 = (f32[32,2560]{1,0:T(8,128)S(1)}, bf16[32,2560]{1,0:T(8,128)(2,1)S(1)}) custom-call(bf16[80,3328]{1,0:T(8,128)(2,1)S(1)} %get-tuple-element.31.hidden, bf16[3328,1024]{1,0:T(8,128)(2,1)S(1)} %get-tuple-element.32.codes, bf16[3328,4096]{1,0:T(8,128)(2,1)} %later.5, f32[104,4096]{1,0:T(8,128)S(1)} %copy-done.1), custom_call_target="tpu_custom_call" | custom-call | flops 1090519040 | bytes 36315136 | tf_op jit(solution)/shard_map/second/pallas_call | solution.py:35
  46.5 0.9 %collective-permute-start.10 = (bf16[32,2560]{1,0:T(8,128)(2,1)S(1)}, bf16[32,2560]{1,0:T(8,128)(2,1)S(1)}, u32[]{:S(2)}, u32[]{:S(2)}) collective-permute-start(bf16[32,2560]{1,0:T(8,128)(2,1)S(1)} %get-tuple-element.34), channel_id=1, source_target_pairs={{0,1},{1,0},{2,3},{3,2},{4,5},{5,4},{6,7},{7,6},{8,9},{9,8},{10,11... | collective-permute-start | bytes 491528 | tf_op jit(solution)/shard_map/ppermute | solution.py:239
  47.4 5.3 %collective-permute-done.10.refs_3_ = bf16[32,2560]{1,0:T(8,128)(2,1)S(1)} collective-permute-done((bf16[32,2560]{1,0:T(8,128)(2,1)S(1)}, bf16[32,2560]{1,0:T(8,128)(2,1)S(1)}, u32[]{:S(2)}, u32[]{:S(2)}) %collective-permute-start.10) | collective-permute-done | bytes 163872 | tf_op jit(solution)/shard_map/ppermute | solution.py:239
  52.8 1.7 %collective-permute-start.11 = (bf16[8,5120]{1,0:T(8,128)(2,1)S(1)}, bf16[8,5120]{1,0:T(8,128)(2,1)S(1)}, u32[]{:S(2)}, u32[]{:S(2)}) collective-permute-start(bf16[8,5120]{1,0:T(8,128)(2,1)S(1)} %get-tuple-element.36), channel_id=1, source_target_pairs={{0,6},{1,7},{2,0},{3,1},{4,2},{5,3},{6,4},{7,5},{8,14},{9,15},{10,... | collective-permute-start | bytes 245768 | tf_op jit(solution)/shard_map/ppermute | solution.py:242
  54.5 1.1 %collective-permute-start.13 = (bf16[8,5120]{1,0:T(8,128)(2,1)S(1)}, bf16[8,5120]{1,0:T(8,128)(2,1)S(1)}, u32[]{:S(2)}, u32[]{:S(2)}) collective-permute-start(bf16[8,5120]{1,0:T(8,128)(2,1)S(1)} %get-tuple-element.38), channel_id=1, source_target_pairs={{0,2},{1,3},{2,4},{3,5},{4,6},{5,7},{6,0},{7,1},{8,10},{9,11},{10,... | collective-permute-start | bytes 245768 | tf_op jit(solution)/shard_map/ppermute | solution.py:242
  55.6 2.0 %collective-permute-done.11.refs_1_ = bf16[8,5120]{1,0:T(8,128)(2,1)S(1)} collective-permute-done((bf16[8,5120]{1,0:T(8,128)(2,1)S(1)}, bf16[8,5120]{1,0:T(8,128)(2,1)S(1)}, u32[]{:S(2)}, u32[]{:S(2)}) %collective-permute-start.11) | collective-permute-done | bytes 81952 | tf_op jit(solution)/shard_map/ppermute | solution.py:242
  57.7 4.5 %collective-permute-done.12.refs_2_ = bf16[8,5120]{1,0:T(8,128)(2,1)S(1)} collective-permute-done((bf16[8,5120]{1,0:T(8,128)(2,1)S(1)}, bf16[8,5120]{1,0:T(8,128)(2,1)S(1)}, u32[]{:S(2)}, u32[]{:S(2)}) %collective-permute-start.12) | collective-permute-done | bytes 81952 | tf_op jit(solution)/shard_map/ppermute | solution.py:242
  62.1 0.7 %last.1 = bf16[10,4096]{1,0:T(8,128)(2,1)} custom-call(f32[8,5120]{1,0:T(8,128)S(1)} %get-tuple-element.35.refs_0_, bf16[8,5120]{1,0:T(8,128)(2,1)S(1)} %collective-permute-done.11.refs_1_, bf16[8,5120]{1,0:T(8,128)(2,1)S(1)} %collective-permute-done.12.refs_2_, bf16[8,5120]{1,0:T(8,128)(2,1)S(1)} %collective-permute-done.13.refs_3_), custom_call_target="tpu_custom_call" | custom-call | bytes 409600 | tf_op jit(solution)/shard_map/last/pallas_call | solution.py:35
  (21 shorter events, 0.6 us)
Async XLA Ops:
  0.0 19.8 %copy-start.2 = (f32[128,3328]{1,0:T(8,128)S(1)}, f32[128,3328]{1,0:T(8,128)}, u32[]{:S(2)}) copy-start(f32[128,3328]{1,0:T(8,128)} %refs_9_.1) | copy-start | bytes 5111812
  0.0 1.0 %copy-start.4 = (bf16[10,4096]{1,0:T(8,128)(2,1)S(1)}, bf16[10,4096]{1,0:T(8,128)(2,1)}, u32[]{:S(2)}) copy-start(bf16[10,4096]{1,0:T(8,128)(2,1)} %a_ref.1) | copy-start | bytes 245764
  1.0 18.8 %copy-start = (bf16[4096,3328]{1,0:T(8,128)(2,1)S(1)}, bf16[4096,3328]{1,0:T(8,128)(2,1)}, u32[]{:S(2)}) copy-start(bf16[4096,3328]{1,0:T(8,128)(2,1)} %refs_8_.1) | copy-start | bytes 81788928
  1.1 23.9 %copy-start.3 = (f32[128,3328]{1,0:T(8,128)S(1)}, f32[128,3328]{1,0:T(8,128)}, u32[]{:S(2)}) copy-start(f32[128,3328]{1,0:T(8,128)} %scales.3) | copy-start | bytes 5111812
  1.1 8.0 %collective-permute-start.2 = (bf16[8,5120]{1,0:T(8,128)(2,1)S(1)}, bf16[8,5120]{1,0:T(8,128)(2,1)S(1)}, u32[]{:S(2)}, u32[]{:S(2)}) collective-permute-start(bf16[8,5120]{1,0:T(8,128)(2,1)S(1)} %pack.1.refs_0_), channel_id=1, source_target_pairs={{0,6},{1,7},{2,0},{3,1},{4,2},{5,3},{6,4},{7,5},{8,14},{9,15},{10,... | collective-permute-start | bytes 245768 | tf_op jit(solution)/shard_map/ppermute | solution.py:242
  6.2 7.5 %collective-permute-start.1 = (bf16[8,5120]{1,0:T(8,128)(2,1)S(1)}, bf16[8,5120]{1,0:T(8,128)(2,1)S(1)}, u32[]{:S(2)}, u32[]{:S(2)}) collective-permute-start(bf16[8,5120]{1,0:T(8,128)(2,1)S(1)} %pack.1.refs_0_), channel_id=1, source_target_pairs={{0,4},{1,5},{2,6},{3,7},{4,0},{5,1},{6,2},{7,3},{8,12},{9,13},{10,... | collective-permute-start | bytes 245768 | tf_op jit(solution)/shard_map/ppermute | solution.py:242
  6.2 9.0 %collective-permute-start = (bf16[8,5120]{1,0:T(8,128)(2,1)S(1)}, bf16[8,5120]{1,0:T(8,128)(2,1)S(1)}, u32[]{:S(2)}, u32[]{:S(2)}) collective-permute-start(bf16[8,5120]{1,0:T(8,128)(2,1)S(1)} %pack.1.refs_0_), channel_id=1, source_target_pairs={{0,2},{1,3},{2,4},{3,5},{4,6},{5,7},{6,0},{7,1},{8,10},{9,11},{10,... | collective-permute-start | bytes 245768 | tf_op jit(solution)/shard_map/ppermute | solution.py:242
  7.2 8.5 %collective-permute-start.3 = (bf16[8,5120]{1,0:T(8,128)(2,1)S(1)}, bf16[8,5120]{1,0:T(8,128)(2,1)S(1)}, u32[]{:S(2)}, u32[]{:S(2)}) collective-permute-start(bf16[8,5120]{1,0:T(8,128)(2,1)S(1)} %pack.1.refs_0_), channel_id=1, source_target_pairs={{0,1},{1,0},{2,3},{3,2},{4,5},{5,4},{6,7},{7,6},{8,9},{9,8},{10,11... | collective-permute-start | bytes 245768 | tf_op jit(solution)/shard_map/ppermute | solution.py:239
  9.0 6.7 %collective-permute-start.6 = (bf16[8,5120]{1,0:T(8,128)(2,1)S(1)}, bf16[8,5120]{1,0:T(8,128)(2,1)S(1)}, u32[]{:S(2)}, u32[]{:S(2)}) collective-permute-start(bf16[8,5120]{1,0:T(8,128)(2,1)S(1)} %collective-permute-done.2.refs_3_), channel_id=1, source_target_pairs={{0,1},{1,0},{2,3},{3,2},{4,5},{5,4},{6,7},{7,6},{8,9},{9,8},{10,11... | collective-permute-start | bytes 245768 | tf_op jit(solution)/shard_map/ppermute | solution.py:239
  13.7 5.3 %collective-permute-start.5 = (bf16[8,5120]{1,0:T(8,128)(2,1)S(1)}, bf16[8,5120]{1,0:T(8,128)(2,1)S(1)}, u32[]{:S(2)}, u32[]{:S(2)}) collective-permute-start(bf16[8,5120]{1,0:T(8,128)(2,1)S(1)} %collective-permute-done.1.refs_2_), channel_id=1, source_target_pairs={{0,1},{1,0},{2,3},{3,2},{4,5},{5,4},{6,7},{7,6},{8,9},{9,8},{10,11... | collective-permute-start | bytes 245768 | tf_op jit(solution)/shard_map/ppermute | solution.py:239
  15.2 4.7 %collective-permute-start.4 = (bf16[8,5120]{1,0:T(8,128)(2,1)S(1)}, bf16[8,5120]{1,0:T(8,128)(2,1)S(1)}, u32[]{:S(2)}, u32[]{:S(2)}) collective-permute-start(bf16[8,5120]{1,0:T(8,128)(2,1)S(1)} %collective-permute-done.refs_1_), channel_id=1, source_target_pairs={{0,1},{1,0},{2,3},{3,2},{4,5},{5,4},{6,7},{7,6},{8,9},{9,8},{10,11... | collective-permute-start | bytes 245768 | tf_op jit(solution)/shard_map/ppermute | solution.py:239
  24.9 7.7 %collective-permute-start.7 = (bf16[80,3328]{1,0:T(8,128)(2,1)S(1)}, bf16[80,3328]{1,0:T(8,128)(2,1)S(1)}, u32[]{:S(2)}, u32[]{:S(2)}) collective-permute-start(bf16[80,3328]{1,0:T(8,128)(2,1)S(1)} %get-tuple-element.23), channel_id=1, source_target_pairs={{0,8},{8,0},{1,9},{9,1},{2,10},{10,2},{3,11},{11,3},{4,12},{12,4},... | collective-permute-start | bytes 1597448 | tf_op jit(solution)/shard_map/ppermute | solution.py:245
  25.0 9.1 %copy-start.1 = (f32[104,4096]{1,0:T(8,128)S(1)}, f32[104,4096]{1,0:T(8,128)}, u32[]{:S(2)}) copy-start(f32[104,4096]{1,0:T(8,128)} %scales.5) | copy-start | bytes 5111812
  32.0 2.1 %collective-permute-start.8 = (bf16[80,3328]{1,0:T(8,128)(2,1)S(1)}, bf16[80,3328]{1,0:T(8,128)(2,1)S(1)}, u32[]{:S(2)}, u32[]{:S(2)}) collective-permute-start(bf16[80,3328]{1,0:T(8,128)(2,1)S(1)} %get-tuple-element.27), channel_id=1, source_target_pairs={{0,8},{8,0},{1,9},{9,1},{2,10},{10,2},{3,11},{11,3},{4,12},{12,4},... | collective-permute-start | bytes 1597448 | tf_op jit(solution)/shard_map/ppermute | solution.py:245
  40.3 7.2 %collective-permute-start.9 = (bf16[32,2560]{1,0:T(8,128)(2,1)S(1)}, bf16[32,2560]{1,0:T(8,128)(2,1)S(1)}, u32[]{:S(2)}, u32[]{:S(2)}) collective-permute-start(bf16[32,2560]{1,0:T(8,128)(2,1)S(1)} %get-tuple-element.30), channel_id=1, source_target_pairs={{0,1},{1,0},{2,3},{3,2},{4,5},{5,4},{6,7},{7,6},{8,9},{9,8},{10,11... | collective-permute-start | bytes 491528 | tf_op jit(solution)/shard_map/ppermute | solution.py:239
  46.5 6.2 %collective-permute-start.10 = (bf16[32,2560]{1,0:T(8,128)(2,1)S(1)}, bf16[32,2560]{1,0:T(8,128)(2,1)S(1)}, u32[]{:S(2)}, u32[]{:S(2)}) collective-permute-start(bf16[32,2560]{1,0:T(8,128)(2,1)S(1)} %get-tuple-element.34), channel_id=1, source_target_pairs={{0,1},{1,0},{2,3},{3,2},{4,5},{5,4},{6,7},{7,6},{8,9},{9,8},{10,11... | collective-permute-start | bytes 491528 | tf_op jit(solution)/shard_map/ppermute | solution.py:239
  52.8 4.9 %collective-permute-start.11 = (bf16[8,5120]{1,0:T(8,128)(2,1)S(1)}, bf16[8,5120]{1,0:T(8,128)(2,1)S(1)}, u32[]{:S(2)}, u32[]{:S(2)}) collective-permute-start(bf16[8,5120]{1,0:T(8,128)(2,1)S(1)} %get-tuple-element.36), channel_id=1, source_target_pairs={{0,6},{1,7},{2,0},{3,1},{4,2},{5,3},{6,4},{7,5},{8,14},{9,15},{10,... | collective-permute-start | bytes 245768 | tf_op jit(solution)/shard_map/ppermute | solution.py:242
  54.5 7.6 %collective-permute-start.12 = (bf16[8,5120]{1,0:T(8,128)(2,1)S(1)}, bf16[8,5120]{1,0:T(8,128)(2,1)S(1)}, u32[]{:S(2)}, u32[]{:S(2)}) collective-permute-start(bf16[8,5120]{1,0:T(8,128)(2,1)S(1)} %get-tuple-element.37), channel_id=1, source_target_pairs={{0,4},{1,5},{2,6},{3,7},{4,0},{5,1},{6,2},{7,3},{8,12},{9,13},{10,... | collective-permute-start | bytes 245768 | tf_op jit(solution)/shard_map/ppermute | solution.py:242
  54.5 7.6 %collective-permute-start.13 = (bf16[8,5120]{1,0:T(8,128)(2,1)S(1)}, bf16[8,5120]{1,0:T(8,128)(2,1)S(1)}, u32[]{:S(2)}, u32[]{:S(2)}) collective-permute-start(bf16[8,5120]{1,0:T(8,128)(2,1)S(1)} %get-tuple-element.38), channel_id=1, source_target_pairs={{0,2},{1,3},{2,4},{3,5},{4,6},{5,7},{6,0},{7,1},{8,10},{9,11},{10,... | collective-permute-start | bytes 245768 | tf_op jit(solution)/shard_map/ppermute | solution.py:242

commit v5 on v4

--- a/solution.py
+++ b/solution.py
@@ -70,11 +70,18 @@
     return total[first * TILE : (first + 1) * TILE, :], jnp.concatenate(left, axis=0)
 
 
-def dequant(codes, scales):
+def dequant_short(codes, scales):
     depth, width = codes.shape
     groups = scales.shape[0]
     spread = jnp.broadcast_to(scales[:, None, :], (groups, depth // groups, width)).astype(BF16)
     return (codes.reshape(groups, depth // groups, width) * spread).reshape(depth, width)
+
+
+def dequant(codes, scales):
+    depth, width = codes.shape
+    groups = scales.shape[0]
+    shaped = codes.astype(F32).reshape(groups, depth // groups, width)
+    return (shaped * scales[:, None, :]).astype(BF16).reshape(depth, width)
 
 
 def pieces(width, shares):
@@ -85,13 +92,13 @@
     return [(128 * a, 128 * (b - a)) for a, b in zip(ends, ends[1:])]
 
 
-def project(a_ref, codes_ref, at, scales_ref, start, size):
+def project(a_ref, codes_ref, at, scales_ref, start, size, product=dequant):
     depth = codes_ref.shape[0]
     block = depth // scales_ref.shape[0]
     rows = divisor(depth, 512, 8 * block)
     total = jnp.zeros((a_ref.shape[0], size), F32)
     for k in range(0, depth, rows):
-        w = dequant(codes_ref[k : k + rows, at : at + size], scales_ref[k // block : (k + rows) // block, start : start + size])
+        w = product(codes_ref[k : k + rows, at : at + size], scales_ref[k // block : (k + rows) // block, start : start + size])
         total += jnp.dot(a_ref[:, k : k + rows], w, preferred_element_type=F32)
     return total
 
@@ -129,7 +136,7 @@
             at += 1
     acts[...] = wide[...].astype(BF16)
     for start, size in pieces(codes.shape[1], (1, 1)):
-        total = project(acts, codes, start, scales, start, size)
+        total = project(acts, codes, start, scales, start, size, dequant_short)
         own[:, start : start + size] = total
         sent[:, start : start + size] = total.astype(BF16)
     copy.wait(0)
@@ -250,7 +257,8 @@
     packed = call(pack_body, sds((TILE, dense), BF16), [acts], "pack", flops=PACK_WEIGHT)
     if pair:
         line = [packed] + [along(packed, s) for s in range(1, far)]
-        blocks = line + [flip(x) for x in line]
+        across = flip(packed)
+        blocks = line + [across] + [along(across, s) if s == 2 else flip(line[s]) for s in range(1, far)]
     else:
         blocks = [lax.all_gather(packed, "hidden", axis=0, tiled=True)]
     spare = 2 * MIB + 4096 * rows

time: 63 us -> 63.6 us (level)
  Pallas kernels: 24 us -> 25.6 us
    ppermute x6 -> x5, waiting for transfers between devices: 9.43 us -> 4.72 us  [flip(): return lax.ppermute(x, 'hidden', [(h, h ^ 1) for h in range(peers)])]
    ppermute x6 -> x7, waiting for transfers between devices: 10 us -> 14.3 us  [along(): lax.ppermute(x, 'hidden', [(h, (h + 2 * s) % peers) for h in range(peers)])]
    pallas_call x7, Pallas kernels: 24 us -> 25.6 us  [call(): pl.pallas_call(body, in_specs=[pl.BlockSpec(memory_space=pltpu.HBM if i i...]
    ppermute x6 -> x5, starting transfers between devices: 7.18 us -> 6.24 us  [flip(): return lax.ppermute(x, 'hidden', [(h, h ^ 1) for h in range(peers)])]
    ppermute x6 -> x7, starting transfers between devices: 8.92 us -> 9.28 us  [along(): lax.ppermute(x, 'hidden', [(h, (h + 2 * s) % peers) for h in range(peers)])]
  transfers between devices with their start and end apart: 14 -> 14, of which waited for: 8 -> 7; matrix products, arithmetic and copies ran while one was open for 0% -> 0% of each run, Pallas kernels for 19% -> 20%
where the time goes in v5:
time: 63.6 us; the launch traced here: 63.4 us
  Pallas kernels  25.6 us (40%)
  waiting for transfers between devices  20.6 us (32%)
  starting transfers between devices  16.1 us (25%)
  local copies, waits for them, and re-layouts  1.05 us (2%)
    pallas_call x7, Pallas kernels, call(): pl.pallas_call(body, in_specs=[pl.BlockSpec(memory_space=pltpu.HBM if i i...  25.6 us
    ppermute x7, waiting for transfers between devices, along(): lax.ppermute(x, 'hidden', [(h, (h + 2 * s) % peers) for h in range(peers)])  14.3 us
    ppermute x7, starting transfers between devices, along(): lax.ppermute(x, 'hidden', [(h, (h + 2 * s) % peers) for h in range(peers)])  9.28 us
    ppermute x5, starting transfers between devices, flip(): return lax.ppermute(x, 'hidden', [(h, h ^ 1) for h in range(peers)])  6.24 us
    ppermute x5, waiting for transfers between devices, flip(): return lax.ppermute(x, 'hidden', [(h, h ^ 1) for h in range(peers)])  4.72 us
    ppermute x2, waiting for transfers between devices, swap(): return lax.ppermute(x, 'width', [(0, 1), (1, 0)])  1.55 us
  transfers between devices with their start and end apart: 14, of which 7 were waited for; matrix products, arithmetic and copies ran while one was open for 0% of the time, Pallas kernels for 20%

profile of v5, /device:TPU:0, one launch (start us, length us, event | category | flops | bytes accessed | tf_op | source)
XLA Modules:
  0.0 63.4 jit_solution(15207894370846806295)
XLA Ops:
  0.0 1.0 %copy-done.4 = bf16[10,4096]{1,0:T(8,128)(2,1)S(1)} copy-done((bf16[10,4096]{1,0:T(8,128)(2,1)S(1)}, bf16[10,4096]{1,0:T(8,128)(2,1)}, u32[]{:S(2)}) %copy-start.4) | copy-done | bytes 81944
  1.1 3.0 %collective-permute-start.3 = (bf16[8,5120]{1,0:T(8,128)(2,1)S(1)}, bf16[8,5120]{1,0:T(8,128)(2,1)S(1)}, u32[]{:S(2)}, u32[]{:S(2)}) collective-permute-start(bf16[8,5120]{1,0:T(8,128)(2,1)S(1)} %pack.1.refs_0_), channel_id=1, source_target_pairs={{0,1},{1,0},{2,3},{3,2},{4,5},{5,4},{6,7},{7,6},{8,9},{9,8},{10,11... | collective-permute-start | bytes 245768 | tf_op jit(solution)/shard_map/ppermute | solution.py:246
  4.1 3.6 %collective-permute-start.2 = (bf16[8,5120]{1,0:T(8,128)(2,1)S(1)}, bf16[8,5120]{1,0:T(8,128)(2,1)S(1)}, u32[]{:S(2)}, u32[]{:S(2)}) collective-permute-start(bf16[8,5120]{1,0:T(8,128)(2,1)S(1)} %pack.1.refs_0_), channel_id=1, source_target_pairs={{0,6},{1,7},{2,0},{3,1},{4,2},{5,3},{6,4},{7,5},{8,14},{9,15},{10,... | collective-permute-start | bytes 245768 | tf_op jit(solution)/shard_map/ppermute | solution.py:249
  7.7 1.0 %collective-permute-start.1 = (bf16[8,5120]{1,0:T(8,128)(2,1)S(1)}, bf16[8,5120]{1,0:T(8,128)(2,1)S(1)}, u32[]{:S(2)}, u32[]{:S(2)}) collective-permute-start(bf16[8,5120]{1,0:T(8,128)(2,1)S(1)} %pack.1.refs_0_), channel_id=1, source_target_pairs={{0,4},{1,5},{2,6},{3,7},{4,0},{5,1},{6,2},{7,3},{8,12},{9,13},{10,... | collective-permute-start | bytes 245768 | tf_op jit(solution)/shard_map/ppermute | solution.py:249
  8.7 1.9 %collective-permute-start.5 = (bf16[8,5120]{1,0:T(8,128)(2,1)S(1)}, bf16[8,5120]{1,0:T(8,128)(2,1)S(1)}, u32[]{:S(2)}, u32[]{:S(2)}) collective-permute-start(bf16[8,5120]{1,0:T(8,128)(2,1)S(1)} %collective-permute-done.3.refs_4_), channel_id=1, source_target_pairs={{0,4},{1,5},{2,6},{3,7},{4,0},{5,1},{6,2},{7,3},{8,12},{9,13},{10,... | collective-permute-start | bytes 245768 | tf_op jit(solution)/shard_map/ppermute | solution.py:249
  10.6 0.5 collective-permute-start.6
  11.1 3.3 %collective-permute-done.refs_1_ = bf16[8,5120]{1,0:T(8,128)(2,1)S(1)} collective-permute-done((bf16[8,5120]{1,0:T(8,128)(2,1)S(1)}, bf16[8,5120]{1,0:T(8,128)(2,1)S(1)}, u32[]{:S(2)}, u32[]{:S(2)}) %collective-permute-start) | collective-permute-done | bytes 81952 | tf_op jit(solution)/shard_map/ppermute | solution.py:249
  14.4 0.5 collective-permute-start.4
  15.0 3.4 %collective-permute-done.1.refs_2_ = bf16[8,5120]{1,0:T(8,128)(2,1)S(1)} collective-permute-done((bf16[8,5120]{1,0:T(8,128)(2,1)S(1)}, bf16[8,5120]{1,0:T(8,128)(2,1)S(1)}, u32[]{:S(2)}, u32[]{:S(2)}) %collective-permute-start.1) | collective-permute-done | bytes 81952 | tf_op jit(solution)/shard_map/ppermute | solution.py:249
  18.3 0.9 %collective-permute-done.5.refs_6_ = bf16[8,5120]{1,0:T(8,128)(2,1)S(1)} collective-permute-done((bf16[8,5120]{1,0:T(8,128)(2,1)S(1)}, bf16[8,5120]{1,0:T(8,128)(2,1)S(1)}, u32[]{:S(2)}, u32[]{:S(2)}) %collective-permute-start.5) | collective-permute-done | bytes 81952 | tf_op jit(solution)/shard_map/ppermute | solution.py:249
  19.2 5.0 %gate.1 = (bf16[80,4096]{1,0:T(8,128)(2,1)S(1)}, f32[80,3328]{1,0:T(8,128)S(1)}, bf16[80,3328]{1,0:T(8,128)(2,1)S(1)}, bf16[4096,1664]{1,0:T(8,128)(2,1)S(1)}) custom-call(bf16[8,5120]{1,0:T(8,128)(2,1)S(1)} %pack.1.refs_0_, bf16[8,5120]{1,0:T(8,128)(2,1)S(1)} %collective-permute-done.refs_1_, bf16[8,5120]{1,0:T(8,128)(2,1)S(1)} %collective-permute-done.1.refs_2_, ...), custom_call_target="tpu_custom_call" | custom-call | flops 10000000000 | bytes 56885248 | tf_op jit(solution)/shard_map/gate/pallas_call | solution.py:35
  24.4 7.2 %up.1 = (f32[80,3328]{1,0:T(8,128)S(1)}, bf16[80,3328]{1,0:T(8,128)(2,1)S(1)}, bf16[3328,1024]{1,0:T(8,128)(2,1)S(1)}) custom-call(bf16[80,4096]{1,0:T(8,128)(2,1)S(1)} %get-tuple-element.24.acts, bf16[4096,1664]{1,0:T(8,128)(2,1)S(1)} %get-tuple-element.25.first, bf16[4096,3328]{1,0:T(8,128)(2,1)} %codes.1, f32[128,3328]{1,0:T(8,128)S(1)} %copy-done.3, ...), custom_call_target="tpu_custom_call" | custom-call | flops 10000000000 | bytes 70516736 | tf_op jit(solution)/shard_map/up/pallas_call | solution.py:35
  31.6 0.5 collective-permute-start.8
  32.1 1.5 %collective-permute-done.8.up_other = bf16[80,3328]{1,0:T(8,128)(2,1)S(1)} collective-permute-done((bf16[80,3328]{1,0:T(8,128)(2,1)S(1)}, bf16[80,3328]{1,0:T(8,128)(2,1)S(1)}, u32[]{:S(2)}, u32[]{:S(2)}) %collective-permute-start.8) | collective-permute-done | bytes 532512 | tf_op jit(solution)/shard_map/ppermute | solution.py:252
  33.7 7.0 %first.1 = (f32[32,2560]{1,0:T(8,128)S(1)}, bf16[32,2560]{1,0:T(8,128)(2,1)S(1)}, bf16[80,3328]{1,0:T(8,128)(2,1)S(1)}, bf16[3328,1024]{1,0:T(8,128)(2,1)S(1)}) custom-call(f32[80,3328]{1,0:T(8,128)S(1)} %get-tuple-element.22.gate, bf16[80,3328]{1,0:T(8,128)(2,1)S(1)} %collective-permute-done.7.gate_other, f32[80,3328]{1,0:T(8,128)S(1)} %get-tuple-element.26.up, ...), custom_call_target="tpu_custom_call" | custom-call | flops 1090519040 | bytes 38977536 | tf_op jit(solution)/shard_map/first/pallas_call | solution.py:35
  40.6 0.6 collective-permute-start.9
  41.3 5.6 %second.1 = (f32[32,2560]{1,0:T(8,128)S(1)}, bf16[32,2560]{1,0:T(8,128)(2,1)S(1)}) custom-call(bf16[80,3328]{1,0:T(8,128)(2,1)S(1)} %get-tuple-element.31.hidden, bf16[3328,1024]{1,0:T(8,128)(2,1)S(1)} %get-tuple-element.32.codes, bf16[3328,4096]{1,0:T(8,128)(2,1)} %later.5, f32[104,4096]{1,0:T(8,128)S(1)} %copy-done.1), custom_call_target="tpu_custom_call" | custom-call | flops 1090519040 | bytes 36315136 | tf_op jit(solution)/shard_map/second/pallas_call | solution.py:35
  46.9 1.5 %collective-permute-start.10 = (bf16[32,2560]{1,0:T(8,128)(2,1)S(1)}, bf16[32,2560]{1,0:T(8,128)(2,1)S(1)}, u32[]{:S(2)}, u32[]{:S(2)}) collective-permute-start(bf16[32,2560]{1,0:T(8,128)(2,1)S(1)} %get-tuple-element.34), channel_id=1, source_target_pairs={{0,1},{1,0},{2,3},{3,2},{4,5},{5,4},{6,7},{7,6},{8,9},{9,8},{10,11... | collective-permute-start | bytes 491528 | tf_op jit(solution)/shard_map/ppermute | solution.py:246
  48.4 4.7 %collective-permute-done.10.refs_3_ = bf16[32,2560]{1,0:T(8,128)(2,1)S(1)} collective-permute-done((bf16[32,2560]{1,0:T(8,128)(2,1)S(1)}, bf16[32,2560]{1,0:T(8,128)(2,1)S(1)}, u32[]{:S(2)}, u32[]{:S(2)}) %collective-permute-start.10) | collective-permute-done | bytes 163872 | tf_op jit(solution)/shard_map/ppermute | solution.py:246
  53.2 2.1 %collective-permute-start.11 = (bf16[8,5120]{1,0:T(8,128)(2,1)S(1)}, bf16[8,5120]{1,0:T(8,128)(2,1)S(1)}, u32[]{:S(2)}, u32[]{:S(2)}) collective-permute-start(bf16[8,5120]{1,0:T(8,128)(2,1)S(1)} %get-tuple-element.36), channel_id=1, source_target_pairs={{0,6},{1,7},{2,0},{3,1},{4,2},{5,3},{6,4},{7,5},{8,14},{9,15},{10,... | collective-permute-start | bytes 245768 | tf_op jit(solution)/shard_map/ppermute | solution.py:249
  55.3 0.6 %collective-permute-start.13 = (bf16[8,5120]{1,0:T(8,128)(2,1)S(1)}, bf16[8,5120]{1,0:T(8,128)(2,1)S(1)}, u32[]{:S(2)}, u32[]{:S(2)}) collective-permute-start(bf16[8,5120]{1,0:T(8,128)(2,1)S(1)} %get-tuple-element.38), channel_id=1, source_target_pairs={{0,2},{1,3},{2,4},{3,5},{4,6},{5,7},{6,0},{7,1},{8,10},{9,11},{10,... | collective-permute-start | bytes 245768 | tf_op jit(solution)/shard_map/ppermute | solution.py:249
  55.9 2.2 %collective-permute-done.11.refs_1_ = bf16[8,5120]{1,0:T(8,128)(2,1)S(1)} collective-permute-done((bf16[8,5120]{1,0:T(8,128)(2,1)S(1)}, bf16[8,5120]{1,0:T(8,128)(2,1)S(1)}, u32[]{:S(2)}, u32[]{:S(2)}) %collective-permute-start.11) | collective-permute-done | bytes 81952 | tf_op jit(solution)/shard_map/ppermute | solution.py:249
  58.2 4.5 %collective-permute-done.12.refs_2_ = bf16[8,5120]{1,0:T(8,128)(2,1)S(1)} collective-permute-done((bf16[8,5120]{1,0:T(8,128)(2,1)S(1)}, bf16[8,5120]{1,0:T(8,128)(2,1)S(1)}, u32[]{:S(2)}, u32[]{:S(2)}) %collective-permute-start.12) | collective-permute-done | bytes 81952 | tf_op jit(solution)/shard_map/ppermute | solution.py:249
  62.7 0.7 %last.1 = bf16[10,4096]{1,0:T(8,128)(2,1)} custom-call(f32[8,5120]{1,0:T(8,128)S(1)} %get-tuple-element.35.refs_0_, bf16[8,5120]{1,0:T(8,128)(2,1)S(1)} %collective-permute-done.11.refs_1_, bf16[8,5120]{1,0:T(8,128)(2,1)S(1)} %collective-permute-done.12.refs_2_, bf16[8,5120]{1,0:T(8,128)(2,1)S(1)} %collective-permute-done.13.refs_3_), custom_call_target="tpu_custom_call" | custom-call | bytes 409600 | tf_op jit(solution)/shard_map/last/pallas_call | solution.py:35
  (21 shorter events, 0.2 us)
Async XLA Ops:
  0.0 19.2 %copy-start.2 = (f32[128,3328]{1,0:T(8,128)S(1)}, f32[128,3328]{1,0:T(8,128)}, u32[]{:S(2)}) copy-start(f32[128,3328]{1,0:T(8,128)} %refs_9_.1) | copy-start | bytes 5111812
  0.0 1.0 %copy-start.4 = (bf16[10,4096]{1,0:T(8,128)(2,1)S(1)}, bf16[10,4096]{1,0:T(8,128)(2,1)}, u32[]{:S(2)}) copy-start(bf16[10,4096]{1,0:T(8,128)(2,1)} %a_ref.1) | copy-start | bytes 245764
  1.0 18.2 %copy-start = (bf16[4096,3328]{1,0:T(8,128)(2,1)S(1)}, bf16[4096,3328]{1,0:T(8,128)(2,1)}, u32[]{:S(2)}) copy-start(bf16[4096,3328]{1,0:T(8,128)(2,1)} %refs_8_.1) | copy-start | bytes 81788928
  1.1 23.3 %copy-start.3 = (f32[128,3328]{1,0:T(8,128)S(1)}, f32[128,3328]{1,0:T(8,128)}, u32[]{:S(2)}) copy-start(f32[128,3328]{1,0:T(8,128)} %scales.3) | copy-start | bytes 5111812
  1.1 7.6 %collective-permute-start.3 = (bf16[8,5120]{1,0:T(8,128)(2,1)S(1)}, bf16[8,5120]{1,0:T(8,128)(2,1)S(1)}, u32[]{:S(2)}, u32[]{:S(2)}) collective-permute-start(bf16[8,5120]{1,0:T(8,128)(2,1)S(1)} %pack.1.refs_0_), channel_id=1, source_target_pairs={{0,1},{1,0},{2,3},{3,2},{4,5},{5,4},{6,7},{7,6},{8,9},{9,8},{10,11... | collective-permute-start | bytes 245768 | tf_op jit(solution)/shard_map/ppermute | solution.py:246
  4.1 6.5 %collective-permute-start.2 = (bf16[8,5120]{1,0:T(8,128)(2,1)S(1)}, bf16[8,5120]{1,0:T(8,128)(2,1)S(1)}, u32[]{:S(2)}, u32[]{:S(2)}) collective-permute-start(bf16[8,5120]{1,0:T(8,128)(2,1)S(1)} %pack.1.refs_0_), channel_id=1, source_target_pairs={{0,6},{1,7},{2,0},{3,1},{4,2},{5,3},{6,4},{7,5},{8,14},{9,15},{10,... | collective-permute-start | bytes 245768 | tf_op jit(solution)/shard_map/ppermute | solution.py:249
  7.7 6.8 %collective-permute-start = (bf16[8,5120]{1,0:T(8,128)(2,1)S(1)}, bf16[8,5120]{1,0:T(8,128)(2,1)S(1)}, u32[]{:S(2)}, u32[]{:S(2)}) collective-permute-start(bf16[8,5120]{1,0:T(8,128)(2,1)S(1)} %pack.1.refs_0_), channel_id=1, source_target_pairs={{0,2},{1,3},{2,4},{3,5},{4,6},{5,7},{6,0},{7,1},{8,10},{9,11},{10,... | collective-permute-start | bytes 245768 | tf_op jit(solution)/shard_map/ppermute | solution.py:249
  7.7 10.7 %collective-permute-start.1 = (bf16[8,5120]{1,0:T(8,128)(2,1)S(1)}, bf16[8,5120]{1,0:T(8,128)(2,1)S(1)}, u32[]{:S(2)}, u32[]{:S(2)}) collective-permute-start(bf16[8,5120]{1,0:T(8,128)(2,1)S(1)} %pack.1.refs_0_), channel_id=1, source_target_pairs={{0,4},{1,5},{2,6},{3,7},{4,0},{5,1},{6,2},{7,3},{8,12},{9,13},{10,... | collective-permute-start | bytes 245768 | tf_op jit(solution)/shard_map/ppermute | solution.py:249
  8.7 10.5 %collective-permute-start.5 = (bf16[8,5120]{1,0:T(8,128)(2,1)S(1)}, bf16[8,5120]{1,0:T(8,128)(2,1)S(1)}, u32[]{:S(2)}, u32[]{:S(2)}) collective-permute-start(bf16[8,5120]{1,0:T(8,128)(2,1)S(1)} %collective-permute-done.3.refs_4_), channel_id=1, source_target_pairs={{0,4},{1,5},{2,6},{3,7},{4,0},{5,1},{6,2},{7,3},{8,12},{9,13},{10,... | collective-permute-start | bytes 245768 | tf_op jit(solution)/shard_map/ppermute | solution.py:249
  10.6 8.6 %collective-permute-start.6 = (bf16[8,5120]{1,0:T(8,128)(2,1)S(1)}, bf16[8,5120]{1,0:T(8,128)(2,1)S(1)}, u32[]{:S(2)}, u32[]{:S(2)}) collective-permute-start(bf16[8,5120]{1,0:T(8,128)(2,1)S(1)} %collective-permute-done.2.refs_3_), channel_id=1, source_target_pairs={{0,1},{1,0},{2,3},{3,2},{4,5},{5,4},{6,7},{7,6},{8,9},{9,8},{10,11... | collective-permute-start | bytes 245768 | tf_op jit(solution)/shard_map/ppermute | solution.py:246
  14.4 4.8 %collective-permute-start.4 = (bf16[8,5120]{1,0:T(8,128)(2,1)S(1)}, bf16[8,5120]{1,0:T(8,128)(2,1)S(1)}, u32[]{:S(2)}, u32[]{:S(2)}) collective-permute-start(bf16[8,5120]{1,0:T(8,128)(2,1)S(1)} %collective-permute-done.refs_1_), channel_id=1, source_target_pairs={{0,1},{1,0},{2,3},{3,2},{4,5},{5,4},{6,7},{7,6},{8,9},{9,8},{10,11... | collective-permute-start | bytes 245768 | tf_op jit(solution)/shard_map/ppermute | solution.py:246
  24.3 7.8 %collective-permute-start.7 = (bf16[80,3328]{1,0:T(8,128)(2,1)S(1)}, bf16[80,3328]{1,0:T(8,128)(2,1)S(1)}, u32[]{:S(2)}, u32[]{:S(2)}) collective-permute-start(bf16[80,3328]{1,0:T(8,128)(2,1)S(1)} %get-tuple-element.23), channel_id=1, source_target_pairs={{0,8},{8,0},{1,9},{9,1},{2,10},{10,2},{3,11},{11,3},{4,12},{12,4},... | collective-permute-start | bytes 1597448 | tf_op jit(solution)/shard_map/ppermute | solution.py:252
  24.4 9.3 %copy-start.1 = (f32[104,4096]{1,0:T(8,128)S(1)}, f32[104,4096]{1,0:T(8,128)}, u32[]{:S(2)}) copy-start(f32[104,4096]{1,0:T(8,128)} %scales.5) | copy-start | bytes 5111812
  31.6 2.1 %collective-permute-start.8 = (bf16[80,3328]{1,0:T(8,128)(2,1)S(1)}, bf16[80,3328]{1,0:T(8,128)(2,1)S(1)}, u32[]{:S(2)}, u32[]{:S(2)}) collective-permute-start(bf16[80,3328]{1,0:T(8,128)(2,1)S(1)} %get-tuple-element.27), channel_id=1, source_target_pairs={{0,8},{8,0},{1,9},{9,1},{2,10},{10,2},{3,11},{11,3},{4,12},{12,4},... | collective-permute-start | bytes 1597448 | tf_op jit(solution)/shard_map/ppermute | solution.py:252
  40.6 7.8 %collective-permute-start.9 = (bf16[32,2560]{1,0:T(8,128)(2,1)S(1)}, bf16[32,2560]{1,0:T(8,128)(2,1)S(1)}, u32[]{:S(2)}, u32[]{:S(2)}) collective-permute-start(bf16[32,2560]{1,0:T(8,128)(2,1)S(1)} %get-tuple-element.30), channel_id=1, source_target_pairs={{0,1},{1,0},{2,3},{3,2},{4,5},{5,4},{6,7},{7,6},{8,9},{9,8},{10,11... | collective-permute-start | bytes 491528 | tf_op jit(solution)/shard_map/ppermute | solution.py:246
  46.9 6.3 %collective-permute-start.10 = (bf16[32,2560]{1,0:T(8,128)(2,1)S(1)}, bf16[32,2560]{1,0:T(8,128)(2,1)S(1)}, u32[]{:S(2)}, u32[]{:S(2)}) collective-permute-start(bf16[32,2560]{1,0:T(8,128)(2,1)S(1)} %get-tuple-element.34), channel_id=1, source_target_pairs={{0,1},{1,0},{2,3},{3,2},{4,5},{5,4},{6,7},{7,6},{8,9},{9,8},{10,11... | collective-permute-start | bytes 491528 | tf_op jit(solution)/shard_map/ppermute | solution.py:246
  53.2 5.0 %collective-permute-start.11 = (bf16[8,5120]{1,0:T(8,128)(2,1)S(1)}, bf16[8,5120]{1,0:T(8,128)(2,1)S(1)}, u32[]{:S(2)}, u32[]{:S(2)}) collective-permute-start(bf16[8,5120]{1,0:T(8,128)(2,1)S(1)} %get-tuple-element.36), channel_id=1, source_target_pairs={{0,6},{1,7},{2,0},{3,1},{4,2},{5,3},{6,4},{7,5},{8,14},{9,15},{10,... | collective-permute-start | bytes 245768 | tf_op jit(solution)/shard_map/ppermute | solution.py:249
  55.3 7.4 %collective-permute-start.12 = (bf16[8,5120]{1,0:T(8,128)(2,1)S(1)}, bf16[8,5120]{1,0:T(8,128)(2,1)S(1)}, u32[]{:S(2)}, u32[]{:S(2)}) collective-permute-start(bf16[8,5120]{1,0:T(8,128)(2,1)S(1)} %get-tuple-element.37), channel_id=1, source_target_pairs={{0,4},{1,5},{2,6},{3,7},{4,0},{5,1},{6,2},{7,3},{8,12},{9,13},{10,... | collective-permute-start | bytes 245768 | tf_op jit(solution)/shard_map/ppermute | solution.py:249
  55.3 7.4 %collective-permute-start.13 = (bf16[8,5120]{1,0:T(8,128)(2,1)S(1)}, bf16[8,5120]{1,0:T(8,128)(2,1)S(1)}, u32[]{:S(2)}, u32[]{:S(2)}) collective-permute-start(bf16[8,5120]{1,0:T(8,128)(2,1)S(1)} %get-tuple-element.38), channel_id=1, source_target_pairs={{0,2},{1,3},{2,4},{3,5},{4,6},{5,7},{6,0},{7,1},{8,10},{9,11},{10,... | collective-permute-start | bytes 245768 | tf_op jit(solution)/shard_map/ppermute | solution.py:249

commit v6 on v5

--- a/solution.py
+++ b/solution.py
@@ -219,17 +219,19 @@
 
 
 def last_body(halves, *refs):
-    out = refs[-1]
-    total = refs[0][...]
-    for ref in refs[1:-1]:
-        total += ref[...].astype(F32)
-    dense, width = total.shape[1] // halves, out.shape[1] // halves
+    out, count = refs[-1], len(refs) // halves
+    width = out.shape[1] // halves
     for k in range(halves):
+        terms = refs[k * count : (k + 1) * count]
+        total = terms[0][...]
+        for ref in terms[1:]:
+            total += ref[...].astype(F32)
+
         def store(row, column, values):
             column += k * width
             out[row : row + values.shape[0], column : column + values.shape[1]] = values.astype(out.dtype)
 
-        unpack_rows(total[:, k * dense : (k + 1) * dense], out.shape[0] - TILE, store)
+        unpack_rows(total, out.shape[0] - TILE, store)
 
 
 def local(peers, acts, gate_codes, gate_scales, up_codes, up_scales, down_codes, down_scales):
@@ -315,16 +317,18 @@
         apart=(2,),
     )
     if pair:
-        sums = call(
-            functools.partial(add_body, 2),
-            [sds((TILE, dense), F32)] + [sds((TILE, dense), BF16)] * (far - 1),
-            [first[0], first_other, second[0], flip(second[1])],
-            "add",
-        )
-        terms = [sums[0]] + [along(x, far - s) for s, x in zip(range(1, far), sums[1:])]
+        terms = []
+        for mine, other in ((first[0], first_other), (second[0], flip(second[1]))):
+            sums = call(
+                functools.partial(add_body, 1),
+                [sds((TILE, packed_half), F32)] + [sds((TILE, packed_half), BF16)] * (far - 1),
+                [mine, other],
+                "add",
+            )
+            terms += [sums[0]] + [along(x, far - s) for s, x in zip(range(1, far), sums[1:])]
     else:
-        both = jnp.concatenate([first[0], second[0]], axis=1)
-        terms = [lax.psum_scatter(both, "hidden", scatter_dimension=0, tiled=True)]
+        both = [lax.psum_scatter(x[0], "hidden", scatter_dimension=0, tiled=True) for x in (first, second)]
+        terms = both
     return call(functools.partial(last_body, 2), sds((m, width), BF16), terms, "last")
 
 

time: 63.6 us -> 62.3 us (0.980)
  waiting for transfers between devices: 20.6 us -> 16.5 us
  starting transfers between devices: 16.1 us -> 18.9 us
    ppermute x5, waiting for transfers between devices: 4.72 us -> 1.91 us  [flip(): return lax.ppermute(x, 'hidden', [(h, h ^ 1) for h in range(peers)])]
    ppermute x7 -> x10, starting transfers between devices: 9.28 us -> 12 us  [along(): lax.ppermute(x, 'hidden', [(h, (h + 2 * s) % peers) for h in range(peers)])]
    ppermute x7 -> x10, waiting for transfers between devices: 14.3 us -> 13.1 us  [along(): lax.ppermute(x, 'hidden', [(h, (h + 2 * s) % peers) for h in range(peers)])]
    pallas_call x7 -> x8, Pallas kernels: 25.6 us -> 25.6 us  [call(): pl.pallas_call(body, in_specs=[pl.BlockSpec(memory_space=pltpu.HBM if i i...]
  transfers between devices with their start and end apart: 14 -> 17, of which waited for: 7 -> 9; matrix products, arithmetic and copies ran while one was open for 0% -> 0% of each run, Pallas kernels for 20% -> 21%
where the time goes in v6:
time: 62.3 us; the launch traced here: 62.1 us
  Pallas kernels  25.6 us (41%)
  starting transfers between devices  18.9 us (30%)
  waiting for transfers between devices  16.5 us (26%)
  local copies, waits for them, and re-layouts  1.05 us (2%)
    pallas_call x8, Pallas kernels, call(): pl.pallas_call(body, in_specs=[pl.BlockSpec(memory_space=pltpu.HBM if i i...  25.6 us
    ppermute x10, waiting for transfers between devices, along(): lax.ppermute(x, 'hidden', [(h, (h + 2 * s) % peers) for h in range(peers)])  13.1 us
    ppermute x10, starting transfers between devices, along(): lax.ppermute(x, 'hidden', [(h, (h + 2 * s) % peers) for h in range(peers)])  12 us
    ppermute x5, starting transfers between devices, flip(): return lax.ppermute(x, 'hidden', [(h, h ^ 1) for h in range(peers)])  6.24 us
    ppermute x5, waiting for transfers between devices, flip(): return lax.ppermute(x, 'hidden', [(h, h ^ 1) for h in range(peers)])  1.91 us
    ppermute x2, waiting for transfers between devices, swap(): return lax.ppermute(x, 'width', [(0, 1), (1, 0)])  1.55 us
  transfers between devices with their start and end apart: 17, of which 9 were waited for; matrix products, arithmetic and copies ran while one was open for 0% of the time, Pallas kernels for 21%

profile of v6, /device:TPU:0, one launch (start us, length us, event | category | flops | bytes accessed | tf_op | source)
XLA Modules:
  0.0 62.1 jit_solution(7298003390252579082)
XLA Ops:
  0.0 1.0 %copy-done.4 = bf16[10,4096]{1,0:T(8,128)(2,1)S(1)} copy-done((bf16[10,4096]{1,0:T(8,128)(2,1)S(1)}, bf16[10,4096]{1,0:T(8,128)(2,1)}, u32[]{:S(2)}) %copy-start.4) | copy-done | bytes 81944
  1.1 3.0 %collective-permute-start.3 = (bf16[8,5120]{1,0:T(8,128)(2,1)S(1)}, bf16[8,5120]{1,0:T(8,128)(2,1)S(1)}, u32[]{:S(2)}, u32[]{:S(2)}) collective-permute-start(bf16[8,5120]{1,0:T(8,128)(2,1)S(1)} %pack.1.refs_0_), channel_id=1, source_target_pairs={{0,1},{1,0},{2,3},{3,2},{4,5},{5,4},{6,7},{7,6},{8,9},{9,8},{10,11... | collective-permute-start | bytes 245768 | tf_op jit(solution)/shard_map/ppermute | solution.py:248
  4.1 3.6 %collective-permute-start.2 = (bf16[8,5120]{1,0:T(8,128)(2,1)S(1)}, bf16[8,5120]{1,0:T(8,128)(2,1)S(1)}, u32[]{:S(2)}, u32[]{:S(2)}) collective-permute-start(bf16[8,5120]{1,0:T(8,128)(2,1)S(1)} %pack.1.refs_0_), channel_id=1, source_target_pairs={{0,6},{1,7},{2,0},{3,1},{4,2},{5,3},{6,4},{7,5},{8,14},{9,15},{10,... | collective-permute-start | bytes 245768 | tf_op jit(solution)/shard_map/ppermute | solution.py:251
  7.7 1.0 %collective-permute-start.1 = (bf16[8,5120]{1,0:T(8,128)(2,1)S(1)}, bf16[8,5120]{1,0:T(8,128)(2,1)S(1)}, u32[]{:S(2)}, u32[]{:S(2)}) collective-permute-start(bf16[8,5120]{1,0:T(8,128)(2,1)S(1)} %pack.1.refs_0_), channel_id=1, source_target_pairs={{0,4},{1,5},{2,6},{3,7},{4,0},{5,1},{6,2},{7,3},{8,12},{9,13},{10,... | collective-permute-start | bytes 245768 | tf_op jit(solution)/shard_map/ppermute | solution.py:251
  8.7 1.9 %collective-permute-start.5 = (bf16[8,5120]{1,0:T(8,128)(2,1)S(1)}, bf16[8,5120]{1,0:T(8,128)(2,1)S(1)}, u32[]{:S(2)}, u32[]{:S(2)}) collective-permute-start(bf16[8,5120]{1,0:T(8,128)(2,1)S(1)} %collective-permute-done.3.refs_4_), channel_id=1, source_target_pairs={{0,4},{1,5},{2,6},{3,7},{4,0},{5,1},{6,2},{7,3},{8,12},{9,13},{10,... | collective-permute-start | bytes 245768 | tf_op jit(solution)/shard_map/ppermute | solution.py:251
  11.1 3.3 %collective-permute-done.refs_1_ = bf16[8,5120]{1,0:T(8,128)(2,1)S(1)} collective-permute-done((bf16[8,5120]{1,0:T(8,128)(2,1)S(1)}, bf16[8,5120]{1,0:T(8,128)(2,1)S(1)}, u32[]{:S(2)}, u32[]{:S(2)}) %collective-permute-start) | collective-permute-done | bytes 81952 | tf_op jit(solution)/shard_map/ppermute | solution.py:251
  15.0 3.4 %collective-permute-done.1.refs_2_ = bf16[8,5120]{1,0:T(8,128)(2,1)S(1)} collective-permute-done((bf16[8,5120]{1,0:T(8,128)(2,1)S(1)}, bf16[8,5120]{1,0:T(8,128)(2,1)S(1)}, u32[]{:S(2)}, u32[]{:S(2)}) %collective-permute-start.1) | collective-permute-done | bytes 81952 | tf_op jit(solution)/shard_map/ppermute | solution.py:251
  18.3 0.9 %collective-permute-done.5.refs_6_ = bf16[8,5120]{1,0:T(8,128)(2,1)S(1)} collective-permute-done((bf16[8,5120]{1,0:T(8,128)(2,1)S(1)}, bf16[8,5120]{1,0:T(8,128)(2,1)S(1)}, u32[]{:S(2)}, u32[]{:S(2)}) %collective-permute-start.5) | collective-permute-done | bytes 81952 | tf_op jit(solution)/shard_map/ppermute | solution.py:251
  19.2 5.0 %gate.1 = (bf16[80,4096]{1,0:T(8,128)(2,1)S(1)}, f32[80,3328]{1,0:T(8,128)S(1)}, bf16[80,3328]{1,0:T(8,128)(2,1)S(1)}, bf16[4096,1664]{1,0:T(8,128)(2,1)S(1)}) custom-call(bf16[8,5120]{1,0:T(8,128)(2,1)S(1)} %pack.1.refs_0_, bf16[8,5120]{1,0:T(8,128)(2,1)S(1)} %collective-permute-done.refs_1_, bf16[8,5120]{1,0:T(8,128)(2,1)S(1)} %collective-permute-done.1.refs_2_, ...), custom_call_target="tpu_custom_call" | custom-call | flops 10000000000 | bytes 56885248 | tf_op jit(solution)/shard_map/gate/pallas_call | solution.py:35
  24.4 7.2 %up.1 = (f32[80,3328]{1,0:T(8,128)S(1)}, bf16[80,3328]{1,0:T(8,128)(2,1)S(1)}, bf16[3328,1024]{1,0:T(8,128)(2,1)S(1)}) custom-call(bf16[80,4096]{1,0:T(8,128)(2,1)S(1)} %get-tuple-element.28.acts, bf16[4096,1664]{1,0:T(8,128)(2,1)S(1)} %get-tuple-element.29.first, bf16[4096,3328]{1,0:T(8,128)(2,1)} %codes.1, f32[128,3328]{1,0:T(8,128)S(1)} %copy-done.3, ...), custom_call_target="tpu_custom_call" | custom-call | flops 10000000000 | bytes 70516736 | tf_op jit(solution)/shard_map/up/pallas_call | solution.py:35
  32.1 1.5 %collective-permute-done.8.up_other = bf16[80,3328]{1,0:T(8,128)(2,1)S(1)} collective-permute-done((bf16[80,3328]{1,0:T(8,128)(2,1)S(1)}, bf16[80,3328]{1,0:T(8,128)(2,1)S(1)}, u32[]{:S(2)}, u32[]{:S(2)}) %collective-permute-start.8) | collective-permute-done | bytes 532512 | tf_op jit(solution)/shard_map/ppermute | solution.py:254
  33.7 7.0 %first.1 = (f32[32,2560]{1,0:T(8,128)S(1)}, bf16[32,2560]{1,0:T(8,128)(2,1)S(1)}, bf16[80,3328]{1,0:T(8,128)(2,1)S(1)}, bf16[3328,1024]{1,0:T(8,128)(2,1)S(1)}) custom-call(f32[80,3328]{1,0:T(8,128)S(1)} %get-tuple-element.26.gate, bf16[80,3328]{1,0:T(8,128)(2,1)S(1)} %collective-permute-done.7.gate_other, f32[80,3328]{1,0:T(8,128)S(1)} %get-tuple-element.30.up, ...), custom_call_target="tpu_custom_call" | custom-call | flops 1090519040 | bytes 38977536 | tf_op jit(solution)/shard_map/first/pallas_call | solution.py:35
  40.6 0.6 %collective-permute-start.9 = (bf16[32,2560]{1,0:T(8,128)(2,1)S(1)}, bf16[32,2560]{1,0:T(8,128)(2,1)S(1)}, u32[]{:S(2)}, u32[]{:S(2)}) collective-permute-start(bf16[32,2560]{1,0:T(8,128)(2,1)S(1)} %get-tuple-element.34), channel_id=1, source_target_pairs={{0,1},{1,0},{2,3},{3,2},{4,5},{5,4},{6,7},{7,6},{8,9},{9,8},{10,11... | collective-permute-start | bytes 491528 | tf_op jit(solution)/shard_map/ppermute | solution.py:248
  41.3 5.6 %second.1 = (f32[32,2560]{1,0:T(8,128)S(1)}, bf16[32,2560]{1,0:T(8,128)(2,1)S(1)}) custom-call(bf16[80,3328]{1,0:T(8,128)(2,1)S(1)} %get-tuple-element.39.hidden, bf16[3328,1024]{1,0:T(8,128)(2,1)S(1)} %get-tuple-element.40.codes, bf16[3328,4096]{1,0:T(8,128)(2,1)} %later.5, f32[104,4096]{1,0:T(8,128)S(1)} %copy-done.1), custom_call_target="tpu_custom_call" | custom-call | flops 1090519040 | bytes 36315136 | tf_op jit(solution)/shard_map/second/pallas_call | solution.py:35
  46.9 1.5 %collective-permute-start.13 = (bf16[32,2560]{1,0:T(8,128)(2,1)S(1)}, bf16[32,2560]{1,0:T(8,128)(2,1)S(1)}, u32[]{:S(2)}, u32[]{:S(2)}) collective-permute-start(bf16[32,2560]{1,0:T(8,128)(2,1)S(1)} %get-tuple-element.42), channel_id=1, source_target_pairs={{0,1},{1,0},{2,3},{3,2},{4,5},{5,4},{6,7},{7,6},{8,9},{9,8},{10,11... | collective-permute-start | bytes 491528 | tf_op jit(solution)/shard_map/ppermute | solution.py:248
  48.4 2.1 %collective-permute-start.10 = (bf16[8,2560]{1,0:T(8,128)(2,1)S(1)}, bf16[8,2560]{1,0:T(8,128)(2,1)S(1)}, u32[]{:S(2)}, u32[]{:S(2)}) collective-permute-start(bf16[8,2560]{1,0:T(8,128)(2,1)S(1)} %get-tuple-element.36), channel_id=1, source_target_pairs={{0,6},{1,7},{2,0},{3,1},{4,2},{5,3},{6,4},{7,5},{8,14},{9,15},{10,... | collective-permute-start | bytes 122888 | tf_op jit(solution)/shard_map/ppermute | solution.py:251
  50.6 0.6 %collective-permute-start.12 = (bf16[8,2560]{1,0:T(8,128)(2,1)S(1)}, bf16[8,2560]{1,0:T(8,128)(2,1)S(1)}, u32[]{:S(2)}, u32[]{:S(2)}) collective-permute-start(bf16[8,2560]{1,0:T(8,128)(2,1)S(1)} %get-tuple-element.38), channel_id=1, source_target_pairs={{0,2},{1,3},{2,4},{3,5},{4,6},{5,7},{6,0},{7,1},{8,10},{9,11},{10,... | collective-permute-start | bytes 122888 | tf_op jit(solution)/shard_map/ppermute | solution.py:251
  51.2 1.9 %collective-permute-done.13.refs_1_ = bf16[32,2560]{1,0:T(8,128)(2,1)S(1)} collective-permute-done((bf16[32,2560]{1,0:T(8,128)(2,1)S(1)}, bf16[32,2560]{1,0:T(8,128)(2,1)S(1)}, u32[]{:S(2)}, u32[]{:S(2)}) %collective-permute-start.13) | collective-permute-done | bytes 163872 | tf_op jit(solution)/shard_map/ppermute | solution.py:248
  53.2 2.1 %collective-permute-start.14 = (bf16[8,2560]{1,0:T(8,128)(2,1)S(1)}, bf16[8,2560]{1,0:T(8,128)(2,1)S(1)}, u32[]{:S(2)}, u32[]{:S(2)}) collective-permute-start(bf16[8,2560]{1,0:T(8,128)(2,1)S(1)} %get-tuple-element.44), channel_id=1, source_target_pairs={{0,6},{1,7},{2,0},{3,1},{4,2},{5,3},{6,4},{7,5},{8,14},{9,15},{10,... | collective-permute-start | bytes 122888 | tf_op jit(solution)/shard_map/ppermute | solution.py:251
  55.9 0.7 %collective-permute-done.11.refs_2_ = bf16[8,2560]{1,0:T(8,128)(2,1)S(1)} collective-permute-done((bf16[8,2560]{1,0:T(8,128)(2,1)S(1)}, bf16[8,2560]{1,0:T(8,128)(2,1)S(1)}, u32[]{:S(2)}, u32[]{:S(2)}) %collective-permute-start.11) | collective-permute-done | bytes 40992 | tf_op jit(solution)/shard_map/ppermute | solution.py:251
  56.6 0.6 collective-permute-done.14.refs_5_
  57.2 3.0 %collective-permute-done.15.refs_6_ = bf16[8,2560]{1,0:T(8,128)(2,1)S(1)} collective-permute-done((bf16[8,2560]{1,0:T(8,128)(2,1)S(1)}, bf16[8,2560]{1,0:T(8,128)(2,1)S(1)}, u32[]{:S(2)}, u32[]{:S(2)}) %collective-permute-start.15) | collective-permute-done | bytes 40992 | tf_op jit(solution)/shard_map/ppermute | solution.py:251
  60.2 1.3 %collective-permute-done.16.refs_7_ = bf16[8,2560]{1,0:T(8,128)(2,1)S(1)} collective-permute-done((bf16[8,2560]{1,0:T(8,128)(2,1)S(1)}, bf16[8,2560]{1,0:T(8,128)(2,1)S(1)}, u32[]{:S(2)}, u32[]{:S(2)}) %collective-permute-start.16) | collective-permute-done | bytes 40992 | tf_op jit(solution)/shard_map/ppermute | solution.py:251
  61.4 0.7 %last.1 = bf16[10,4096]{1,0:T(8,128)(2,1)} custom-call(f32[8,2560]{1,0:T(8,128)S(1)} %get-tuple-element.35.refs_0_, bf16[8,2560]{1,0:T(8,128)(2,1)S(1)} %collective-permute-done.10.refs_1_, bf16[8,2560]{1,0:T(8,128)(2,1)S(1)} %collective-permute-done.11.refs_2_, bf16[8,2560]{1,0:T(8,128)(2,1)S(1)} %collective-permute-done.12.refs_3_, ...), custom_call_target="tpu_custom_call" | custom-call | bytes 409600 | tf_op jit(solution)/shard_map/last/pallas_call | solution.py:35
  (28 shorter events, 2.5 us)
Async XLA Ops:
  0.0 19.2 %copy-start.2 = (f32[128,3328]{1,0:T(8,128)S(1)}, f32[128,3328]{1,0:T(8,128)}, u32[]{:S(2)}) copy-start(f32[128,3328]{1,0:T(8,128)} %refs_9_.1) | copy-start | bytes 5111812
  0.0 1.0 %copy-start.4 = (bf16[10,4096]{1,0:T(8,128)(2,1)S(1)}, bf16[10,4096]{1,0:T(8,128)(2,1)}, u32[]{:S(2)}) copy-start(bf16[10,4096]{1,0:T(8,128)(2,1)} %a_ref.1) | copy-start | bytes 245764
  1.0 18.2 %copy-start = (bf16[4096,3328]{1,0:T(8,128)(2,1)S(1)}, bf16[4096,3328]{1,0:T(8,128)(2,1)}, u32[]{:S(2)}) copy-start(bf16[4096,3328]{1,0:T(8,128)(2,1)} %refs_8_.1) | copy-start | bytes 81788928
  1.1 23.3 %copy-start.3 = (f32[128,3328]{1,0:T(8,128)S(1)}, f32[128,3328]{1,0:T(8,128)}, u32[]{:S(2)}) copy-start(f32[128,3328]{1,0:T(8,128)} %scales.3) | copy-start | bytes 5111812
  1.1 7.6 %collective-permute-start.3 = (bf16[8,5120]{1,0:T(8,128)(2,1)S(1)}, bf16[8,5120]{1,0:T(8,128)(2,1)S(1)}, u32[]{:S(2)}, u32[]{:S(2)}) collective-permute-start(bf16[8,5120]{1,0:T(8,128)(2,1)S(1)} %pack.1.refs_0_), channel_id=1, source_target_pairs={{0,1},{1,0},{2,3},{3,2},{4,5},{5,4},{6,7},{7,6},{8,9},{9,8},{10,11... | collective-permute-start | bytes 245768 | tf_op jit(solution)/shard_map/ppermute | solution.py:248
  4.1 6.5 %collective-permute-start.2 = (bf16[8,5120]{1,0:T(8,128)(2,1)S(1)}, bf16[8,5120]{1,0:T(8,128)(2,1)S(1)}, u32[]{:S(2)}, u32[]{:S(2)}) collective-permute-start(bf16[8,5120]{1,0:T(8,128)(2,1)S(1)} %pack.1.refs_0_), channel_id=1, source_target_pairs={{0,6},{1,7},{2,0},{3,1},{4,2},{5,3},{6,4},{7,5},{8,14},{9,15},{10,... | collective-permute-start | bytes 245768 | tf_op jit(solution)/shard_map/ppermute | solution.py:251
  7.7 6.8 %collective-permute-start = (bf16[8,5120]{1,0:T(8,128)(2,1)S(1)}, bf16[8,5120]{1,0:T(8,128)(2,1)S(1)}, u32[]{:S(2)}, u32[]{:S(2)}) collective-permute-start(bf16[8,5120]{1,0:T(8,128)(2,1)S(1)} %pack.1.refs_0_), channel_id=1, source_target_pairs={{0,2},{1,3},{2,4},{3,5},{4,6},{5,7},{6,0},{7,1},{8,10},{9,11},{10,... | collective-permute-start | bytes 245768 | tf_op jit(solution)/shard_map/ppermute | solution.py:251
  7.7 10.7 %collective-permute-start.1 = (bf16[8,5120]{1,0:T(8,128)(2,1)S(1)}, bf16[8,5120]{1,0:T(8,128)(2,1)S(1)}, u32[]{:S(2)}, u32[]{:S(2)}) collective-permute-start(bf16[8,5120]{1,0:T(8,128)(2,1)S(1)} %pack.1.refs_0_), channel_id=1, source_target_pairs={{0,4},{1,5},{2,6},{3,7},{4,0},{5,1},{6,2},{7,3},{8,12},{9,13},{10,... | collective-permute-start | bytes 245768 | tf_op jit(solution)/shard_map/ppermute | solution.py:251
  8.7 10.5 %collective-permute-start.5 = (bf16[8,5120]{1,0:T(8,128)(2,1)S(1)}, bf16[8,5120]{1,0:T(8,128)(2,1)S(1)}, u32[]{:S(2)}, u32[]{:S(2)}) collective-permute-start(bf16[8,5120]{1,0:T(8,128)(2,1)S(1)} %collective-permute-done.3.refs_4_), channel_id=1, source_target_pairs={{0,4},{1,5},{2,6},{3,7},{4,0},{5,1},{6,2},{7,3},{8,12},{9,13},{10,... | collective-permute-start | bytes 245768 | tf_op jit(solution)/shard_map/ppermute | solution.py:251
  10.6 8.6 %collective-permute-start.6 = (bf16[8,5120]{1,0:T(8,128)(2,1)S(1)}, bf16[8,5120]{1,0:T(8,128)(2,1)S(1)}, u32[]{:S(2)}, u32[]{:S(2)}) collective-permute-start(bf16[8,5120]{1,0:T(8,128)(2,1)S(1)} %collective-permute-done.2.refs_3_), channel_id=1, source_target_pairs={{0,1},{1,0},{2,3},{3,2},{4,5},{5,4},{6,7},{7,6},{8,9},{9,8},{10,11... | collective-permute-start | bytes 245768 | tf_op jit(solution)/shard_map/ppermute | solution.py:248
  14.4 4.8 %collective-permute-start.4 = (bf16[8,5120]{1,0:T(8,128)(2,1)S(1)}, bf16[8,5120]{1,0:T(8,128)(2,1)S(1)}, u32[]{:S(2)}, u32[]{:S(2)}) collective-permute-start(bf16[8,5120]{1,0:T(8,128)(2,1)S(1)} %collective-permute-done.refs_1_), channel_id=1, source_target_pairs={{0,1},{1,0},{2,3},{3,2},{4,5},{5,4},{6,7},{7,6},{8,9},{9,8},{10,11... | collective-permute-start | bytes 245768 | tf_op jit(solution)/shard_map/ppermute | solution.py:248
  24.3 7.8 %collective-permute-start.7 = (bf16[80,3328]{1,0:T(8,128)(2,1)S(1)}, bf16[80,3328]{1,0:T(8,128)(2,1)S(1)}, u32[]{:S(2)}, u32[]{:S(2)}) collective-permute-start(bf16[80,3328]{1,0:T(8,128)(2,1)S(1)} %get-tuple-element.27), channel_id=1, source_target_pairs={{0,8},{8,0},{1,9},{9,1},{2,10},{10,2},{3,11},{11,3},{4,12},{12,4},... | collective-permute-start | bytes 1597448 | tf_op jit(solution)/shard_map/ppermute | solution.py:254
  24.4 9.3 %copy-start.1 = (f32[104,4096]{1,0:T(8,128)S(1)}, f32[104,4096]{1,0:T(8,128)}, u32[]{:S(2)}) copy-start(f32[104,4096]{1,0:T(8,128)} %scales.5) | copy-start | bytes 5111812
  31.6 2.1 %collective-permute-start.8 = (bf16[80,3328]{1,0:T(8,128)(2,1)S(1)}, bf16[80,3328]{1,0:T(8,128)(2,1)S(1)}, u32[]{:S(2)}, u32[]{:S(2)}) collective-permute-start(bf16[80,3328]{1,0:T(8,128)(2,1)S(1)} %get-tuple-element.31), channel_id=1, source_target_pairs={{0,8},{8,0},{1,9},{9,1},{2,10},{10,2},{3,11},{11,3},{4,12},{12,4},... | collective-permute-start | bytes 1597448 | tf_op jit(solution)/shard_map/ppermute | solution.py:254
  40.6 7.8 %collective-permute-start.9 = (bf16[32,2560]{1,0:T(8,128)(2,1)S(1)}, bf16[32,2560]{1,0:T(8,128)(2,1)S(1)}, u32[]{:S(2)}, u32[]{:S(2)}) collective-permute-start(bf16[32,2560]{1,0:T(8,128)(2,1)S(1)} %get-tuple-element.34), channel_id=1, source_target_pairs={{0,1},{1,0},{2,3},{3,2},{4,5},{5,4},{6,7},{7,6},{8,9},{9,8},{10,11... | collective-permute-start | bytes 491528 | tf_op jit(solution)/shard_map/ppermute | solution.py:248
  46.9 6.3 %collective-permute-start.13 = (bf16[32,2560]{1,0:T(8,128)(2,1)S(1)}, bf16[32,2560]{1,0:T(8,128)(2,1)S(1)}, u32[]{:S(2)}, u32[]{:S(2)}) collective-permute-start(bf16[32,2560]{1,0:T(8,128)(2,1)S(1)} %get-tuple-element.42), channel_id=1, source_target_pairs={{0,1},{1,0},{2,3},{3,2},{4,5},{5,4},{6,7},{7,6},{8,9},{9,8},{10,11... | collective-permute-start | bytes 491528 | tf_op jit(solution)/shard_map/ppermute | solution.py:248
  48.4 7.2 %collective-permute-start.10 = (bf16[8,2560]{1,0:T(8,128)(2,1)S(1)}, bf16[8,2560]{1,0:T(8,128)(2,1)S(1)}, u32[]{:S(2)}, u32[]{:S(2)}) collective-permute-start(bf16[8,2560]{1,0:T(8,128)(2,1)S(1)} %get-tuple-element.36), channel_id=1, source_target_pairs={{0,6},{1,7},{2,0},{3,1},{4,2},{5,3},{6,4},{7,5},{8,14},{9,15},{10,... | collective-permute-start | bytes 122888 | tf_op jit(solution)/shard_map/ppermute | solution.py:251
  50.6 6.0 %collective-permute-start.11 = (bf16[8,2560]{1,0:T(8,128)(2,1)S(1)}, bf16[8,2560]{1,0:T(8,128)(2,1)S(1)}, u32[]{:S(2)}, u32[]{:S(2)}) collective-permute-start(bf16[8,2560]{1,0:T(8,128)(2,1)S(1)} %get-tuple-element.37), channel_id=1, source_target_pairs={{0,4},{1,5},{2,6},{3,7},{4,0},{5,1},{6,2},{7,3},{8,12},{9,13},{10,... | collective-permute-start | bytes 122888 | tf_op jit(solution)/shard_map/ppermute | solution.py:251
  50.6 6.0 %collective-permute-start.12 = (bf16[8,2560]{1,0:T(8,128)(2,1)S(1)}, bf16[8,2560]{1,0:T(8,128)(2,1)S(1)}, u32[]{:S(2)}, u32[]{:S(2)}) collective-permute-start(bf16[8,2560]{1,0:T(8,128)(2,1)S(1)} %get-tuple-element.38), channel_id=1, source_target_pairs={{0,2},{1,3},{2,4},{3,5},{4,6},{5,7},{6,0},{7,1},{8,10},{9,11},{10,... | collective-permute-start | bytes 122888 | tf_op jit(solution)/shard_map/ppermute | solution.py:251
  53.2 4.1 %collective-permute-start.14 = (bf16[8,2560]{1,0:T(8,128)(2,1)S(1)}, bf16[8,2560]{1,0:T(8,128)(2,1)S(1)}, u32[]{:S(2)}, u32[]{:S(2)}) collective-permute-start(bf16[8,2560]{1,0:T(8,128)(2,1)S(1)} %get-tuple-element.44), channel_id=1, source_target_pairs={{0,6},{1,7},{2,0},{3,1},{4,2},{5,3},{6,4},{7,5},{8,14},{9,15},{10,... | collective-permute-start | bytes 122888 | tf_op jit(solution)/shard_map/ppermute | solution.py:251
  55.3 4.9 %collective-permute-start.15 = (bf16[8,2560]{1,0:T(8,128)(2,1)S(1)}, bf16[8,2560]{1,0:T(8,128)(2,1)S(1)}, u32[]{:S(2)}, u32[]{:S(2)}) collective-permute-start(bf16[8,2560]{1,0:T(8,128)(2,1)S(1)} %get-tuple-element.45), channel_id=1, source_target_pairs={{0,4},{1,5},{2,6},{3,7},{4,0},{5,1},{6,2},{7,3},{8,12},{9,13},{10,... | collective-permute-start | bytes 122888 | tf_op jit(solution)/shard_map/ppermute | solution.py:251
  55.6 5.8 %collective-permute-start.16 = (bf16[8,2560]{1,0:T(8,128)(2,1)S(1)}, bf16[8,2560]{1,0:T(8,128)(2,1)S(1)}, u32[]{:S(2)}, u32[]{:S(2)}) collective-permute-start(bf16[8,2560]{1,0:T(8,128)(2,1)S(1)} %get-tuple-element.46), channel_id=1, source_target_pairs={{0,2},{1,3},{2,4},{3,5},{4,6},{5,7},{6,0},{7,1},{8,10},{9,11},{10,... | collective-permute-start | bytes 122888 | tf_op jit(solution)/shard_map/ppermute | solution.py:251

commit v7 on v6

--- a/solution.py
+++ b/solution.py
@@ -185,8 +185,9 @@
         u = up[:, cols] + up_other[:, cols].astype(F32)
         hidden[:, cols] = (jax.nn.silu(g) * u).astype(BF16)
     copies.start()
-    terms[:, :size] = project(hidden, codes, 0, scales, 0, size)
-    copies.start()
+    for k in range(2):
+        terms[:, k * part : (k + 1) * part] = project(hidden, codes, k * part, scales, k * part, part)
+        copies.start()
     for k in range(2):
         copies.wait(k)
         terms[:, size + k * part : size + (k + 1) * part] = project(hidden, tail, k * part, scales, size + k * part, part)

time: 62.3 us -> 61.6 us (0.989)
  Pallas kernels: 25.6 us -> 24.9 us
    pallas_call x8, Pallas kernels: 25.6 us -> 24.9 us  [call(): pl.pallas_call(body, in_specs=[pl.BlockSpec(memory_space=pltpu.HBM if i i...]
where the time goes in v7:
time: 61.6 us; the launch traced here: 61.5 us
  Pallas kernels  24.9 us (40%)
  starting transfers between devices  18.9 us (31%)
  waiting for transfers between devices  16.5 us (27%)
  local copies, waits for them, and re-layouts  1.05 us (2%)
    pallas_call x8, Pallas kernels, call(): pl.pallas_call(body, in_specs=[pl.BlockSpec(memory_space=pltpu.HBM if i i...  24.9 us
    ppermute x10, waiting for transfers between devices, along(): lax.ppermute(x, 'hidden', [(h, (h + 2 * s) % peers) for h in range(peers)])  13.1 us
    ppermute x10, starting transfers between devices, along(): lax.ppermute(x, 'hidden', [(h, (h + 2 * s) % peers) for h in range(peers)])  12 us
    ppermute x5, starting transfers between devices, flip(): return lax.ppermute(x, 'hidden', [(h, h ^ 1) for h in range(peers)])  6.24 us
    ppermute x5, waiting for transfers between devices, flip(): return lax.ppermute(x, 'hidden', [(h, h ^ 1) for h in range(peers)])  1.91 us
    ppermute x2, waiting for transfers between devices, swap(): return lax.ppermute(x, 'width', [(0, 1), (1, 0)])  1.55 us
  transfers between devices with their start and end apart: 17, of which 9 were waited for; matrix products, arithmetic and copies ran while one was open for 0% of the time, Pallas kernels for 21%

profile of v7, /device:TPU:0, one launch (start us, length us, event | category | flops | bytes accessed | tf_op | source)
XLA Modules:
  0.0 61.5 jit_solution(16143136396535427396)
XLA Ops:
  0.0 1.0 %copy-done.4 = bf16[10,4096]{1,0:T(8,128)(2,1)S(1)} copy-done((bf16[10,4096]{1,0:T(8,128)(2,1)S(1)}, bf16[10,4096]{1,0:T(8,128)(2,1)}, u32[]{:S(2)}) %copy-start.4) | copy-done | bytes 81944
  1.1 3.0 %collective-permute-start.3 = (bf16[8,5120]{1,0:T(8,128)(2,1)S(1)}, bf16[8,5120]{1,0:T(8,128)(2,1)S(1)}, u32[]{:S(2)}, u32[]{:S(2)}) collective-permute-start(bf16[8,5120]{1,0:T(8,128)(2,1)S(1)} %pack.1.refs_0_), channel_id=1, source_target_pairs={{0,1},{1,0},{2,3},{3,2},{4,5},{5,4},{6,7},{7,6},{8,9},{9,8},{10,11... | collective-permute-start | bytes 245768 | tf_op jit(solution)/shard_map/ppermute | solution.py:249
  4.1 3.6 %collective-permute-start.2 = (bf16[8,5120]{1,0:T(8,128)(2,1)S(1)}, bf16[8,5120]{1,0:T(8,128)(2,1)S(1)}, u32[]{:S(2)}, u32[]{:S(2)}) collective-permute-start(bf16[8,5120]{1,0:T(8,128)(2,1)S(1)} %pack.1.refs_0_), channel_id=1, source_target_pairs={{0,6},{1,7},{2,0},{3,1},{4,2},{5,3},{6,4},{7,5},{8,14},{9,15},{10,... | collective-permute-start | bytes 245768 | tf_op jit(solution)/shard_map/ppermute | solution.py:252
  7.7 1.0 %collective-permute-start.1 = (bf16[8,5120]{1,0:T(8,128)(2,1)S(1)}, bf16[8,5120]{1,0:T(8,128)(2,1)S(1)}, u32[]{:S(2)}, u32[]{:S(2)}) collective-permute-start(bf16[8,5120]{1,0:T(8,128)(2,1)S(1)} %pack.1.refs_0_), channel_id=1, source_target_pairs={{0,4},{1,5},{2,6},{3,7},{4,0},{5,1},{6,2},{7,3},{8,12},{9,13},{10,... | collective-permute-start | bytes 245768 | tf_op jit(solution)/shard_map/ppermute | solution.py:252
  8.7 1.9 %collective-permute-start.5 = (bf16[8,5120]{1,0:T(8,128)(2,1)S(1)}, bf16[8,5120]{1,0:T(8,128)(2,1)S(1)}, u32[]{:S(2)}, u32[]{:S(2)}) collective-permute-start(bf16[8,5120]{1,0:T(8,128)(2,1)S(1)} %collective-permute-done.3.refs_4_), channel_id=1, source_target_pairs={{0,4},{1,5},{2,6},{3,7},{4,0},{5,1},{6,2},{7,3},{8,12},{9,13},{10,... | collective-permute-start | bytes 245768 | tf_op jit(solution)/shard_map/ppermute | solution.py:252
  11.1 3.3 %collective-permute-done.refs_1_ = bf16[8,5120]{1,0:T(8,128)(2,1)S(1)} collective-permute-done((bf16[8,5120]{1,0:T(8,128)(2,1)S(1)}, bf16[8,5120]{1,0:T(8,128)(2,1)S(1)}, u32[]{:S(2)}, u32[]{:S(2)}) %collective-permute-start) | collective-permute-done | bytes 81952 | tf_op jit(solution)/shard_map/ppermute | solution.py:252
  15.0 3.4 %collective-permute-done.1.refs_2_ = bf16[8,5120]{1,0:T(8,128)(2,1)S(1)} collective-permute-done((bf16[8,5120]{1,0:T(8,128)(2,1)S(1)}, bf16[8,5120]{1,0:T(8,128)(2,1)S(1)}, u32[]{:S(2)}, u32[]{:S(2)}) %collective-permute-start.1) | collective-permute-done | bytes 81952 | tf_op jit(solution)/shard_map/ppermute | solution.py:252
  18.3 0.9 %collective-permute-done.5.refs_6_ = bf16[8,5120]{1,0:T(8,128)(2,1)S(1)} collective-permute-done((bf16[8,5120]{1,0:T(8,128)(2,1)S(1)}, bf16[8,5120]{1,0:T(8,128)(2,1)S(1)}, u32[]{:S(2)}, u32[]{:S(2)}) %collective-permute-start.5) | collective-permute-done | bytes 81952 | tf_op jit(solution)/shard_map/ppermute | solution.py:252
  19.2 5.0 %gate.1 = (bf16[80,4096]{1,0:T(8,128)(2,1)S(1)}, f32[80,3328]{1,0:T(8,128)S(1)}, bf16[80,3328]{1,0:T(8,128)(2,1)S(1)}, bf16[4096,1664]{1,0:T(8,128)(2,1)S(1)}) custom-call(bf16[8,5120]{1,0:T(8,128)(2,1)S(1)} %pack.1.refs_0_, bf16[8,5120]{1,0:T(8,128)(2,1)S(1)} %collective-permute-done.refs_1_, bf16[8,5120]{1,0:T(8,128)(2,1)S(1)} %collective-permute-done.1.refs_2_, ...), custom_call_target="tpu_custom_call" | custom-call | flops 10000000000 | bytes 56885248 | tf_op jit(solution)/shard_map/gate/pallas_call | solution.py:35
  24.4 7.2 %up.1 = (f32[80,3328]{1,0:T(8,128)S(1)}, bf16[80,3328]{1,0:T(8,128)(2,1)S(1)}, bf16[3328,1024]{1,0:T(8,128)(2,1)S(1)}) custom-call(bf16[80,4096]{1,0:T(8,128)(2,1)S(1)} %get-tuple-element.28.acts, bf16[4096,1664]{1,0:T(8,128)(2,1)S(1)} %get-tuple-element.29.first, bf16[4096,3328]{1,0:T(8,128)(2,1)} %codes.1, f32[128,3328]{1,0:T(8,128)S(1)} %copy-done.3, ...), custom_call_target="tpu_custom_call" | custom-call | flops 10000000000 | bytes 70516736 | tf_op jit(solution)/shard_map/up/pallas_call | solution.py:35
  32.1 1.5 %collective-permute-done.8.up_other = bf16[80,3328]{1,0:T(8,128)(2,1)S(1)} collective-permute-done((bf16[80,3328]{1,0:T(8,128)(2,1)S(1)}, bf16[80,3328]{1,0:T(8,128)(2,1)S(1)}, u32[]{:S(2)}, u32[]{:S(2)}) %collective-permute-start.8) | collective-permute-done | bytes 532512 | tf_op jit(solution)/shard_map/ppermute | solution.py:255
  33.7 6.3 %first.1 = (f32[32,2560]{1,0:T(8,128)S(1)}, bf16[32,2560]{1,0:T(8,128)(2,1)S(1)}, bf16[80,3328]{1,0:T(8,128)(2,1)S(1)}, bf16[3328,1024]{1,0:T(8,128)(2,1)S(1)}) custom-call(f32[80,3328]{1,0:T(8,128)S(1)} %get-tuple-element.26.gate, bf16[80,3328]{1,0:T(8,128)(2,1)S(1)} %collective-permute-done.7.gate_other, f32[80,3328]{1,0:T(8,128)S(1)} %get-tuple-element.30.up, ...), custom_call_target="tpu_custom_call" | custom-call | flops 1090519040 | bytes 38977536 | tf_op jit(solution)/shard_map/first/pallas_call | solution.py:35
  40.0 0.6 %collective-permute-start.9 = (bf16[32,2560]{1,0:T(8,128)(2,1)S(1)}, bf16[32,2560]{1,0:T(8,128)(2,1)S(1)}, u32[]{:S(2)}, u32[]{:S(2)}) collective-permute-start(bf16[32,2560]{1,0:T(8,128)(2,1)S(1)} %get-tuple-element.34), channel_id=1, source_target_pairs={{0,1},{1,0},{2,3},{3,2},{4,5},{5,4},{6,7},{7,6},{8,9},{9,8},{10,11... | collective-permute-start | bytes 491528 | tf_op jit(solution)/shard_map/ppermute | solution.py:249
  40.6 5.6 %second.1 = (f32[32,2560]{1,0:T(8,128)S(1)}, bf16[32,2560]{1,0:T(8,128)(2,1)S(1)}) custom-call(bf16[80,3328]{1,0:T(8,128)(2,1)S(1)} %get-tuple-element.39.hidden, bf16[3328,1024]{1,0:T(8,128)(2,1)S(1)} %get-tuple-element.40.codes, bf16[3328,4096]{1,0:T(8,128)(2,1)} %later.5, f32[104,4096]{1,0:T(8,128)S(1)} %copy-done.1), custom_call_target="tpu_custom_call" | custom-call | flops 1090519040 | bytes 36315136 | tf_op jit(solution)/shard_map/second/pallas_call | solution.py:35
  46.2 1.5 %collective-permute-start.13 = (bf16[32,2560]{1,0:T(8,128)(2,1)S(1)}, bf16[32,2560]{1,0:T(8,128)(2,1)S(1)}, u32[]{:S(2)}, u32[]{:S(2)}) collective-permute-start(bf16[32,2560]{1,0:T(8,128)(2,1)S(1)} %get-tuple-element.42), channel_id=1, source_target_pairs={{0,1},{1,0},{2,3},{3,2},{4,5},{5,4},{6,7},{7,6},{8,9},{9,8},{10,11... | collective-permute-start | bytes 491528 | tf_op jit(solution)/shard_map/ppermute | solution.py:249
  47.8 2.1 %collective-permute-start.10 = (bf16[8,2560]{1,0:T(8,128)(2,1)S(1)}, bf16[8,2560]{1,0:T(8,128)(2,1)S(1)}, u32[]{:S(2)}, u32[]{:S(2)}) collective-permute-start(bf16[8,2560]{1,0:T(8,128)(2,1)S(1)} %get-tuple-element.36), channel_id=1, source_target_pairs={{0,6},{1,7},{2,0},{3,1},{4,2},{5,3},{6,4},{7,5},{8,14},{9,15},{10,... | collective-permute-start | bytes 122888 | tf_op jit(solution)/shard_map/ppermute | solution.py:252
  49.9 0.6 %collective-permute-start.12 = (bf16[8,2560]{1,0:T(8,128)(2,1)S(1)}, bf16[8,2560]{1,0:T(8,128)(2,1)S(1)}, u32[]{:S(2)}, u32[]{:S(2)}) collective-permute-start(bf16[8,2560]{1,0:T(8,128)(2,1)S(1)} %get-tuple-element.38), channel_id=1, source_target_pairs={{0,2},{1,3},{2,4},{3,5},{4,6},{5,7},{6,0},{7,1},{8,10},{9,11},{10,... | collective-permute-start | bytes 122888 | tf_op jit(solution)/shard_map/ppermute | solution.py:252
  50.5 1.9 %collective-permute-done.13.refs_1_ = bf16[32,2560]{1,0:T(8,128)(2,1)S(1)} collective-permute-done((bf16[32,2560]{1,0:T(8,128)(2,1)S(1)}, bf16[32,2560]{1,0:T(8,128)(2,1)S(1)}, u32[]{:S(2)}, u32[]{:S(2)}) %collective-permute-start.13) | collective-permute-done | bytes 163872 | tf_op jit(solution)/shard_map/ppermute | solution.py:249
  52.5 2.1 %collective-permute-start.14 = (bf16[8,2560]{1,0:T(8,128)(2,1)S(1)}, bf16[8,2560]{1,0:T(8,128)(2,1)S(1)}, u32[]{:S(2)}, u32[]{:S(2)}) collective-permute-start(bf16[8,2560]{1,0:T(8,128)(2,1)S(1)} %get-tuple-element.44), channel_id=1, source_target_pairs={{0,6},{1,7},{2,0},{3,1},{4,2},{5,3},{6,4},{7,5},{8,14},{9,15},{10,... | collective-permute-start | bytes 122888 | tf_op jit(solution)/shard_map/ppermute | solution.py:252
  55.2 0.7 %collective-permute-done.11.refs_2_ = bf16[8,2560]{1,0:T(8,128)(2,1)S(1)} collective-permute-done((bf16[8,2560]{1,0:T(8,128)(2,1)S(1)}, bf16[8,2560]{1,0:T(8,128)(2,1)S(1)}, u32[]{:S(2)}, u32[]{:S(2)}) %collective-permute-start.11) | collective-permute-done | bytes 40992 | tf_op jit(solution)/shard_map/ppermute | solution.py:252
  55.9 0.6 collective-permute-done.14.refs_5_
  56.5 3.0 %collective-permute-done.15.refs_6_ = bf16[8,2560]{1,0:T(8,128)(2,1)S(1)} collective-permute-done((bf16[8,2560]{1,0:T(8,128)(2,1)S(1)}, bf16[8,2560]{1,0:T(8,128)(2,1)S(1)}, u32[]{:S(2)}, u32[]{:S(2)}) %collective-permute-start.15) | collective-permute-done | bytes 40992 | tf_op jit(solution)/shard_map/ppermute | solution.py:252
  59.5 1.3 %collective-permute-done.16.refs_7_ = bf16[8,2560]{1,0:T(8,128)(2,1)S(1)} collective-permute-done((bf16[8,2560]{1,0:T(8,128)(2,1)S(1)}, bf16[8,2560]{1,0:T(8,128)(2,1)S(1)}, u32[]{:S(2)}, u32[]{:S(2)}) %collective-permute-start.16) | collective-permute-done | bytes 40992 | tf_op jit(solution)/shard_map/ppermute | solution.py:252
  60.8 0.7 %last.1 = bf16[10,4096]{1,0:T(8,128)(2,1)} custom-call(f32[8,2560]{1,0:T(8,128)S(1)} %get-tuple-element.35.refs_0_, bf16[8,2560]{1,0:T(8,128)(2,1)S(1)} %collective-permute-done.10.refs_1_, bf16[8,2560]{1,0:T(8,128)(2,1)S(1)} %collective-permute-done.11.refs_2_, bf16[8,2560]{1,0:T(8,128)(2,1)S(1)} %collective-permute-done.12.refs_3_, ...), custom_call_target="tpu_custom_call" | custom-call | bytes 409600 | tf_op jit(solution)/shard_map/last/pallas_call | solution.py:35
  (28 shorter events, 2.5 us)
Async XLA Ops:
  0.0 19.2 %copy-start.2 = (f32[128,3328]{1,0:T(8,128)S(1)}, f32[128,3328]{1,0:T(8,128)}, u32[]{:S(2)}) copy-start(f32[128,3328]{1,0:T(8,128)} %refs_9_.1) | copy-start | bytes 5111812
  0.0 1.0 %copy-start.4 = (bf16[10,4096]{1,0:T(8,128)(2,1)S(1)}, bf16[10,4096]{1,0:T(8,128)(2,1)}, u32[]{:S(2)}) copy-start(bf16[10,4096]{1,0:T(8,128)(2,1)} %a_ref.1) | copy-start | bytes 245764
  1.0 18.2 %copy-start = (bf16[4096,3328]{1,0:T(8,128)(2,1)S(1)}, bf16[4096,3328]{1,0:T(8,128)(2,1)}, u32[]{:S(2)}) copy-start(bf16[4096,3328]{1,0:T(8,128)(2,1)} %refs_8_.1) | copy-start | bytes 81788928
  1.1 23.3 %copy-start.3 = (f32[128,3328]{1,0:T(8,128)S(1)}, f32[128,3328]{1,0:T(8,128)}, u32[]{:S(2)}) copy-start(f32[128,3328]{1,0:T(8,128)} %scales.3) | copy-start | bytes 5111812
  1.1 7.6 %collective-permute-start.3 = (bf16[8,5120]{1,0:T(8,128)(2,1)S(1)}, bf16[8,5120]{1,0:T(8,128)(2,1)S(1)}, u32[]{:S(2)}, u32[]{:S(2)}) collective-permute-start(bf16[8,5120]{1,0:T(8,128)(2,1)S(1)} %pack.1.refs_0_), channel_id=1, source_target_pairs={{0,1},{1,0},{2,3},{3,2},{4,5},{5,4},{6,7},{7,6},{8,9},{9,8},{10,11... | collective-permute-start | bytes 245768 | tf_op jit(solution)/shard_map/ppermute | solution.py:249
  4.1 6.5 %collective-permute-start.2 = (bf16[8,5120]{1,0:T(8,128)(2,1)S(1)}, bf16[8,5120]{1,0:T(8,128)(2,1)S(1)}, u32[]{:S(2)}, u32[]{:S(2)}) collective-permute-start(bf16[8,5120]{1,0:T(8,128)(2,1)S(1)} %pack.1.refs_0_), channel_id=1, source_target_pairs={{0,6},{1,7},{2,0},{3,1},{4,2},{5,3},{6,4},{7,5},{8,14},{9,15},{10,... | collective-permute-start | bytes 245768 | tf_op jit(solution)/shard_map/ppermute | solution.py:252
  7.7 6.8 %collective-permute-start = (bf16[8,5120]{1,0:T(8,128)(2,1)S(1)}, bf16[8,5120]{1,0:T(8,128)(2,1)S(1)}, u32[]{:S(2)}, u32[]{:S(2)}) collective-permute-start(bf16[8,5120]{1,0:T(8,128)(2,1)S(1)} %pack.1.refs_0_), channel_id=1, source_target_pairs={{0,2},{1,3},{2,4},{3,5},{4,6},{5,7},{6,0},{7,1},{8,10},{9,11},{10,... | collective-permute-start | bytes 245768 | tf_op jit(solution)/shard_map/ppermute | solution.py:252
  7.7 10.7 %collective-permute-start.1 = (bf16[8,5120]{1,0:T(8,128)(2,1)S(1)}, bf16[8,5120]{1,0:T(8,128)(2,1)S(1)}, u32[]{:S(2)}, u32[]{:S(2)}) collective-permute-start(bf16[8,5120]{1,0:T(8,128)(2,1)S(1)} %pack.1.refs_0_), channel_id=1, source_target_pairs={{0,4},{1,5},{2,6},{3,7},{4,0},{5,1},{6,2},{7,3},{8,12},{9,13},{10,... | collective-permute-start | bytes 245768 | tf_op jit(solution)/shard_map/ppermute | solution.py:252
  8.7 10.5 %collective-permute-start.5 = (bf16[8,5120]{1,0:T(8,128)(2,1)S(1)}, bf16[8,5120]{1,0:T(8,128)(2,1)S(1)}, u32[]{:S(2)}, u32[]{:S(2)}) collective-permute-start(bf16[8,5120]{1,0:T(8,128)(2,1)S(1)} %collective-permute-done.3.refs_4_), channel_id=1, source_target_pairs={{0,4},{1,5},{2,6},{3,7},{4,0},{5,1},{6,2},{7,3},{8,12},{9,13},{10,... | collective-permute-start | bytes 245768 | tf_op jit(solution)/shard_map/ppermute | solution.py:252
  10.6 8.6 %collective-permute-start.6 = (bf16[8,5120]{1,0:T(8,128)(2,1)S(1)}, bf16[8,5120]{1,0:T(8,128)(2,1)S(1)}, u32[]{:S(2)}, u32[]{:S(2)}) collective-permute-start(bf16[8,5120]{1,0:T(8,128)(2,1)S(1)} %collective-permute-done.2.refs_3_), channel_id=1, source_target_pairs={{0,1},{1,0},{2,3},{3,2},{4,5},{5,4},{6,7},{7,6},{8,9},{9,8},{10,11... | collective-permute-start | bytes 245768 | tf_op jit(solution)/shard_map/ppermute | solution.py:249
  14.4 4.8 %collective-permute-start.4 = (bf16[8,5120]{1,0:T(8,128)(2,1)S(1)}, bf16[8,5120]{1,0:T(8,128)(2,1)S(1)}, u32[]{:S(2)}, u32[]{:S(2)}) collective-permute-start(bf16[8,5120]{1,0:T(8,128)(2,1)S(1)} %collective-permute-done.refs_1_), channel_id=1, source_target_pairs={{0,1},{1,0},{2,3},{3,2},{4,5},{5,4},{6,7},{7,6},{8,9},{9,8},{10,11... | collective-permute-start | bytes 245768 | tf_op jit(solution)/shard_map/ppermute | solution.py:249
  24.3 7.8 %collective-permute-start.7 = (bf16[80,3328]{1,0:T(8,128)(2,1)S(1)}, bf16[80,3328]{1,0:T(8,128)(2,1)S(1)}, u32[]{:S(2)}, u32[]{:S(2)}) collective-permute-start(bf16[80,3328]{1,0:T(8,128)(2,1)S(1)} %get-tuple-element.27), channel_id=1, source_target_pairs={{0,8},{8,0},{1,9},{9,1},{2,10},{10,2},{3,11},{11,3},{4,12},{12,4},... | collective-permute-start | bytes 1597448 | tf_op jit(solution)/shard_map/ppermute | solution.py:255
  24.4 9.3 %copy-start.1 = (f32[104,4096]{1,0:T(8,128)S(1)}, f32[104,4096]{1,0:T(8,128)}, u32[]{:S(2)}) copy-start(f32[104,4096]{1,0:T(8,128)} %scales.5) | copy-start | bytes 5111812
  31.6 2.1 %collective-permute-start.8 = (bf16[80,3328]{1,0:T(8,128)(2,1)S(1)}, bf16[80,3328]{1,0:T(8,128)(2,1)S(1)}, u32[]{:S(2)}, u32[]{:S(2)}) collective-permute-start(bf16[80,3328]{1,0:T(8,128)(2,1)S(1)} %get-tuple-element.31), channel_id=1, source_target_pairs={{0,8},{8,0},{1,9},{9,1},{2,10},{10,2},{3,11},{11,3},{4,12},{12,4},... | collective-permute-start | bytes 1597448 | tf_op jit(solution)/shard_map/ppermute | solution.py:255
  40.0 7.8 %collective-permute-start.9 = (bf16[32,2560]{1,0:T(8,128)(2,1)S(1)}, bf16[32,2560]{1,0:T(8,128)(2,1)S(1)}, u32[]{:S(2)}, u32[]{:S(2)}) collective-permute-start(bf16[32,2560]{1,0:T(8,128)(2,1)S(1)} %get-tuple-element.34), channel_id=1, source_target_pairs={{0,1},{1,0},{2,3},{3,2},{4,5},{5,4},{6,7},{7,6},{8,9},{9,8},{10,11... | collective-permute-start | bytes 491528 | tf_op jit(solution)/shard_map/ppermute | solution.py:249
  46.2 6.3 %collective-permute-start.13 = (bf16[32,2560]{1,0:T(8,128)(2,1)S(1)}, bf16[32,2560]{1,0:T(8,128)(2,1)S(1)}, u32[]{:S(2)}, u32[]{:S(2)}) collective-permute-start(bf16[32,2560]{1,0:T(8,128)(2,1)S(1)} %get-tuple-element.42), channel_id=1, source_target_pairs={{0,1},{1,0},{2,3},{3,2},{4,5},{5,4},{6,7},{7,6},{8,9},{9,8},{10,11... | collective-permute-start | bytes 491528 | tf_op jit(solution)/shard_map/ppermute | solution.py:249
  47.8 7.2 %collective-permute-start.10 = (bf16[8,2560]{1,0:T(8,128)(2,1)S(1)}, bf16[8,2560]{1,0:T(8,128)(2,1)S(1)}, u32[]{:S(2)}, u32[]{:S(2)}) collective-permute-start(bf16[8,2560]{1,0:T(8,128)(2,1)S(1)} %get-tuple-element.36), channel_id=1, source_target_pairs={{0,6},{1,7},{2,0},{3,1},{4,2},{5,3},{6,4},{7,5},{8,14},{9,15},{10,... | collective-permute-start | bytes 122888 | tf_op jit(solution)/shard_map/ppermute | solution.py:252
  49.9 6.0 %collective-permute-start.11 = (bf16[8,2560]{1,0:T(8,128)(2,1)S(1)}, bf16[8,2560]{1,0:T(8,128)(2,1)S(1)}, u32[]{:S(2)}, u32[]{:S(2)}) collective-permute-start(bf16[8,2560]{1,0:T(8,128)(2,1)S(1)} %get-tuple-element.37), channel_id=1, source_target_pairs={{0,4},{1,5},{2,6},{3,7},{4,0},{5,1},{6,2},{7,3},{8,12},{9,13},{10,... | collective-permute-start | bytes 122888 | tf_op jit(solution)/shard_map/ppermute | solution.py:252
  49.9 6.0 %collective-permute-start.12 = (bf16[8,2560]{1,0:T(8,128)(2,1)S(1)}, bf16[8,2560]{1,0:T(8,128)(2,1)S(1)}, u32[]{:S(2)}, u32[]{:S(2)}) collective-permute-start(bf16[8,2560]{1,0:T(8,128)(2,1)S(1)} %get-tuple-element.38), channel_id=1, source_target_pairs={{0,2},{1,3},{2,4},{3,5},{4,6},{5,7},{6,0},{7,1},{8,10},{9,11},{10,... | collective-permute-start | bytes 122888 | tf_op jit(solution)/shard_map/ppermute | solution.py:252
  52.5 4.1 %collective-permute-start.14 = (bf16[8,2560]{1,0:T(8,128)(2,1)S(1)}, bf16[8,2560]{1,0:T(8,128)(2,1)S(1)}, u32[]{:S(2)}, u32[]{:S(2)}) collective-permute-start(bf16[8,2560]{1,0:T(8,128)(2,1)S(1)} %get-tuple-element.44), channel_id=1, source_target_pairs={{0,6},{1,7},{2,0},{3,1},{4,2},{5,3},{6,4},{7,5},{8,14},{9,15},{10,... | collective-permute-start | bytes 122888 | tf_op jit(solution)/shard_map/ppermute | solution.py:252
  54.6 4.9 %collective-permute-start.15 = (bf16[8,2560]{1,0:T(8,128)(2,1)S(1)}, bf16[8,2560]{1,0:T(8,128)(2,1)S(1)}, u32[]{:S(2)}, u32[]{:S(2)}) collective-permute-start(bf16[8,2560]{1,0:T(8,128)(2,1)S(1)} %get-tuple-element.45), channel_id=1, source_target_pairs={{0,4},{1,5},{2,6},{3,7},{4,0},{5,1},{6,2},{7,3},{8,12},{9,13},{10,... | collective-permute-start | bytes 122888 | tf_op jit(solution)/shard_map/ppermute | solution.py:252
  55.0 5.8 %collective-permute-start.16 = (bf16[8,2560]{1,0:T(8,128)(2,1)S(1)}, bf16[8,2560]{1,0:T(8,128)(2,1)S(1)}, u32[]{:S(2)}, u32[]{:S(2)}) collective-permute-start(bf16[8,2560]{1,0:T(8,128)(2,1)S(1)} %get-tuple-element.46), channel_id=1, source_target_pairs={{0,2},{1,3},{2,4},{3,5},{4,6},{5,7},{6,0},{7,1},{8,10},{9,11},{10,... | collective-permute-start | bytes 122888 | tf_op jit(solution)/shard_map/ppermute | solution.py:252

commit v8 on v7

--- a/solution.py
+++ b/solution.py
@@ -186,11 +186,11 @@
         hidden[:, cols] = (jax.nn.silu(g) * u).astype(BF16)
     copies.start()
     for k in range(2):
-        terms[:, k * part : (k + 1) * part] = project(hidden, codes, k * part, scales, k * part, part)
+        terms[:, k * part : (k + 1) * part] = project(hidden, codes, k * part, scales, k * part, part, dequant_short)
         copies.start()
     for k in range(2):
         copies.wait(k)
-        terms[:, size + k * part : size + (k + 1) * part] = project(hidden, tail, k * part, scales, size + k * part, part)
+        terms[:, size + k * part : size + (k + 1) * part] = project(hidden, tail, k * part, scales, size + k * part, part, dequant_short)
     emit(terms, blocks, rest, outs)
     copies.wait(2)
 
@@ -201,11 +201,11 @@
     part = size // 2
     copies = Copies(*[(later, 3 * size + k * part, part, tail, k * part, done.at[k]) for k in range(2)])
     for k in range(2):
-        terms[:, k * part : (k + 1) * part] = project(hidden, codes, k * part, scales, 2 * size + k * part, part)
+        terms[:, k * part : (k + 1) * part] = project(hidden, codes, k * part, scales, 2 * size + k * part, part, dequant_short)
         copies.start()
     for k in range(2):
         copies.wait(k)
-        terms[:, size + k * part : size + (k + 1) * part] = project(hidden, tail, k * part, scales, 3 * size + k * part, part)
+        terms[:, size + k * part : size + (k + 1) * part] = project(hidden, tail, k * part, scales, 3 * size + k * part, part, dequant_short)
     emit(terms, blocks, rest, outs)
 
 

time: 61.6 us -> 60.6 us (0.984)
  Pallas kernels: 24.9 us -> 23.9 us
    pallas_call x8, Pallas kernels: 24.9 us -> 23.9 us  [call(): pl.pallas_call(body, in_specs=[pl.BlockSpec(memory_space=pltpu.HBM if i i...]
  transfers between devices with their start and end apart: 17 -> 17, of which waited for: 9 -> 9; matrix products, arithmetic and copies ran while one was open for 0% -> 0% of each run, Pallas kernels for 21% -> 20%
where the time goes in v8:
time: 60.6 us; the launch traced here: 60.5 us
  Pallas kernels  23.9 us (39%)
  starting transfers between devices  18.9 us (31%)
  waiting for transfers between devices  16.5 us (27%)
  local copies, waits for them, and re-layouts  1.05 us (2%)
    pallas_call x8, Pallas kernels, call(): pl.pallas_call(body, in_specs=[pl.BlockSpec(memory_space=pltpu.HBM if i i...  23.9 us
    ppermute x10, waiting for transfers between devices, along(): lax.ppermute(x, 'hidden', [(h, (h + 2 * s) % peers) for h in range(peers)])  13.1 us
    ppermute x10, starting transfers between devices, along(): lax.ppermute(x, 'hidden', [(h, (h + 2 * s) % peers) for h in range(peers)])  12 us
    ppermute x5, starting transfers between devices, flip(): return lax.ppermute(x, 'hidden', [(h, h ^ 1) for h in range(peers)])  6.24 us
    ppermute x5, waiting for transfers between devices, flip(): return lax.ppermute(x, 'hidden', [(h, h ^ 1) for h in range(peers)])  1.91 us
    ppermute x2, waiting for transfers between devices, swap(): return lax.ppermute(x, 'width', [(0, 1), (1, 0)])  1.55 us
  transfers between devices with their start and end apart: 17, of which 9 were waited for; matrix products, arithmetic and copies ran while one was open for 0% of the time, Pallas kernels for 20%

profile of v8, /device:TPU:0, one launch (start us, length us, event | category | flops | bytes accessed | tf_op | source)
XLA Modules:
  0.0 60.5 jit_solution(16958421780900099306)
XLA Ops:
  0.0 1.0 %copy-done.4 = bf16[10,4096]{1,0:T(8,128)(2,1)S(1)} copy-done((bf16[10,4096]{1,0:T(8,128)(2,1)S(1)}, bf16[10,4096]{1,0:T(8,128)(2,1)}, u32[]{:S(2)}) %copy-start.4) | copy-done | bytes 81944
  1.1 3.0 %collective-permute-start.3 = (bf16[8,5120]{1,0:T(8,128)(2,1)S(1)}, bf16[8,5120]{1,0:T(8,128)(2,1)S(1)}, u32[]{:S(2)}, u32[]{:S(2)}) collective-permute-start(bf16[8,5120]{1,0:T(8,128)(2,1)S(1)} %pack.1.refs_0_), channel_id=1, source_target_pairs={{0,1},{1,0},{2,3},{3,2},{4,5},{5,4},{6,7},{7,6},{8,9},{9,8},{10,11... | collective-permute-start | bytes 245768 | tf_op jit(solution)/shard_map/ppermute | solution.py:249
  4.1 3.6 %collective-permute-start.2 = (bf16[8,5120]{1,0:T(8,128)(2,1)S(1)}, bf16[8,5120]{1,0:T(8,128)(2,1)S(1)}, u32[]{:S(2)}, u32[]{:S(2)}) collective-permute-start(bf16[8,5120]{1,0:T(8,128)(2,1)S(1)} %pack.1.refs_0_), channel_id=1, source_target_pairs={{0,6},{1,7},{2,0},{3,1},{4,2},{5,3},{6,4},{7,5},{8,14},{9,15},{10,... | collective-permute-start | bytes 245768 | tf_op jit(solution)/shard_map/ppermute | solution.py:252
  7.7 1.0 %collective-permute-start.1 = (bf16[8,5120]{1,0:T(8,128)(2,1)S(1)}, bf16[8,5120]{1,0:T(8,128)(2,1)S(1)}, u32[]{:S(2)}, u32[]{:S(2)}) collective-permute-start(bf16[8,5120]{1,0:T(8,128)(2,1)S(1)} %pack.1.refs_0_), channel_id=1, source_target_pairs={{0,4},{1,5},{2,6},{3,7},{4,0},{5,1},{6,2},{7,3},{8,12},{9,13},{10,... | collective-permute-start | bytes 245768 | tf_op jit(solution)/shard_map/ppermute | solution.py:252
  8.7 1.9 %collective-permute-start.5 = (bf16[8,5120]{1,0:T(8,128)(2,1)S(1)}, bf16[8,5120]{1,0:T(8,128)(2,1)S(1)}, u32[]{:S(2)}, u32[]{:S(2)}) collective-permute-start(bf16[8,5120]{1,0:T(8,128)(2,1)S(1)} %collective-permute-done.3.refs_4_), channel_id=1, source_target_pairs={{0,4},{1,5},{2,6},{3,7},{4,0},{5,1},{6,2},{7,3},{8,12},{9,13},{10,... | collective-permute-start | bytes 245768 | tf_op jit(solution)/shard_map/ppermute | solution.py:252
  11.1 3.3 %collective-permute-done.refs_1_ = bf16[8,5120]{1,0:T(8,128)(2,1)S(1)} collective-permute-done((bf16[8,5120]{1,0:T(8,128)(2,1)S(1)}, bf16[8,5120]{1,0:T(8,128)(2,1)S(1)}, u32[]{:S(2)}, u32[]{:S(2)}) %collective-permute-start) | collective-permute-done | bytes 81952 | tf_op jit(solution)/shard_map/ppermute | solution.py:252
  15.0 3.4 %collective-permute-done.1.refs_2_ = bf16[8,5120]{1,0:T(8,128)(2,1)S(1)} collective-permute-done((bf16[8,5120]{1,0:T(8,128)(2,1)S(1)}, bf16[8,5120]{1,0:T(8,128)(2,1)S(1)}, u32[]{:S(2)}, u32[]{:S(2)}) %collective-permute-start.1) | collective-permute-done | bytes 81952 | tf_op jit(solution)/shard_map/ppermute | solution.py:252
  18.3 0.9 %collective-permute-done.5.refs_6_ = bf16[8,5120]{1,0:T(8,128)(2,1)S(1)} collective-permute-done((bf16[8,5120]{1,0:T(8,128)(2,1)S(1)}, bf16[8,5120]{1,0:T(8,128)(2,1)S(1)}, u32[]{:S(2)}, u32[]{:S(2)}) %collective-permute-start.5) | collective-permute-done | bytes 81952 | tf_op jit(solution)/shard_map/ppermute | solution.py:252
  19.2 5.0 %gate.1 = (bf16[80,4096]{1,0:T(8,128)(2,1)S(1)}, f32[80,3328]{1,0:T(8,128)S(1)}, bf16[80,3328]{1,0:T(8,128)(2,1)S(1)}, bf16[4096,1664]{1,0:T(8,128)(2,1)S(1)}) custom-call(bf16[8,5120]{1,0:T(8,128)(2,1)S(1)} %pack.1.refs_0_, bf16[8,5120]{1,0:T(8,128)(2,1)S(1)} %collective-permute-done.refs_1_, bf16[8,5120]{1,0:T(8,128)(2,1)S(1)} %collective-permute-done.1.refs_2_, ...), custom_call_target="tpu_custom_call" | custom-call | flops 10000000000 | bytes 56885248 | tf_op jit(solution)/shard_map/gate/pallas_call | solution.py:35
  24.4 7.2 %up.1 = (f32[80,3328]{1,0:T(8,128)S(1)}, bf16[80,3328]{1,0:T(8,128)(2,1)S(1)}, bf16[3328,1024]{1,0:T(8,128)(2,1)S(1)}) custom-call(bf16[80,4096]{1,0:T(8,128)(2,1)S(1)} %get-tuple-element.28.acts, bf16[4096,1664]{1,0:T(8,128)(2,1)S(1)} %get-tuple-element.29.first, bf16[4096,3328]{1,0:T(8,128)(2,1)} %codes.1, f32[128,3328]{1,0:T(8,128)S(1)} %copy-done.3, ...), custom_call_target="tpu_custom_call" | custom-call | flops 10000000000 | bytes 70516736 | tf_op jit(solution)/shard_map/up/pallas_call | solution.py:35
  32.1 1.5 %collective-permute-done.8.up_other = bf16[80,3328]{1,0:T(8,128)(2,1)S(1)} collective-permute-done((bf16[80,3328]{1,0:T(8,128)(2,1)S(1)}, bf16[80,3328]{1,0:T(8,128)(2,1)S(1)}, u32[]{:S(2)}, u32[]{:S(2)}) %collective-permute-start.8) | collective-permute-done | bytes 532512 | tf_op jit(solution)/shard_map/ppermute | solution.py:255
  33.7 5.9 %first.1 = (f32[32,2560]{1,0:T(8,128)S(1)}, bf16[32,2560]{1,0:T(8,128)(2,1)S(1)}, bf16[80,3328]{1,0:T(8,128)(2,1)S(1)}, bf16[3328,1024]{1,0:T(8,128)(2,1)S(1)}) custom-call(f32[80,3328]{1,0:T(8,128)S(1)} %get-tuple-element.26.gate, bf16[80,3328]{1,0:T(8,128)(2,1)S(1)} %collective-permute-done.7.gate_other, f32[80,3328]{1,0:T(8,128)S(1)} %get-tuple-element.30.up, ...), custom_call_target="tpu_custom_call" | custom-call | flops 1090519040 | bytes 38977536 | tf_op jit(solution)/shard_map/first/pallas_call | solution.py:35
  39.5 0.6 %collective-permute-start.9 = (bf16[32,2560]{1,0:T(8,128)(2,1)S(1)}, bf16[32,2560]{1,0:T(8,128)(2,1)S(1)}, u32[]{:S(2)}, u32[]{:S(2)}) collective-permute-start(bf16[32,2560]{1,0:T(8,128)(2,1)S(1)} %get-tuple-element.34), channel_id=1, source_target_pairs={{0,1},{1,0},{2,3},{3,2},{4,5},{5,4},{6,7},{7,6},{8,9},{9,8},{10,11... | collective-permute-start | bytes 491528 | tf_op jit(solution)/shard_map/ppermute | solution.py:249
  40.2 5.0 %second.1 = (f32[32,2560]{1,0:T(8,128)S(1)}, bf16[32,2560]{1,0:T(8,128)(2,1)S(1)}) custom-call(bf16[80,3328]{1,0:T(8,128)(2,1)S(1)} %get-tuple-element.39.hidden, bf16[3328,1024]{1,0:T(8,128)(2,1)S(1)} %get-tuple-element.40.codes, bf16[3328,4096]{1,0:T(8,128)(2,1)} %later.5, f32[104,4096]{1,0:T(8,128)S(1)} %copy-done.1), custom_call_target="tpu_custom_call" | custom-call | flops 1090519040 | bytes 36315136 | tf_op jit(solution)/shard_map/second/pallas_call | solution.py:35
  45.2 1.5 %collective-permute-start.13 = (bf16[32,2560]{1,0:T(8,128)(2,1)S(1)}, bf16[32,2560]{1,0:T(8,128)(2,1)S(1)}, u32[]{:S(2)}, u32[]{:S(2)}) collective-permute-start(bf16[32,2560]{1,0:T(8,128)(2,1)S(1)} %get-tuple-element.42), channel_id=1, source_target_pairs={{0,1},{1,0},{2,3},{3,2},{4,5},{5,4},{6,7},{7,6},{8,9},{9,8},{10,11... | collective-permute-start | bytes 491528 | tf_op jit(solution)/shard_map/ppermute | solution.py:249
  46.8 2.1 %collective-permute-start.10 = (bf16[8,2560]{1,0:T(8,128)(2,1)S(1)}, bf16[8,2560]{1,0:T(8,128)(2,1)S(1)}, u32[]{:S(2)}, u32[]{:S(2)}) collective-permute-start(bf16[8,2560]{1,0:T(8,128)(2,1)S(1)} %get-tuple-element.36), channel_id=1, source_target_pairs={{0,6},{1,7},{2,0},{3,1},{4,2},{5,3},{6,4},{7,5},{8,14},{9,15},{10,... | collective-permute-start | bytes 122888 | tf_op jit(solution)/shard_map/ppermute | solution.py:252
  48.9 0.6 %collective-permute-start.12 = (bf16[8,2560]{1,0:T(8,128)(2,1)S(1)}, bf16[8,2560]{1,0:T(8,128)(2,1)S(1)}, u32[]{:S(2)}, u32[]{:S(2)}) collective-permute-start(bf16[8,2560]{1,0:T(8,128)(2,1)S(1)} %get-tuple-element.38), channel_id=1, source_target_pairs={{0,2},{1,3},{2,4},{3,5},{4,6},{5,7},{6,0},{7,1},{8,10},{9,11},{10,... | collective-permute-start | bytes 122888 | tf_op jit(solution)/shard_map/ppermute | solution.py:252
  49.5 1.9 %collective-permute-done.13.refs_1_ = bf16[32,2560]{1,0:T(8,128)(2,1)S(1)} collective-permute-done((bf16[32,2560]{1,0:T(8,128)(2,1)S(1)}, bf16[32,2560]{1,0:T(8,128)(2,1)S(1)}, u32[]{:S(2)}, u32[]{:S(2)}) %collective-permute-start.13) | collective-permute-done | bytes 163872 | tf_op jit(solution)/shard_map/ppermute | solution.py:249
  51.5 2.1 %collective-permute-start.14 = (bf16[8,2560]{1,0:T(8,128)(2,1)S(1)}, bf16[8,2560]{1,0:T(8,128)(2,1)S(1)}, u32[]{:S(2)}, u32[]{:S(2)}) collective-permute-start(bf16[8,2560]{1,0:T(8,128)(2,1)S(1)} %get-tuple-element.44), channel_id=1, source_target_pairs={{0,6},{1,7},{2,0},{3,1},{4,2},{5,3},{6,4},{7,5},{8,14},{9,15},{10,... | collective-permute-start | bytes 122888 | tf_op jit(solution)/shard_map/ppermute | solution.py:252
  54.2 0.7 %collective-permute-done.11.refs_2_ = bf16[8,2560]{1,0:T(8,128)(2,1)S(1)} collective-permute-done((bf16[8,2560]{1,0:T(8,128)(2,1)S(1)}, bf16[8,2560]{1,0:T(8,128)(2,1)S(1)}, u32[]{:S(2)}, u32[]{:S(2)}) %collective-permute-start.11) | collective-permute-done | bytes 40992 | tf_op jit(solution)/shard_map/ppermute | solution.py:252
  54.9 0.6 collective-permute-done.14.refs_5_
  55.5 3.0 %collective-permute-done.15.refs_6_ = bf16[8,2560]{1,0:T(8,128)(2,1)S(1)} collective-permute-done((bf16[8,2560]{1,0:T(8,128)(2,1)S(1)}, bf16[8,2560]{1,0:T(8,128)(2,1)S(1)}, u32[]{:S(2)}, u32[]{:S(2)}) %collective-permute-start.15) | collective-permute-done | bytes 40992 | tf_op jit(solution)/shard_map/ppermute | solution.py:252
  58.5 1.3 %collective-permute-done.16.refs_7_ = bf16[8,2560]{1,0:T(8,128)(2,1)S(1)} collective-permute-done((bf16[8,2560]{1,0:T(8,128)(2,1)S(1)}, bf16[8,2560]{1,0:T(8,128)(2,1)S(1)}, u32[]{:S(2)}, u32[]{:S(2)}) %collective-permute-start.16) | collective-permute-done | bytes 40992 | tf_op jit(solution)/shard_map/ppermute | solution.py:252
  59.8 0.7 %last.1 = bf16[10,4096]{1,0:T(8,128)(2,1)} custom-call(f32[8,2560]{1,0:T(8,128)S(1)} %get-tuple-element.35.refs_0_, bf16[8,2560]{1,0:T(8,128)(2,1)S(1)} %collective-permute-done.10.refs_1_, bf16[8,2560]{1,0:T(8,128)(2,1)S(1)} %collective-permute-done.11.refs_2_, bf16[8,2560]{1,0:T(8,128)(2,1)S(1)} %collective-permute-done.12.refs_3_, ...), custom_call_target="tpu_custom_call" | custom-call | bytes 409600 | tf_op jit(solution)/shard_map/last/pallas_call | solution.py:35
  (28 shorter events, 2.5 us)
Async XLA Ops:
  0.0 19.2 %copy-start.2 = (f32[128,3328]{1,0:T(8,128)S(1)}, f32[128,3328]{1,0:T(8,128)}, u32[]{:S(2)}) copy-start(f32[128,3328]{1,0:T(8,128)} %refs_9_.1) | copy-start | bytes 5111812
  0.0 1.0 %copy-start.4 = (bf16[10,4096]{1,0:T(8,128)(2,1)S(1)}, bf16[10,4096]{1,0:T(8,128)(2,1)}, u32[]{:S(2)}) copy-start(bf16[10,4096]{1,0:T(8,128)(2,1)} %a_ref.1) | copy-start | bytes 245764
  1.0 18.2 %copy-start = (bf16[4096,3328]{1,0:T(8,128)(2,1)S(1)}, bf16[4096,3328]{1,0:T(8,128)(2,1)}, u32[]{:S(2)}) copy-start(bf16[4096,3328]{1,0:T(8,128)(2,1)} %refs_8_.1) | copy-start | bytes 81788928
  1.1 23.3 %copy-start.3 = (f32[128,3328]{1,0:T(8,128)S(1)}, f32[128,3328]{1,0:T(8,128)}, u32[]{:S(2)}) copy-start(f32[128,3328]{1,0:T(8,128)} %scales.3) | copy-start | bytes 5111812
  1.1 7.6 %collective-permute-start.3 = (bf16[8,5120]{1,0:T(8,128)(2,1)S(1)}, bf16[8,5120]{1,0:T(8,128)(2,1)S(1)}, u32[]{:S(2)}, u32[]{:S(2)}) collective-permute-start(bf16[8,5120]{1,0:T(8,128)(2,1)S(1)} %pack.1.refs_0_), channel_id=1, source_target_pairs={{0,1},{1,0},{2,3},{3,2},{4,5},{5,4},{6,7},{7,6},{8,9},{9,8},{10,11... | collective-permute-start | bytes 245768 | tf_op jit(solution)/shard_map/ppermute | solution.py:249
  4.1 6.5 %collective-permute-start.2 = (bf16[8,5120]{1,0:T(8,128)(2,1)S(1)}, bf16[8,5120]{1,0:T(8,128)(2,1)S(1)}, u32[]{:S(2)}, u32[]{:S(2)}) collective-permute-start(bf16[8,5120]{1,0:T(8,128)(2,1)S(1)} %pack.1.refs_0_), channel_id=1, source_target_pairs={{0,6},{1,7},{2,0},{3,1},{4,2},{5,3},{6,4},{7,5},{8,14},{9,15},{10,... | collective-permute-start | bytes 245768 | tf_op jit(solution)/shard_map/ppermute | solution.py:252
  7.7 6.8 %collective-permute-start = (bf16[8,5120]{1,0:T(8,128)(2,1)S(1)}, bf16[8,5120]{1,0:T(8,128)(2,1)S(1)}, u32[]{:S(2)}, u32[]{:S(2)}) collective-permute-start(bf16[8,5120]{1,0:T(8,128)(2,1)S(1)} %pack.1.refs_0_), channel_id=1, source_target_pairs={{0,2},{1,3},{2,4},{3,5},{4,6},{5,7},{6,0},{7,1},{8,10},{9,11},{10,... | collective-permute-start | bytes 245768 | tf_op jit(solution)/shard_map/ppermute | solution.py:252
  7.7 10.7 %collective-permute-start.1 = (bf16[8,5120]{1,0:T(8,128)(2,1)S(1)}, bf16[8,5120]{1,0:T(8,128)(2,1)S(1)}, u32[]{:S(2)}, u32[]{:S(2)}) collective-permute-start(bf16[8,5120]{1,0:T(8,128)(2,1)S(1)} %pack.1.refs_0_), channel_id=1, source_target_pairs={{0,4},{1,5},{2,6},{3,7},{4,0},{5,1},{6,2},{7,3},{8,12},{9,13},{10,... | collective-permute-start | bytes 245768 | tf_op jit(solution)/shard_map/ppermute | solution.py:252
  8.7 10.5 %collective-permute-start.5 = (bf16[8,5120]{1,0:T(8,128)(2,1)S(1)}, bf16[8,5120]{1,0:T(8,128)(2,1)S(1)}, u32[]{:S(2)}, u32[]{:S(2)}) collective-permute-start(bf16[8,5120]{1,0:T(8,128)(2,1)S(1)} %collective-permute-done.3.refs_4_), channel_id=1, source_target_pairs={{0,4},{1,5},{2,6},{3,7},{4,0},{5,1},{6,2},{7,3},{8,12},{9,13},{10,... | collective-permute-start | bytes 245768 | tf_op jit(solution)/shard_map/ppermute | solution.py:252
  10.6 8.6 %collective-permute-start.6 = (bf16[8,5120]{1,0:T(8,128)(2,1)S(1)}, bf16[8,5120]{1,0:T(8,128)(2,1)S(1)}, u32[]{:S(2)}, u32[]{:S(2)}) collective-permute-start(bf16[8,5120]{1,0:T(8,128)(2,1)S(1)} %collective-permute-done.2.refs_3_), channel_id=1, source_target_pairs={{0,1},{1,0},{2,3},{3,2},{4,5},{5,4},{6,7},{7,6},{8,9},{9,8},{10,11... | collective-permute-start | bytes 245768 | tf_op jit(solution)/shard_map/ppermute | solution.py:249
  14.4 4.8 %collective-permute-start.4 = (bf16[8,5120]{1,0:T(8,128)(2,1)S(1)}, bf16[8,5120]{1,0:T(8,128)(2,1)S(1)}, u32[]{:S(2)}, u32[]{:S(2)}) collective-permute-start(bf16[8,5120]{1,0:T(8,128)(2,1)S(1)} %collective-permute-done.refs_1_), channel_id=1, source_target_pairs={{0,1},{1,0},{2,3},{3,2},{4,5},{5,4},{6,7},{7,6},{8,9},{9,8},{10,11... | collective-permute-start | bytes 245768 | tf_op jit(solution)/shard_map/ppermute | solution.py:249
  24.3 7.8 %collective-permute-start.7 = (bf16[80,3328]{1,0:T(8,128)(2,1)S(1)}, bf16[80,3328]{1,0:T(8,128)(2,1)S(1)}, u32[]{:S(2)}, u32[]{:S(2)}) collective-permute-start(bf16[80,3328]{1,0:T(8,128)(2,1)S(1)} %get-tuple-element.27), channel_id=1, source_target_pairs={{0,8},{8,0},{1,9},{9,1},{2,10},{10,2},{3,11},{11,3},{4,12},{12,4},... | collective-permute-start | bytes 1597448 | tf_op jit(solution)/shard_map/ppermute | solution.py:255
  24.4 9.3 %copy-start.1 = (f32[104,4096]{1,0:T(8,128)S(1)}, f32[104,4096]{1,0:T(8,128)}, u32[]{:S(2)}) copy-start(f32[104,4096]{1,0:T(8,128)} %scales.5) | copy-start | bytes 5111812
  31.6 2.1 %collective-permute-start.8 = (bf16[80,3328]{1,0:T(8,128)(2,1)S(1)}, bf16[80,3328]{1,0:T(8,128)(2,1)S(1)}, u32[]{:S(2)}, u32[]{:S(2)}) collective-permute-start(bf16[80,3328]{1,0:T(8,128)(2,1)S(1)} %get-tuple-element.31), channel_id=1, source_target_pairs={{0,8},{8,0},{1,9},{9,1},{2,10},{10,2},{3,11},{11,3},{4,12},{12,4},... | collective-permute-start | bytes 1597448 | tf_op jit(solution)/shard_map/ppermute | solution.py:255
  39.5 7.2 %collective-permute-start.9 = (bf16[32,2560]{1,0:T(8,128)(2,1)S(1)}, bf16[32,2560]{1,0:T(8,128)(2,1)S(1)}, u32[]{:S(2)}, u32[]{:S(2)}) collective-permute-start(bf16[32,2560]{1,0:T(8,128)(2,1)S(1)} %get-tuple-element.34), channel_id=1, source_target_pairs={{0,1},{1,0},{2,3},{3,2},{4,5},{5,4},{6,7},{7,6},{8,9},{9,8},{10,11... | collective-permute-start | bytes 491528 | tf_op jit(solution)/shard_map/ppermute | solution.py:249
  45.2 6.3 %collective-permute-start.13 = (bf16[32,2560]{1,0:T(8,128)(2,1)S(1)}, bf16[32,2560]{1,0:T(8,128)(2,1)S(1)}, u32[]{:S(2)}, u32[]{:S(2)}) collective-permute-start(bf16[32,2560]{1,0:T(8,128)(2,1)S(1)} %get-tuple-element.42), channel_id=1, source_target_pairs={{0,1},{1,0},{2,3},{3,2},{4,5},{5,4},{6,7},{7,6},{8,9},{9,8},{10,11... | collective-permute-start | bytes 491528 | tf_op jit(solution)/shard_map/ppermute | solution.py:249
  46.8 7.2 %collective-permute-start.10 = (bf16[8,2560]{1,0:T(8,128)(2,1)S(1)}, bf16[8,2560]{1,0:T(8,128)(2,1)S(1)}, u32[]{:S(2)}, u32[]{:S(2)}) collective-permute-start(bf16[8,2560]{1,0:T(8,128)(2,1)S(1)} %get-tuple-element.36), channel_id=1, source_target_pairs={{0,6},{1,7},{2,0},{3,1},{4,2},{5,3},{6,4},{7,5},{8,14},{9,15},{10,... | collective-permute-start | bytes 122888 | tf_op jit(solution)/shard_map/ppermute | solution.py:252
  48.9 6.0 %collective-permute-start.11 = (bf16[8,2560]{1,0:T(8,128)(2,1)S(1)}, bf16[8,2560]{1,0:T(8,128)(2,1)S(1)}, u32[]{:S(2)}, u32[]{:S(2)}) collective-permute-start(bf16[8,2560]{1,0:T(8,128)(2,1)S(1)} %get-tuple-element.37), channel_id=1, source_target_pairs={{0,4},{1,5},{2,6},{3,7},{4,0},{5,1},{6,2},{7,3},{8,12},{9,13},{10,... | collective-permute-start | bytes 122888 | tf_op jit(solution)/shard_map/ppermute | solution.py:252
  48.9 6.0 %collective-permute-start.12 = (bf16[8,2560]{1,0:T(8,128)(2,1)S(1)}, bf16[8,2560]{1,0:T(8,128)(2,1)S(1)}, u32[]{:S(2)}, u32[]{:S(2)}) collective-permute-start(bf16[8,2560]{1,0:T(8,128)(2,1)S(1)} %get-tuple-element.38), channel_id=1, source_target_pairs={{0,2},{1,3},{2,4},{3,5},{4,6},{5,7},{6,0},{7,1},{8,10},{9,11},{10,... | collective-permute-start | bytes 122888 | tf_op jit(solution)/shard_map/ppermute | solution.py:252
  51.5 4.1 %collective-permute-start.14 = (bf16[8,2560]{1,0:T(8,128)(2,1)S(1)}, bf16[8,2560]{1,0:T(8,128)(2,1)S(1)}, u32[]{:S(2)}, u32[]{:S(2)}) collective-permute-start(bf16[8,2560]{1,0:T(8,128)(2,1)S(1)} %get-tuple-element.44), channel_id=1, source_target_pairs={{0,6},{1,7},{2,0},{3,1},{4,2},{5,3},{6,4},{7,5},{8,14},{9,15},{10,... | collective-permute-start | bytes 122888 | tf_op jit(solution)/shard_map/ppermute | solution.py:252
  53.6 4.9 %collective-permute-start.15 = (bf16[8,2560]{1,0:T(8,128)(2,1)S(1)}, bf16[8,2560]{1,0:T(8,128)(2,1)S(1)}, u32[]{:S(2)}, u32[]{:S(2)}) collective-permute-start(bf16[8,2560]{1,0:T(8,128)(2,1)S(1)} %get-tuple-element.45), channel_id=1, source_target_pairs={{0,4},{1,5},{2,6},{3,7},{4,0},{5,1},{6,2},{7,3},{8,12},{9,13},{10,... | collective-permute-start | bytes 122888 | tf_op jit(solution)/shard_map/ppermute | solution.py:252
  54.0 5.8 %collective-permute-start.16 = (bf16[8,2560]{1,0:T(8,128)(2,1)S(1)}, bf16[8,2560]{1,0:T(8,128)(2,1)S(1)}, u32[]{:S(2)}, u32[]{:S(2)}) collective-permute-start(bf16[8,2560]{1,0:T(8,128)(2,1)S(1)} %get-tuple-element.46), channel_id=1, source_target_pairs={{0,2},{1,3},{2,4},{3,5},{4,6},{5,7},{6,0},{7,1},{8,10},{9,11},{10,... | collective-permute-start | bytes 122888 | tf_op jit(solution)/shard_map/ppermute | solution.py:252

commit v9 on v8

--- a/solution.py
+++ b/solution.py
@@ -200,6 +200,7 @@
     size = codes.shape[1]
     part = size // 2
     copies = Copies(*[(later, 3 * size + k * part, part, tail, k * part, done.at[k]) for k in range(2)])
+    copies.start()
     for k in range(2):
         terms[:, k * part : (k + 1) * part] = project(hidden, codes, k * part, scales, 2 * size + k * part, part, dequant_short)
         copies.start()

time: 60.6 us -> 60.6 us (level)
  no operation moved by 1% of the time
where the time goes in v9:
time: 60.6 us; the launch traced here: 60.5 us
  Pallas kernels  23.9 us (39%)
  starting transfers between devices  18.9 us (31%)
  waiting for transfers between devices  16.5 us (27%)
  local copies, waits for them, and re-layouts  1.05 us (2%)
    pallas_call x8, Pallas kernels, call(): pl.pallas_call(body, in_specs=[pl.BlockSpec(memory_space=pltpu.HBM if i i...  23.9 us
    ppermute x10, waiting for transfers between devices, along(): lax.ppermute(x, 'hidden', [(h, (h + 2 * s) % peers) for h in range(peers)])  13.1 us
    ppermute x10, starting transfers between devices, along(): lax.ppermute(x, 'hidden', [(h, (h + 2 * s) % peers) for h in range(peers)])  12 us
    ppermute x5, starting transfers between devices, flip(): return lax.ppermute(x, 'hidden', [(h, h ^ 1) for h in range(peers)])  6.24 us
    ppermute x5, waiting for transfers between devices, flip(): return lax.ppermute(x, 'hidden', [(h, h ^ 1) for h in range(peers)])  1.91 us
    ppermute x2, waiting for transfers between devices, swap(): return lax.ppermute(x, 'width', [(0, 1), (1, 0)])  1.55 us
  transfers between devices with their start and end apart: 17, of which 9 were waited for; matrix products, arithmetic and copies ran while one was open for 0% of the time, Pallas kernels for 20%

profile of v9, /device:TPU:0, one launch (start us, length us, event | category | flops | bytes accessed | tf_op | source)
XLA Modules:
  0.0 60.5 jit_solution(16958421780900099306)
XLA Ops:
  0.0 1.0 %copy-done.4 = bf16[10,4096]{1,0:T(8,128)(2,1)S(1)} copy-done((bf16[10,4096]{1,0:T(8,128)(2,1)S(1)}, bf16[10,4096]{1,0:T(8,128)(2,1)}, u32[]{:S(2)}) %copy-start.4) | copy-done | bytes 81944
  1.1 3.0 %collective-permute-start.3 = (bf16[8,5120]{1,0:T(8,128)(2,1)S(1)}, bf16[8,5120]{1,0:T(8,128)(2,1)S(1)}, u32[]{:S(2)}, u32[]{:S(2)}) collective-permute-start(bf16[8,5120]{1,0:T(8,128)(2,1)S(1)} %pack.1.refs_0_), channel_id=1, source_target_pairs={{0,1},{1,0},{2,3},{3,2},{4,5},{5,4},{6,7},{7,6},{8,9},{9,8},{10,11... | collective-permute-start | bytes 245768 | tf_op jit(solution)/shard_map/ppermute | solution.py:250
  4.1 3.6 %collective-permute-start.2 = (bf16[8,5120]{1,0:T(8,128)(2,1)S(1)}, bf16[8,5120]{1,0:T(8,128)(2,1)S(1)}, u32[]{:S(2)}, u32[]{:S(2)}) collective-permute-start(bf16[8,5120]{1,0:T(8,128)(2,1)S(1)} %pack.1.refs_0_), channel_id=1, source_target_pairs={{0,6},{1,7},{2,0},{3,1},{4,2},{5,3},{6,4},{7,5},{8,14},{9,15},{10,... | collective-permute-start | bytes 245768 | tf_op jit(solution)/shard_map/ppermute | solution.py:253
  7.7 1.0 %collective-permute-start.1 = (bf16[8,5120]{1,0:T(8,128)(2,1)S(1)}, bf16[8,5120]{1,0:T(8,128)(2,1)S(1)}, u32[]{:S(2)}, u32[]{:S(2)}) collective-permute-start(bf16[8,5120]{1,0:T(8,128)(2,1)S(1)} %pack.1.refs_0_), channel_id=1, source_target_pairs={{0,4},{1,5},{2,6},{3,7},{4,0},{5,1},{6,2},{7,3},{8,12},{9,13},{10,... | collective-permute-start | bytes 245768 | tf_op jit(solution)/shard_map/ppermute | solution.py:253
  8.7 1.9 %collective-permute-start.5 = (bf16[8,5120]{1,0:T(8,128)(2,1)S(1)}, bf16[8,5120]{1,0:T(8,128)(2,1)S(1)}, u32[]{:S(2)}, u32[]{:S(2)}) collective-permute-start(bf16[8,5120]{1,0:T(8,128)(2,1)S(1)} %collective-permute-done.3.refs_4_), channel_id=1, source_target_pairs={{0,4},{1,5},{2,6},{3,7},{4,0},{5,1},{6,2},{7,3},{8,12},{9,13},{10,... | collective-permute-start | bytes 245768 | tf_op jit(solution)/shard_map/ppermute | solution.py:253
  11.1 3.3 %collective-permute-done.refs_1_ = bf16[8,5120]{1,0:T(8,128)(2,1)S(1)} collective-permute-done((bf16[8,5120]{1,0:T(8,128)(2,1)S(1)}, bf16[8,5120]{1,0:T(8,128)(2,1)S(1)}, u32[]{:S(2)}, u32[]{:S(2)}) %collective-permute-start) | collective-permute-done | bytes 81952 | tf_op jit(solution)/shard_map/ppermute | solution.py:253
  15.0 3.4 %collective-permute-done.1.refs_2_ = bf16[8,5120]{1,0:T(8,128)(2,1)S(1)} collective-permute-done((bf16[8,5120]{1,0:T(8,128)(2,1)S(1)}, bf16[8,5120]{1,0:T(8,128)(2,1)S(1)}, u32[]{:S(2)}, u32[]{:S(2)}) %collective-permute-start.1) | collective-permute-done | bytes 81952 | tf_op jit(solution)/shard_map/ppermute | solution.py:253
  18.3 0.9 %collective-permute-done.5.refs_6_ = bf16[8,5120]{1,0:T(8,128)(2,1)S(1)} collective-permute-done((bf16[8,5120]{1,0:T(8,128)(2,1)S(1)}, bf16[8,5120]{1,0:T(8,128)(2,1)S(1)}, u32[]{:S(2)}, u32[]{:S(2)}) %collective-permute-start.5) | collective-permute-done | bytes 81952 | tf_op jit(solution)/shard_map/ppermute | solution.py:253
  19.2 5.0 %gate.1 = (bf16[80,4096]{1,0:T(8,128)(2,1)S(1)}, f32[80,3328]{1,0:T(8,128)S(1)}, bf16[80,3328]{1,0:T(8,128)(2,1)S(1)}, bf16[4096,1664]{1,0:T(8,128)(2,1)S(1)}) custom-call(bf16[8,5120]{1,0:T(8,128)(2,1)S(1)} %pack.1.refs_0_, bf16[8,5120]{1,0:T(8,128)(2,1)S(1)} %collective-permute-done.refs_1_, bf16[8,5120]{1,0:T(8,128)(2,1)S(1)} %collective-permute-done.1.refs_2_, ...), custom_call_target="tpu_custom_call" | custom-call | flops 10000000000 | bytes 56885248 | tf_op jit(solution)/shard_map/gate/pallas_call | solution.py:35
  24.4 7.2 %up.1 = (f32[80,3328]{1,0:T(8,128)S(1)}, bf16[80,3328]{1,0:T(8,128)(2,1)S(1)}, bf16[3328,1024]{1,0:T(8,128)(2,1)S(1)}) custom-call(bf16[80,4096]{1,0:T(8,128)(2,1)S(1)} %get-tuple-element.28.acts, bf16[4096,1664]{1,0:T(8,128)(2,1)S(1)} %get-tuple-element.29.first, bf16[4096,3328]{1,0:T(8,128)(2,1)} %codes.1, f32[128,3328]{1,0:T(8,128)S(1)} %copy-done.3, ...), custom_call_target="tpu_custom_call" | custom-call | flops 10000000000 | bytes 70516736 | tf_op jit(solution)/shard_map/up/pallas_call | solution.py:35
  32.1 1.5 %collective-permute-done.8.up_other = bf16[80,3328]{1,0:T(8,128)(2,1)S(1)} collective-permute-done((bf16[80,3328]{1,0:T(8,128)(2,1)S(1)}, bf16[80,3328]{1,0:T(8,128)(2,1)S(1)}, u32[]{:S(2)}, u32[]{:S(2)}) %collective-permute-start.8) | collective-permute-done | bytes 532512 | tf_op jit(solution)/shard_map/ppermute | solution.py:256
  33.7 5.9 %first.1 = (f32[32,2560]{1,0:T(8,128)S(1)}, bf16[32,2560]{1,0:T(8,128)(2,1)S(1)}, bf16[80,3328]{1,0:T(8,128)(2,1)S(1)}, bf16[3328,1024]{1,0:T(8,128)(2,1)S(1)}) custom-call(f32[80,3328]{1,0:T(8,128)S(1)} %get-tuple-element.26.gate, bf16[80,3328]{1,0:T(8,128)(2,1)S(1)} %collective-permute-done.7.gate_other, f32[80,3328]{1,0:T(8,128)S(1)} %get-tuple-element.30.up, ...), custom_call_target="tpu_custom_call" | custom-call | flops 1090519040 | bytes 38977536 | tf_op jit(solution)/shard_map/first/pallas_call | solution.py:35
  39.5 0.6 %collective-permute-start.9 = (bf16[32,2560]{1,0:T(8,128)(2,1)S(1)}, bf16[32,2560]{1,0:T(8,128)(2,1)S(1)}, u32[]{:S(2)}, u32[]{:S(2)}) collective-permute-start(bf16[32,2560]{1,0:T(8,128)(2,1)S(1)} %get-tuple-element.34), channel_id=1, source_target_pairs={{0,1},{1,0},{2,3},{3,2},{4,5},{5,4},{6,7},{7,6},{8,9},{9,8},{10,11... | collective-permute-start | bytes 491528 | tf_op jit(solution)/shard_map/ppermute | solution.py:250
  40.2 5.0 %second.1 = (f32[32,2560]{1,0:T(8,128)S(1)}, bf16[32,2560]{1,0:T(8,128)(2,1)S(1)}) custom-call(bf16[80,3328]{1,0:T(8,128)(2,1)S(1)} %get-tuple-element.39.hidden, bf16[3328,1024]{1,0:T(8,128)(2,1)S(1)} %get-tuple-element.40.codes, bf16[3328,4096]{1,0:T(8,128)(2,1)} %later.5, f32[104,4096]{1,0:T(8,128)S(1)} %copy-done.1), custom_call_target="tpu_custom_call" | custom-call | flops 1090519040 | bytes 36315136 | tf_op jit(solution)/shard_map/second/pallas_call | solution.py:35
  45.2 1.5 %collective-permute-start.13 = (bf16[32,2560]{1,0:T(8,128)(2,1)S(1)}, bf16[32,2560]{1,0:T(8,128)(2,1)S(1)}, u32[]{:S(2)}, u32[]{:S(2)}) collective-permute-start(bf16[32,2560]{1,0:T(8,128)(2,1)S(1)} %get-tuple-element.42), channel_id=1, source_target_pairs={{0,1},{1,0},{2,3},{3,2},{4,5},{5,4},{6,7},{7,6},{8,9},{9,8},{10,11... | collective-permute-start | bytes 491528 | tf_op jit(solution)/shard_map/ppermute | solution.py:250
  46.8 2.1 %collective-permute-start.10 = (bf16[8,2560]{1,0:T(8,128)(2,1)S(1)}, bf16[8,2560]{1,0:T(8,128)(2,1)S(1)}, u32[]{:S(2)}, u32[]{:S(2)}) collective-permute-start(bf16[8,2560]{1,0:T(8,128)(2,1)S(1)} %get-tuple-element.36), channel_id=1, source_target_pairs={{0,6},{1,7},{2,0},{3,1},{4,2},{5,3},{6,4},{7,5},{8,14},{9,15},{10,... | collective-permute-start | bytes 122888 | tf_op jit(solution)/shard_map/ppermute | solution.py:253
  48.9 0.6 %collective-permute-start.12 = (bf16[8,2560]{1,0:T(8,128)(2,1)S(1)}, bf16[8,2560]{1,0:T(8,128)(2,1)S(1)}, u32[]{:S(2)}, u32[]{:S(2)}) collective-permute-start(bf16[8,2560]{1,0:T(8,128)(2,1)S(1)} %get-tuple-element.38), channel_id=1, source_target_pairs={{0,2},{1,3},{2,4},{3,5},{4,6},{5,7},{6,0},{7,1},{8,10},{9,11},{10,... | collective-permute-start | bytes 122888 | tf_op jit(solution)/shard_map/ppermute | solution.py:253
  49.5 1.9 %collective-permute-done.13.refs_1_ = bf16[32,2560]{1,0:T(8,128)(2,1)S(1)} collective-permute-done((bf16[32,2560]{1,0:T(8,128)(2,1)S(1)}, bf16[32,2560]{1,0:T(8,128)(2,1)S(1)}, u32[]{:S(2)}, u32[]{:S(2)}) %collective-permute-start.13) | collective-permute-done | bytes 163872 | tf_op jit(solution)/shard_map/ppermute | solution.py:250
  51.5 2.1 %collective-permute-start.14 = (bf16[8,2560]{1,0:T(8,128)(2,1)S(1)}, bf16[8,2560]{1,0:T(8,128)(2,1)S(1)}, u32[]{:S(2)}, u32[]{:S(2)}) collective-permute-start(bf16[8,2560]{1,0:T(8,128)(2,1)S(1)} %get-tuple-element.44), channel_id=1, source_target_pairs={{0,6},{1,7},{2,0},{3,1},{4,2},{5,3},{6,4},{7,5},{8,14},{9,15},{10,... | collective-permute-start | bytes 122888 | tf_op jit(solution)/shard_map/ppermute | solution.py:253
  54.2 0.7 %collective-permute-done.11.refs_2_ = bf16[8,2560]{1,0:T(8,128)(2,1)S(1)} collective-permute-done((bf16[8,2560]{1,0:T(8,128)(2,1)S(1)}, bf16[8,2560]{1,0:T(8,128)(2,1)S(1)}, u32[]{:S(2)}, u32[]{:S(2)}) %collective-permute-start.11) | collective-permute-done | bytes 40992 | tf_op jit(solution)/shard_map/ppermute | solution.py:253
  54.9 0.6 collective-permute-done.14.refs_5_
  55.5 3.0 %collective-permute-done.15.refs_6_ = bf16[8,2560]{1,0:T(8,128)(2,1)S(1)} collective-permute-done((bf16[8,2560]{1,0:T(8,128)(2,1)S(1)}, bf16[8,2560]{1,0:T(8,128)(2,1)S(1)}, u32[]{:S(2)}, u32[]{:S(2)}) %collective-permute-start.15) | collective-permute-done | bytes 40992 | tf_op jit(solution)/shard_map/ppermute | solution.py:253
  58.5 1.3 %collective-permute-done.16.refs_7_ = bf16[8,2560]{1,0:T(8,128)(2,1)S(1)} collective-permute-done((bf16[8,2560]{1,0:T(8,128)(2,1)S(1)}, bf16[8,2560]{1,0:T(8,128)(2,1)S(1)}, u32[]{:S(2)}, u32[]{:S(2)}) %collective-permute-start.16) | collective-permute-done | bytes 40992 | tf_op jit(solution)/shard_map/ppermute | solution.py:253
  59.8 0.7 %last.1 = bf16[10,4096]{1,0:T(8,128)(2,1)} custom-call(f32[8,2560]{1,0:T(8,128)S(1)} %get-tuple-element.35.refs_0_, bf16[8,2560]{1,0:T(8,128)(2,1)S(1)} %collective-permute-done.10.refs_1_, bf16[8,2560]{1,0:T(8,128)(2,1)S(1)} %collective-permute-done.11.refs_2_, bf16[8,2560]{1,0:T(8,128)(2,1)S(1)} %collective-permute-done.12.refs_3_, ...), custom_call_target="tpu_custom_call" | custom-call | bytes 409600 | tf_op jit(solution)/shard_map/last/pallas_call | solution.py:35
  (28 shorter events, 2.5 us)
Async XLA Ops:
  0.0 19.2 %copy-start.2 = (f32[128,3328]{1,0:T(8,128)S(1)}, f32[128,3328]{1,0:T(8,128)}, u32[]{:S(2)}) copy-start(f32[128,3328]{1,0:T(8,128)} %refs_9_.1) | copy-start | bytes 5111812
  0.0 1.0 %copy-start.4 = (bf16[10,4096]{1,0:T(8,128)(2,1)S(1)}, bf16[10,4096]{1,0:T(8,128)(2,1)}, u32[]{:S(2)}) copy-start(bf16[10,4096]{1,0:T(8,128)(2,1)} %a_ref.1) | copy-start | bytes 245764
  1.0 18.2 %copy-start = (bf16[4096,3328]{1,0:T(8,128)(2,1)S(1)}, bf16[4096,3328]{1,0:T(8,128)(2,1)}, u32[]{:S(2)}) copy-start(bf16[4096,3328]{1,0:T(8,128)(2,1)} %refs_8_.1) | copy-start | bytes 81788928
  1.1 23.3 %copy-start.3 = (f32[128,3328]{1,0:T(8,128)S(1)}, f32[128,3328]{1,0:T(8,128)}, u32[]{:S(2)}) copy-start(f32[128,3328]{1,0:T(8,128)} %scales.3) | copy-start | bytes 5111812
  1.1 7.6 %collective-permute-start.3 = (bf16[8,5120]{1,0:T(8,128)(2,1)S(1)}, bf16[8,5120]{1,0:T(8,128)(2,1)S(1)}, u32[]{:S(2)}, u32[]{:S(2)}) collective-permute-start(bf16[8,5120]{1,0:T(8,128)(2,1)S(1)} %pack.1.refs_0_), channel_id=1, source_target_pairs={{0,1},{1,0},{2,3},{3,2},{4,5},{5,4},{6,7},{7,6},{8,9},{9,8},{10,11... | collective-permute-start | bytes 245768 | tf_op jit(solution)/shard_map/ppermute | solution.py:250
  4.1 6.5 %collective-permute-start.2 = (bf16[8,5120]{1,0:T(8,128)(2,1)S(1)}, bf16[8,5120]{1,0:T(8,128)(2,1)S(1)}, u32[]{:S(2)}, u32[]{:S(2)}) collective-permute-start(bf16[8,5120]{1,0:T(8,128)(2,1)S(1)} %pack.1.refs_0_), channel_id=1, source_target_pairs={{0,6},{1,7},{2,0},{3,1},{4,2},{5,3},{6,4},{7,5},{8,14},{9,15},{10,... | collective-permute-start | bytes 245768 | tf_op jit(solution)/shard_map/ppermute | solution.py:253
  7.7 6.8 %collective-permute-start = (bf16[8,5120]{1,0:T(8,128)(2,1)S(1)}, bf16[8,5120]{1,0:T(8,128)(2,1)S(1)}, u32[]{:S(2)}, u32[]{:S(2)}) collective-permute-start(bf16[8,5120]{1,0:T(8,128)(2,1)S(1)} %pack.1.refs_0_), channel_id=1, source_target_pairs={{0,2},{1,3},{2,4},{3,5},{4,6},{5,7},{6,0},{7,1},{8,10},{9,11},{10,... | collective-permute-start | bytes 245768 | tf_op jit(solution)/shard_map/ppermute | solution.py:253
  7.7 10.7 %collective-permute-start.1 = (bf16[8,5120]{1,0:T(8,128)(2,1)S(1)}, bf16[8,5120]{1,0:T(8,128)(2,1)S(1)}, u32[]{:S(2)}, u32[]{:S(2)}) collective-permute-start(bf16[8,5120]{1,0:T(8,128)(2,1)S(1)} %pack.1.refs_0_), channel_id=1, source_target_pairs={{0,4},{1,5},{2,6},{3,7},{4,0},{5,1},{6,2},{7,3},{8,12},{9,13},{10,... | collective-permute-start | bytes 245768 | tf_op jit(solution)/shard_map/ppermute | solution.py:253
  8.7 10.5 %collective-permute-start.5 = (bf16[8,5120]{1,0:T(8,128)(2,1)S(1)}, bf16[8,5120]{1,0:T(8,128)(2,1)S(1)}, u32[]{:S(2)}, u32[]{:S(2)}) collective-permute-start(bf16[8,5120]{1,0:T(8,128)(2,1)S(1)} %collective-permute-done.3.refs_4_), channel_id=1, source_target_pairs={{0,4},{1,5},{2,6},{3,7},{4,0},{5,1},{6,2},{7,3},{8,12},{9,13},{10,... | collective-permute-start | bytes 245768 | tf_op jit(solution)/shard_map/ppermute | solution.py:253
  10.6 8.6 %collective-permute-start.6 = (bf16[8,5120]{1,0:T(8,128)(2,1)S(1)}, bf16[8,5120]{1,0:T(8,128)(2,1)S(1)}, u32[]{:S(2)}, u32[]{:S(2)}) collective-permute-start(bf16[8,5120]{1,0:T(8,128)(2,1)S(1)} %collective-permute-done.2.refs_3_), channel_id=1, source_target_pairs={{0,1},{1,0},{2,3},{3,2},{4,5},{5,4},{6,7},{7,6},{8,9},{9,8},{10,11... | collective-permute-start | bytes 245768 | tf_op jit(solution)/shard_map/ppermute | solution.py:250
  14.4 4.8 %collective-permute-start.4 = (bf16[8,5120]{1,0:T(8,128)(2,1)S(1)}, bf16[8,5120]{1,0:T(8,128)(2,1)S(1)}, u32[]{:S(2)}, u32[]{:S(2)}) collective-permute-start(bf16[8,5120]{1,0:T(8,128)(2,1)S(1)} %collective-permute-done.refs_1_), channel_id=1, source_target_pairs={{0,1},{1,0},{2,3},{3,2},{4,5},{5,4},{6,7},{7,6},{8,9},{9,8},{10,11... | collective-permute-start | bytes 245768 | tf_op jit(solution)/shard_map/ppermute | solution.py:250
  24.3 7.8 %collective-permute-start.7 = (bf16[80,3328]{1,0:T(8,128)(2,1)S(1)}, bf16[80,3328]{1,0:T(8,128)(2,1)S(1)}, u32[]{:S(2)}, u32[]{:S(2)}) collective-permute-start(bf16[80,3328]{1,0:T(8,128)(2,1)S(1)} %get-tuple-element.27), channel_id=1, source_target_pairs={{0,8},{8,0},{1,9},{9,1},{2,10},{10,2},{3,11},{11,3},{4,12},{12,4},... | collective-permute-start | bytes 1597448 | tf_op jit(solution)/shard_map/ppermute | solution.py:256
  24.4 9.3 %copy-start.1 = (f32[104,4096]{1,0:T(8,128)S(1)}, f32[104,4096]{1,0:T(8,128)}, u32[]{:S(2)}) copy-start(f32[104,4096]{1,0:T(8,128)} %scales.5) | copy-start | bytes 5111812
  31.6 2.1 %collective-permute-start.8 = (bf16[80,3328]{1,0:T(8,128)(2,1)S(1)}, bf16[80,3328]{1,0:T(8,128)(2,1)S(1)}, u32[]{:S(2)}, u32[]{:S(2)}) collective-permute-start(bf16[80,3328]{1,0:T(8,128)(2,1)S(1)} %get-tuple-element.31), channel_id=1, source_target_pairs={{0,8},{8,0},{1,9},{9,1},{2,10},{10,2},{3,11},{11,3},{4,12},{12,4},... | collective-permute-start | bytes 1597448 | tf_op jit(solution)/shard_map/ppermute | solution.py:256
  39.5 7.2 %collective-permute-start.9 = (bf16[32,2560]{1,0:T(8,128)(2,1)S(1)}, bf16[32,2560]{1,0:T(8,128)(2,1)S(1)}, u32[]{:S(2)}, u32[]{:S(2)}) collective-permute-start(bf16[32,2560]{1,0:T(8,128)(2,1)S(1)} %get-tuple-element.34), channel_id=1, source_target_pairs={{0,1},{1,0},{2,3},{3,2},{4,5},{5,4},{6,7},{7,6},{8,9},{9,8},{10,11... | collective-permute-start | bytes 491528 | tf_op jit(solution)/shard_map/ppermute | solution.py:250
  45.2 6.3 %collective-permute-start.13 = (bf16[32,2560]{1,0:T(8,128)(2,1)S(1)}, bf16[32,2560]{1,0:T(8,128)(2,1)S(1)}, u32[]{:S(2)}, u32[]{:S(2)}) collective-permute-start(bf16[32,2560]{1,0:T(8,128)(2,1)S(1)} %get-tuple-element.42), channel_id=1, source_target_pairs={{0,1},{1,0},{2,3},{3,2},{4,5},{5,4},{6,7},{7,6},{8,9},{9,8},{10,11... | collective-permute-start | bytes 491528 | tf_op jit(solution)/shard_map/ppermute | solution.py:250
  46.8 7.2 %collective-permute-start.10 = (bf16[8,2560]{1,0:T(8,128)(2,1)S(1)}, bf16[8,2560]{1,0:T(8,128)(2,1)S(1)}, u32[]{:S(2)}, u32[]{:S(2)}) collective-permute-start(bf16[8,2560]{1,0:T(8,128)(2,1)S(1)} %get-tuple-element.36), channel_id=1, source_target_pairs={{0,6},{1,7},{2,0},{3,1},{4,2},{5,3},{6,4},{7,5},{8,14},{9,15},{10,... | collective-permute-start | bytes 122888 | tf_op jit(solution)/shard_map/ppermute | solution.py:253
  48.9 6.0 %collective-permute-start.11 = (bf16[8,2560]{1,0:T(8,128)(2,1)S(1)}, bf16[8,2560]{1,0:T(8,128)(2,1)S(1)}, u32[]{:S(2)}, u32[]{:S(2)}) collective-permute-start(bf16[8,2560]{1,0:T(8,128)(2,1)S(1)} %get-tuple-element.37), channel_id=1, source_target_pairs={{0,4},{1,5},{2,6},{3,7},{4,0},{5,1},{6,2},{7,3},{8,12},{9,13},{10,... | collective-permute-start | bytes 122888 | tf_op jit(solution)/shard_map/ppermute | solution.py:253
  48.9 6.0 %collective-permute-start.12 = (bf16[8,2560]{1,0:T(8,128)(2,1)S(1)}, bf16[8,2560]{1,0:T(8,128)(2,1)S(1)}, u32[]{:S(2)}, u32[]{:S(2)}) collective-permute-start(bf16[8,2560]{1,0:T(8,128)(2,1)S(1)} %get-tuple-element.38), channel_id=1, source_target_pairs={{0,2},{1,3},{2,4},{3,5},{4,6},{5,7},{6,0},{7,1},{8,10},{9,11},{10,... | collective-permute-start | bytes 122888 | tf_op jit(solution)/shard_map/ppermute | solution.py:253
  51.5 4.1 %collective-permute-start.14 = (bf16[8,2560]{1,0:T(8,128)(2,1)S(1)}, bf16[8,2560]{1,0:T(8,128)(2,1)S(1)}, u32[]{:S(2)}, u32[]{:S(2)}) collective-permute-start(bf16[8,2560]{1,0:T(8,128)(2,1)S(1)} %get-tuple-element.44), channel_id=1, source_target_pairs={{0,6},{1,7},{2,0},{3,1},{4,2},{5,3},{6,4},{7,5},{8,14},{9,15},{10,... | collective-permute-start | bytes 122888 | tf_op jit(solution)/shard_map/ppermute | solution.py:253
  53.6 4.9 %collective-permute-start.15 = (bf16[8,2560]{1,0:T(8,128)(2,1)S(1)}, bf16[8,2560]{1,0:T(8,128)(2,1)S(1)}, u32[]{:S(2)}, u32[]{:S(2)}) collective-permute-start(bf16[8,2560]{1,0:T(8,128)(2,1)S(1)} %get-tuple-element.45), channel_id=1, source_target_pairs={{0,4},{1,5},{2,6},{3,7},{4,0},{5,1},{6,2},{7,3},{8,12},{9,13},{10,... | collective-permute-start | bytes 122888 | tf_op jit(solution)/shard_map/ppermute | solution.py:253
  54.0 5.8 %collective-permute-start.16 = (bf16[8,2560]{1,0:T(8,128)(2,1)S(1)}, bf16[8,2560]{1,0:T(8,128)(2,1)S(1)}, u32[]{:S(2)}, u32[]{:S(2)}) collective-permute-start(bf16[8,2560]{1,0:T(8,128)(2,1)S(1)} %get-tuple-element.46), channel_id=1, source_target_pairs={{0,2},{1,3},{2,4},{3,5},{4,6},{5,7},{6,0},{7,1},{8,10},{9,11},{10,... | collective-permute-start | bytes 122888 | tf_op jit(solution)/shard_map/ppermute | solution.py:253
